TPU v7x, 512 devices: a whole 4x4x16 slice. The times are simulated.
512 devices in a mesh: rep: 64 (over y, z_lo, x), tp: 8 (over z_hi, core).
Axes of the slice: x: 4, y: 4, z: 16 (z_hi: 4, z_lo: 4; z = z_hi * 4 + z_lo), core: 2. Of those that a mesh axis runs over, the one named last changes fastest.
Arguments:
- lookup_vectors: bfloat16 [4, 256, 128, 128], P(None, 'rep', 'tp'), may hold values from -5 to 5
- fresh_token_memory: bfloat16 [4, 256, 2, 8, 128], P(None, 'rep', None, 'tp'), may hold values from -5 to 5
- unfinished_block_memory: bfloat16 [256, 2, 16, 8, 128], P('rep', None, None, 'tp'), may hold values from -5 to 5
- cache_block_store: bfloat16 [4096, 2, 16, 8, 128], P('rep', None, None, 'tp'), may hold values from -7.5 to 7.5
- sequence_block_index: int32 [256, 128], P('rep'), may hold values from 0 to 191
- sequence_history_count: int32 [256], P('rep'), may hold values from 1 to 2048, as said below
- unfinished_block_fill: int32 [256], P('rep'), may hold values from 0 to 12
- migration_sender_block: int32 [4096], P('rep'), may hold values from 0 to 67
- migration_receiver_server: int32 [4096, 1], P('rep'), may hold values from 0 to 63; in each aligned block of 64 rows (0 to 63, 64 to 127, ...) at most 2 rows name the same one
- switch_moment: int32 [256], P('rep'), may hold values from 0 to 4
- output_scaling_weights: float32 [16384], P('tp'), may hold values from 0.5 to 1.5
Outputs:
- normed: bfloat16 [4, 256, 16384], P(None, 'rep', 'tp')
Inputs may be any that keep to these rules, and one draw needn't show every extreme that they name: `sequence_block_index`: an entry below 64 names a page of the request's own replica, an entry 64 + j its arrival slot j. `sequence_history_count`: some request holds the full 128 * 16 tokens in every draw. `migration_sender_block`: an entry below 64 names a page of the replica's own pool, an entry 64 + i the tail page of its request i. `migration_receiver_server`: among the 64 entries of one replica no destination appears more than 2 times.
All inputs are finite; a program needn't handle non-finite values.
Results may differ from a plain program's by a relative error of at most 0.0056.
Values may be sent and summed in bfloat16 or wider, within the bound.
No kernel may reach another device: no remote copies, remote signals or barrier semaphores. Data moves between devices by JAX's collectives and lax.ppermute only.
A program may use at most 64 MiB of HBM per device.

v0:
```python
import math

import jax
import jax.numpy as jnp
from jax import lax
from jax.sharding import PartitionSpec as P


def filled_tail(unfinished_block_memory, fresh_token_memory, unfinished_block_fill):
    decode_steps = fresh_token_memory.shape[0]
    page_entry = unfinished_block_memory.shape[2]
    offsets = jnp.arange(page_entry, dtype=jnp.int32)
    hits = (
        offsets[None, None, :]
        == unfinished_block_fill[None, :, None]
        + jnp.arange(decode_steps, dtype=jnp.int32)[:, None, None]
    )
    placed = jnp.einsum(
        "srp,srckd->rcpkd",
        hits.astype(jnp.bfloat16),
        fresh_token_memory,
        preferred_element_type=jnp.float32,
    )
    covered = jnp.any(hits, axis=0)
    return jnp.where(
        covered[:, None, :, None, None], placed.astype(jnp.bfloat16), unfinished_block_memory
    )


def slot_ranks(target):
    order = jnp.arange(target.shape[0], dtype=jnp.int32)
    same = (target[:, None] == target[None, :]) & (order[None, :] < order[:, None])
    return jnp.sum(same.astype(jnp.int32), axis=1, dtype=jnp.int32)


def pick_rows(selector, table):
    flat = table.reshape(table.shape[0], -1)
    picked = jnp.dot(selector.astype(jnp.bfloat16), flat, preferred_element_type=jnp.float32)
    return picked.astype(jnp.bfloat16).reshape((selector.shape[0],) + table.shape[1:])


def one_hot_rows(index, count):
    return index[:, None] == jnp.arange(count, dtype=jnp.int32)[None, :]


def token_validity(
    page_table_row,
    context_length,
    arrival_length,
    tail_length,
    boundary_marker,
    pool_page_tiles,
    page_entry,
    decode_steps,
):
    entry = jnp.repeat(page_table_row, page_entry)
    position = jnp.arange(entry.shape[0], dtype=jnp.int32)
    offset = position % page_entry
    incoming = entry >= pool_page_tiles
    known = arrival_length[jnp.clip(entry - pool_page_tiles, 0, arrival_length.shape[0] - 1)]
    step = jnp.arange(decode_steps, dtype=jnp.int32)[:, None]
    page_ok = (position < context_length)[None, :] & (
        jnp.logical_not(incoming)[None, :] | (step >= boundary_marker) & (offset < known)[None, :]
    )
    tail_ok = jnp.arange(page_entry, dtype=jnp.int32)[None, :] < tail_length + step + 1
    return jnp.concatenate([page_ok, tail_ok], axis=1)


def attend(query_vector, pages, tail_block, valid_mask):
    decode_steps, heads, hdim = query_vector.shape
    kv_heads = pages.shape[3]
    keys = jnp.concatenate([pages[:, 0].reshape(-1, kv_heads, hdim), tail_block[0]], 0)
    values = jnp.concatenate([pages[:, 1].reshape(-1, kv_heads, hdim), tail_block[1]], 0)
    grouped = query_vector.reshape(decode_steps, kv_heads, heads // kv_heads, hdim)
    scores = jnp.einsum(
        "skgd,lkd->skgl", grouped, keys, preferred_element_type=jnp.float32
    ) / math.sqrt(hdim)
    scores = jnp.where(valid_mask[:, None, None, :], scores, -jnp.inf)
    top = jnp.max(scores, axis=-1, keepdims=True)
    probs = jnp.exp(scores - top)
    total = jnp.sum(probs, axis=-1, keepdims=True)
    weights = probs.astype(jnp.bfloat16)
    mixed = (
        jnp.einsum("skgl,lkd->skgd", weights, values, preferred_element_type=jnp.float32) / total
    )
    return mixed.reshape(decode_steps, heads, hdim).astype(jnp.bfloat16)


def body(
    lookup_vectors,
    fresh_token_memory,
    unfinished_block_memory,
    cache_block_store,
    sequence_block_index,
    sequence_history_count,
    unfinished_block_fill,
    migration_sender_block,
    migration_receiver_server,
    switch_moment,
    output_scaling_weights,
):
    replicas = lax.axis_size("rep")
    decode_steps, requests, heads, hdim = lookup_vectors.shape
    pool_page_tiles = cache_block_store.shape[0]
    page_entry = cache_block_store.shape[2]
    entries = migration_sender_block.shape[0]
    capacity = max(2, 2 * entries // replicas)
    slot_count = replicas * capacity
    from_tail = migration_sender_block >= pool_page_tiles
    pool_pick = jnp.clip(migration_sender_block, 0, pool_page_tiles - 1)
    tail_pick = jnp.clip(migration_sender_block - pool_page_tiles, 0, requests - 1)
    lengths = jnp.where(
        from_tail, unfinished_block_fill[tail_pick] + switch_moment[tail_pick], page_entry
    )
    target = migration_receiver_server[:, 0]
    landing = target * capacity + slot_ranks(target)
    out_len = jnp.zeros((slot_count,), jnp.int32).at[landing].set(lengths)
    placement = jnp.transpose(one_hot_rows(landing, slot_count))
    pool_select = one_hot_rows(pool_pick, pool_page_tiles)
    tail_select = one_hot_rows(tail_pick, requests)
    tails = filled_tail(unfinished_block_memory, fresh_token_memory, unfinished_block_fill)
    moved = jnp.where(
        from_tail[:, None, None, None, None],
        pick_rows(tail_select, tails),
        pick_rows(pool_select, cache_block_store),
    )
    outgoing = pick_rows(placement, moved)
    arrived, arrival_length = (
        lax.all_to_all(outgoing, "rep", split_axis=0, concat_axis=0, tiled=True),
        lax.all_to_all(out_len, "rep", split_axis=0, concat_axis=0, tiled=True),
    )
    extended = jnp.concatenate([cache_block_store, arrived], 0)
    extended_count = extended.shape[0]

    def one_request(request_element):
        query_vector, page_table_row, tail_block, context_length, tail_length, handover_step = (
            request_element
        )
        valid_mask = token_validity(
            page_table_row,
            context_length,
            arrival_length,
            tail_length,
            handover_step,
            pool_page_tiles,
            page_entry,
            decode_steps,
        )
        pages = pick_rows(one_hot_rows(page_table_row, extended_count), extended)
        return attend(query_vector, pages, tail_block, valid_mask)

    mixed = lax.map(
        one_request,
        (
            jnp.transpose(lookup_vectors, (1, 0, 2, 3)),
            sequence_block_index,
            tails,
            sequence_history_count,
            unfinished_block_fill,
            switch_moment,
        ),
    )
    attn = jnp.transpose(mixed.reshape(requests, decode_steps, heads * hdim), (1, 0, 2))
    wide = attn.astype(jnp.float32)
    width = heads * hdim * lax.axis_size("tp")
    squared = lax.psum(jnp.sum(wide * wide, axis=-1, keepdims=True), "tp")
    mean = squared / width
    return (wide * lax.rsqrt(mean + 1e-05) * output_scaling_weights).astype(jnp.bfloat16)


def solution(mesh):
    placed = (
        P(None, "rep", "tp", None),
        P(None, "rep", None, "tp", None),
        P("rep", None, None, "tp", None),
        P("rep", None, None, "tp", None),
        P("rep", None),
        P("rep"),
        P("rep"),
        P("rep"),
        P("rep", None),
        P("rep"),
        P("tp"),
    )
    return jax.shard_map(
        body, mesh=mesh, in_specs=placed, out_specs=P(None, "rep", "tp"), check_vma=False
    )
```

profile of v0, /device:TPU:1, one launch (start us, length us, event | category | flops | bytes accessed | tf_op | source)
XLA Modules:
  0.0 170.6 jit_solution(9037360625597588332)
XLA Ops:
  0.0 1.4 fusion.58
  1.4 1.5 fusion.59
  2.9 0.9 convert_reduce_fusion
  3.8 0.7 fusion.51
  4.5 5.6 %fusion.50 = (s32[64]{0:T(128)S(1)}, s32[64]{0:T(128)S(1)}, s32[64]{0:T(128)S(1)}) fusion(s32[]{:T(128)} %bitcast.39, s32[]{:T(128)} %bitcast.40, s32[]{:T(128)} %bitcast.41, s32[]{:T(128)} %bitcast.42, s32[]{:T(128)} %bitcast.35, s32[]{:T(128)} %bitcast.36, s32[]{:T(128)} %bitcast.37, s32[]{:T(128)} %bitcast.38, s32[64]{0:T(128)} %param.20), kind=kLoop, calls=%fused_computation.93 | loop fusion | flops 1152 | bytes 1056 | tf_op jit(solution)/shard_map/jit(_where)/select_n | solution.py:112
  10.1 0.8 scatter_custom_fusion
  10.9 0.8 all_to_all.12
  11.6 12.6 %all-to-all-start.1 = ((s32[64,2,1]{1,2,0:T(1,128)}), s32[64,2,1]{1,2,0:T(1,128)S(1)}, u32[]{:S(2)}, u32[]{:S(2)}) async-start(s32[64,2,1]{1,2,0:T(1,128)} %bitcast.43), calls=%async_computation.1 | async-start | bytes 65536 | tf_op jit(solution)/shard_map/all_to_all | solution.py:130
  24.2 0.7 iota_add_fusion
  24.9 0.7 broadcast_compare_fusion
  25.6 1.0 fusion.30
  27.0 1.7 fusion.28
  28.7 1.2 copy.47
  29.9 3.0 %all-to-all-done.1 = s32[64,2,1]{1,2,0:T(1,128)S(1)} async-done(((s32[64,2,1]{1,2,0:T(1,128)}), s32[64,2,1]{1,2,0:T(1,128)S(1)}, u32[]{:S(2)}, u32[]{:S(2)}) %all-to-all-start.1) | async-done | bytes 544 | tf_op jit(solution)/shard_map/all_to_all | solution.py:130
  33.0 7.2 %all-to-all-start = ((bf16[128,2,16,1,128]{4,2,1,3,0:T(8,128)(2,1)}), bf16[128,2,16,1,128]{4,2,1,3,0:T(8,128)(2,1)S(1)}, u32[]{:S(2)}, u32[]{:S(2)}) async-start(bf16[128,2,16,1,128]{4,2,1,3,0:T(8,128)(2,1)} %bitcast.31), calls=%async_computation | async-start | bytes 2097152 | tf_op jit(solution)/shard_map/all_to_all | solution.py:129
  40.8 0.8 reduce.11
  41.7 26.3 %all-to-all-done = bf16[128,2,16,1,128]{4,2,1,3,0:T(8,128)(2,1)S(1)} async-done(((bf16[128,2,16,1,128]{4,2,1,3,0:T(8,128)(2,1)}), bf16[128,2,16,1,128]{4,2,1,3,0:T(8,128)(2,1)S(1)}, u32[]{:S(2)}, u32[]{:S(2)}) %all-to-all-start) | async-done | bytes 1048608 | tf_op jit(solution)/shard_map/all_to_all | solution.py:129
  68.2 0.7 reshape.276
  69.4 78.1 %while.13 = (s32[]{:T(128)}, bf16[4,4,16,128]{3,2,1,0:T(8,128)(2,1)S(1)}, s32[4,128]{1,0:T(4,128)}, bf16[192,2,16,1,128]{4,2,1,0,3:T(8,128)(2,1)}, bf16[4,2,16,1...) while((s32[]{:T(128)}, ...), condition=%wide.wide.region_6.7_spmd, body=%wide.wide.region_3.6_spmd.sunk | while | flops 272621056 | bytes 9683901 | solution.py:152
  69.4 0.7 compare_not_fusion.3
  70.3 12.6 %gather_fusion = s32[2048]{0:T(1024)S(1)} fusion(s32[128]{0:T(128)S(1)} %get-tuple-element.388, s32[2048]{0:T(1024)S(1)} %broadcast_clamp_fusion.4), kind=kCustom, calls=%fused_computation.clone.clone.1 | custom fusion | bytes 24576 | tf_op jit(solution)/shard_map/while/body/eval_jaxpr/gather | solution.py:60
  82.9 0.6 dynamic_slice.60
  83.5 0.6 fusion.82
  84.3 0.6 dynamic_slice.61
  85.0 0.6 iota_compare_fusion.22
  85.7 0.6 dynamic_slice.59
  88.9 0.7 compare_not_fusion.3
  89.8 12.6 %gather_fusion = s32[2048]{0:T(1024)S(1)} fusion(s32[128]{0:T(128)S(1)} %get-tuple-element.388, s32[2048]{0:T(1024)S(1)} %broadcast_clamp_fusion.4), kind=kCustom, calls=%fused_computation.clone.clone.1 | custom fusion | bytes 24576 | tf_op jit(solution)/shard_map/while/body/eval_jaxpr/gather | solution.py:60
  102.4 0.6 dynamic_slice.60
  103.1 0.6 fusion.82
  103.9 0.6 dynamic_slice.61
  104.5 0.6 iota_compare_fusion.22
  105.2 0.6 dynamic_slice.59
  108.4 0.7 compare_not_fusion.3
  109.3 12.6 %gather_fusion = s32[2048]{0:T(1024)S(1)} fusion(s32[128]{0:T(128)S(1)} %get-tuple-element.388, s32[2048]{0:T(1024)S(1)} %broadcast_clamp_fusion.4), kind=kCustom, calls=%fused_computation.clone.clone.1 | custom fusion | bytes 24576 | tf_op jit(solution)/shard_map/while/body/eval_jaxpr/gather | solution.py:60
  122.0 0.6 dynamic_slice.60
  122.6 0.6 fusion.82
  123.4 0.6 dynamic_slice.61
  124.0 0.6 iota_compare_fusion.22
  124.7 0.6 dynamic_slice.59
  128.0 0.7 compare_not_fusion.3
  128.9 12.6 %gather_fusion = s32[2048]{0:T(1024)S(1)} fusion(s32[128]{0:T(128)S(1)} %get-tuple-element.388, s32[2048]{0:T(1024)S(1)} %broadcast_clamp_fusion.4), kind=kCustom, calls=%fused_computation.clone.clone.1 | custom fusion | bytes 24576 | tf_op jit(solution)/shard_map/while/body/eval_jaxpr/gather | solution.py:60
  141.5 0.6 dynamic_slice.60
  142.1 0.6 fusion.82
  142.9 0.6 dynamic_slice.61
  144.2 0.6 dynamic_slice.59
  147.7 22.2 %psum.7 = f32[4,4,1]{1,0,2:T(4,128)S(1)} all-reduce(f32[4,4,1]{1,0,2:T(4,128)S(1)} %bitcast.197), channel_id=1, replica_groups=mesh['rep'=64,'tp'=8] {'tp'}, use_global_device_ids=true, to_apply=%region_8.9 | all-reduce | flops 16 | bytes 128 | tf_op jit(solution)/shard_map/psum | solution.py:166
  169.9 0.7 fusion.38
  (100 shorter events, 14.6 us)
Async XLA Ops:
  0.0 25.6 %copy-start = (bf16[4,4,2,1,128]{4,2,3,1,0:T(2,128)(2,1)S(1)}, bf16[4,4,2,1,128]{4,2,3,1,0:T(2,128)(2,1)}, u32[]{:S(2)}) copy-start(bf16[4,4,2,1,128]{4,2,3,1,0:T(2,128)(2,1)} %param.14) | copy-start | bytes 24580
  11.6 21.4 %all-to-all-start.1 = ((s32[64,2,1]{1,2,0:T(1,128)}), s32[64,2,1]{1,2,0:T(1,128)S(1)}, u32[]{:S(2)}, u32[]{:S(2)}) async-start(s32[64,2,1]{1,2,0:T(1,128)} %bitcast.43), calls=%async_computation.1 | async-start | bytes 65536 | tf_op jit(solution)/shard_map/all_to_all | solution.py:130
  29.9 10.3 %copy-start.3 = (bf16[4,4,16,128]{3,2,1,0:T(8,128)(2,1)S(1)}, bf16[4,4,16,128]{3,2,1,0:T(8,128)(2,1)}, u32[]{:S(2)}) copy-start(bf16[4,4,16,128]{3,2,1,0:T(8,128)(2,1)} %param.13) | copy-start | bytes 196612
  29.9 38.1 %copy-start.2 = (bf16[64,2,16,1,128]{4,2,3,1,0:T(8,128)(2,1)S(1)}, bf16[64,2,16,1,128]{4,2,3,1,0:T(8,128)(2,1)}, u32[]{:S(2)}) copy-start(bf16[64,2,16,1,128]{4,2,3,1,0:T(8,128)(2,1)} %param.16) | copy-start | bytes 1572868
  33.0 35.1 %all-to-all-start = ((bf16[128,2,16,1,128]{4,2,1,3,0:T(8,128)(2,1)}), bf16[128,2,16,1,128]{4,2,1,3,0:T(8,128)(2,1)S(1)}, u32[]{:S(2)}, u32[]{:S(2)}) async-start(bf16[128,2,16,1,128]{4,2,1,3,0:T(8,128)(2,1)} %bitcast.31), calls=%async_computation | async-start | bytes 2097152 | tf_op jit(solution)/shard_map/all_to_all | solution.py:129
  68.2 1.2 copy-start.1
  68.2 1.1 copy-start.4
  68.2 1.1 copy-start.6
  68.2 1.1 copy-start.7
  69.4 100.5 %copy-start.5 = (f32[2048]{0:T(1024)S(1)}, f32[2048]{0:T(1024)}, u32[]{:S(2)}) copy-start(f32[2048]{0:T(1024)} %param.23) | copy-start | bytes 24580
where the time goes:
time: 173 us; the launch traced here: 171 us
  local copies, waits for them, and re-layouts  68.6 us (40%)
  waiting for transfers between devices  29.4 us (17%)
  other arithmetic  22.2 us (13%)
  blocking collectives  22.2 us (13%)
  starting transfers between devices  19.7 us (11%)
  matrix products  7.86 us (5%)
    gather x4, local copies, waits for them, and re-layouts, token_validity(): arrival_length[jnp.clip(entry - pool_page_tiles, 0, arrival_length.shape[...  50.5 us
    all_to_all x1, waiting for transfers between devices, body(): lax.all_to_all(outgoing, 'rep', split_axis=0, concat_axis=0, tiled=True)  26.3 us
    psum x1, blocking collectives, body(): squared = lax.psum(jnp.sum(wide * wide, axis=-1, keepdims=True), 'tp')  22.2 us
    all_to_all x1, starting transfers between devices, body(): lax.all_to_all(out_len, 'rep', split_axis=0, concat_axis=0, tiled=True)  12.6 us
    dynamic_slice x12, local copies, waits for them, and re-layouts, body(): lax.map(one_request, (jnp.transpose(lookup_vectors, (1, 0, 2, 3)), sequen...  7.4 us
    all_to_all x1, starting transfers between devices, body(): lax.all_to_all(outgoing, 'rep', split_axis=0, concat_axis=0, tiled=True)  7.2 us
    select_n x1, other arithmetic, body(): jnp.where(from_tail, unfinished_block_fill[tail_pick] + switch_moment[tai...  5.6 us
    dot_general x6, matrix products, pick_rows(): jnp.dot(selector.astype(jnp.bfloat16), flat, preferred_element_type=jnp.f...  3.94 us
  transfers between devices with their start and end apart: 2, of which 2 were waited for; matrix products, arithmetic and copies ran while one was open for 4% of the time, Pallas kernels for 0%

commit v1 on v0

v1 whole, which is shorter than its diff:
```python
import jax
import jax.numpy as jnp
from jax import lax
from jax.experimental import pallas as pl
from jax.experimental.pallas import tpu as pltpu
from jax.sharding import PartitionSpec as P

STEPS, REQS, HEADS, HD = 4, 4, 16, 128
ROWS = STEPS * REQS * HEADS
PAIRS = STEPS * REQS
PAGE = 16
POOL = 64
MIGS = 64
PEERS = 32
TOKENS = POOL * PAGE
NEG = -1e30
MARK = 4096.0
SCALE = 1.4426950408889634 / HD**0.5
F32, BF16, I32 = jnp.float32, jnp.bfloat16, jnp.int32
VMEM = pl.BlockSpec(memory_space=pltpu.VMEM)
SMEM = pl.BlockSpec(memory_space=pltpu.SMEM)


def dot(a, b, ca, cb):
    return lax.dot_general(a, b, (((ca,), (cb,)), ((), ())), preferred_element_type=F32)


def iota(shape, axis):
    return lax.broadcasted_iota(I32, shape, axis)


def tail_tile(r, kv, fill, unfinished_ref, fresh_ref):
    rows = iota((PAGE, HD), 0)
    tile = unfinished_ref[r, kv * PAGE : (kv + 1) * PAGE, :].astype(F32)
    for s in range(STEPS):
        row = fresh_ref[s, r].astype(F32)[kv : kv + 1, :]
        tile = jnp.where(rows == fill + s, row, tile)
    return tile


def send_kernel(half_ref, target_ref, source_ref, fill_ref, switch_ref, pool_ref, unfinished_ref, fresh_ref, out_ref, cut_ref):
    rows = iota((PAGE, HD), 0)
    blank = jnp.concatenate([jnp.full((PAGE, HD), MARK, BF16), jnp.zeros((PAGE, HD), BF16)], 0)
    out_ref[...] = jnp.broadcast_to(blank[None], out_ref.shape)
    for r in range(REQS):
        fill = fill_ref[r]
        key = tail_tile(r, 0, fill, unfinished_ref, fresh_ref)
        value = tail_tile(r, 1, fill, unfinished_ref, fresh_ref)
        key = jnp.where(rows < fill + switch_ref[r], key, MARK)
        cut_ref[r] = jnp.concatenate([key, value], 0).astype(BF16)
    half = half_ref[0]
    low = jnp.int32(0)
    high = jnp.int32(0)
    for e in range(MIGS):
        t = target_ref[e]
        m = source_ref[e]
        first = t < 32
        shift = t & 31
        word = jnp.where(first, low, high)
        rank = (word >> shift) & 1
        word = word | (jnp.int32(1) << shift)
        low = jnp.where(first, word, low)
        high = jnp.where(first, high, word)
        peer = ((t >> 4) << 3) | (t & 7)
        which = ((t >> 3) & 1) ^ half
        slot = peer * 4 + which * 2 + rank
        pooled = pool_ref[jnp.minimum(m, POOL - 1)]
        cut = cut_ref[jnp.maximum(m - POOL, 0)]
        out_ref[slot] = jnp.where(m < POOL, pooled, cut)


def send_tiles(half, target, source, fill, switch, pool, unfinished, fresh):
    return pl.pallas_call(
        send_kernel,
        out_shape=jax.ShapeDtypeStruct((PEERS * 4, 2 * PAGE, HD), BF16),
        in_specs=[SMEM] * 5 + [VMEM] * 3,
        out_specs=VMEM,
        scratch_shapes=[pltpu.VMEM((REQS, 2 * PAGE, HD), BF16)],
        cost_estimate=pl.CostEstimate(flops=1000, bytes_accessed=2**21, transcendentals=0),
        name="send_tiles",
    )(half, target, source, fill, switch, pool, unfinished, fresh)


def count_kernel(half_ref, length_ref, switch_ref, table_ref, pool_ref, near_ref, far_ref):
    half = half_ref[0]
    offset = iota((PAGE, HD), 0)
    position = iota((PAGE, HD), 1) * PAGE + offset
    slot = iota((POOL, HD), 0)
    spread = (iota((POOL, TOKENS), 1) // PAGE == iota((POOL, TOKENS), 0)).astype(BF16)
    own = iota((POOL, TOKENS), 1) % PAGE == iota((POOL, TOKENS), 0) % PAGE
    fold = (iota((PAIRS, POOL), 1) // PAGE == iota((PAIRS, POOL), 0) % REQS).astype(BF16)
    pair = iota((PAIRS, TOKENS), 0)
    step, req = pair // REQS, pair % REQS
    moment = jnp.zeros((PAIRS, TOKENS), I32)
    for g in range(REQS):
        moment = jnp.where(req == g, switch_ref[g], moment)
    for section, ref in ((0, pool_ref), (1, near_ref), (2, far_ref)):
        if section == 0:
            page = slot
        else:
            side = half if section == 1 else 1 - half
            page = POOL + (slot // 16) * 32 + side * 16 + slot % 16
        counts = []
        for g in range(REQS):
            valid = (position < length_ref[g]).astype(BF16)
            hit = (table_ref[g : g + 1, :] == page).astype(BF16)
            counts.append(dot(valid, hit, 1, 1))
        counts = jnp.concatenate(counts, 0).astype(BF16)
        wide = jnp.where(own, dot(counts, spread, 1, 0), 0.0).astype(BF16)
        wide = dot(fold, wide, 1, 0)
        if section:
            wide = jnp.where(step >= moment, wide, 0.0)
        ref[...] = wide.astype(BF16)


def count_tokens(half, length, switch, table):
    shape = jax.ShapeDtypeStruct((PAIRS, TOKENS), BF16)
    return pl.pallas_call(
        count_kernel,
        out_shape=(shape,) * 3,
        in_specs=[SMEM] * 3 + [VMEM],
        out_specs=(VMEM,) * 3,
        cost_estimate=pl.CostEstimate(flops=2**27, bytes_accessed=2**18, transcendentals=0),
        name="count_tokens",
    )(half, length, switch, table)


def bias_of(count):
    count = count.astype(F32)
    return jnp.where(count > 0, jnp.log2(jnp.maximum(count, 1.0)), NEG)


def attend(query, key, value, bias, probs_ref):
    scores = dot(query, key, 1, 1)
    width = key.shape[0]
    logs, sums = [], []
    for h in range(HEADS):
        rows = slice(h * PAIRS, (h + 1) * PAIRS)
        x = scores[rows] * SCALE + bias
        top = jnp.max(x, axis=-1, keepdims=True)
        p = jnp.exp2(x - top)
        total = jnp.sum(p, axis=-1, keepdims=True)
        probs_ref[rows, :width] = p.astype(BF16)
        logs.append(top + jnp.log2(total))
        sums.append(total)
    mixed = dot(probs_ref[:, :width], value, 1, 0) / jnp.concatenate(sums, 0)
    return mixed, jnp.concatenate(logs, 0)


def combine(a, b):
    (x, p), (y, q) = a, b
    top = jnp.maximum(p, q)
    u, v = jnp.exp2(p - top), jnp.exp2(q - top)
    return (x * u + y * v) / (u + v), top + jnp.log2(u + v)


def local_kernel(fill_ref, query_ref, pool_ref, unfinished_ref, fresh_ref, count_ref, mixed_ref, log_ref, probs_ref):
    query = query_ref[...]
    key = pool_ref[:, :PAGE, :].reshape(TOKENS, HD)
    value = pool_ref[:, PAGE:, :].reshape(TOKENS, HD)
    part = attend(query, key, value, bias_of(count_ref[...]), probs_ref)
    tail = REQS * PAGE
    keys, values = [], []
    pair, lane = iota((PAIRS, tail), 0), iota((PAIRS, tail), 1)
    step, req = pair // REQS, pair % REQS
    held = jnp.zeros((PAIRS, tail), I32)
    for r in range(REQS):
        fill = fill_ref[r]
        keys.append(tail_tile(r, 0, fill, unfinished_ref, fresh_ref))
        values.append(tail_tile(r, 1, fill, unfinished_ref, fresh_ref))
        held = jnp.where(req == r, fill, held)
    valid = (lane // PAGE == req) & (lane % PAGE < held + step + 1)
    keys = jnp.concatenate(keys, 0).astype(BF16)
    values = jnp.concatenate(values, 0).astype(BF16)
    tails = attend(query, keys, values, jnp.where(valid, 0.0, NEG), probs_ref)
    mixed, log = combine(part, tails)
    mixed_ref[...] = mixed
    log_ref[...] = jnp.broadcast_to(log, log_ref.shape)


def local_part(fill, query, pool, unfinished, fresh, count):
    shape = jax.ShapeDtypeStruct((ROWS, HD), F32)
    return pl.pallas_call(
        local_kernel,
        out_shape=(shape, shape),
        in_specs=[SMEM] + [VMEM] * 5,
        out_specs=(VMEM, VMEM),
        scratch_shapes=[pltpu.VMEM((ROWS, TOKENS), BF16)],
        cost_estimate=pl.CostEstimate(flops=2**28, bytes_accessed=2**20, transcendentals=2**18),
        name="local_part",
    )(fill, query, pool, unfinished, fresh, count)


def arrived_part(query, count, tiles_ref, which, probs_ref):
    tiles = tiles_ref[:, 2 * which : 2 * which + 2]
    key = tiles[:, :, :PAGE, :].reshape(TOKENS, HD)
    value = tiles[:, :, PAGE:, :].reshape(TOKENS, HD)
    pick = (iota((PAIRS, HD), 1) == 0).astype(BF16)
    there = dot(pick, key, 1, 1) < MARK / 2
    bias = jnp.where(there, bias_of(count), NEG)
    return attend(query, key, value, bias, probs_ref)


def far_kernel(request_ref, tiles_ref, out_ref, probs_ref):
    query = request_ref[:ROWS, :]
    count = jnp.concatenate([request_ref[ROWS + PAIRS * i : ROWS + PAIRS * (i + 1), :] for i in range(TOKENS // HD)], 1)
    mixed, log = arrived_part(query, count, tiles_ref, 1, probs_ref)
    out_ref[:ROWS, :] = mixed.astype(BF16)
    lane = iota((ROWS, HD), 1)
    high = log.astype(BF16).astype(F32)
    middle = (log - high).astype(BF16).astype(F32)
    least = log - high - middle
    parts = jnp.where(lane == 0, high, jnp.where(lane == 1, middle, jnp.where(lane == 2, least, 0.0)))
    eye = (iota((8, HD), 0) == iota((8, HD), 1)).astype(BF16)
    across = dot(eye, parts.astype(BF16), 1, 1)
    out_ref[ROWS:, :] = jnp.concatenate([across[:, :HD], across[:, HD:]], 0).astype(BF16)


def far_part(request, tiles):
    return pl.pallas_call(
        far_kernel,
        out_shape=jax.ShapeDtypeStruct((ROWS + 16, HD), BF16),
        in_specs=[VMEM, VMEM],
        out_specs=VMEM,
        scratch_shapes=[pltpu.VMEM((ROWS, TOKENS), BF16)],
        cost_estimate=pl.CostEstimate(flops=2**28, bytes_accessed=2**20, transcendentals=2**18),
        name="far_part",
    )(request, tiles)


def near_kernel(query_ref, count_ref, tiles_ref, mixed_ref, log_ref, out_ref, sum_ref, probs_ref):
    part = arrived_part(query_ref[...], count_ref[...], tiles_ref, 0, probs_ref)
    mixed, log = combine((mixed_ref[...], log_ref[...]), part)
    out_ref[...] = mixed
    sum_ref[...] = log


def near_part(query, count, tiles, mixed, log):
    shape = jax.ShapeDtypeStruct((ROWS, HD), F32)
    return pl.pallas_call(
        near_kernel,
        out_shape=(shape, shape),
        in_specs=[VMEM] * 5,
        out_specs=(VMEM, VMEM),
        scratch_shapes=[pltpu.VMEM((ROWS, TOKENS), BF16)],
        cost_estimate=pl.CostEstimate(flops=2**28, bytes_accessed=2**20, transcendentals=2**18),
        name="near_part",
    )(query, count, tiles, mixed, log)


def merge_kernel(mixed_ref, log_ref, back_ref, attn_ref, square_ref):
    stats = back_ref[ROWS:, :].astype(F32)
    stats = jnp.concatenate([stats[:8], stats[8:]], 1).astype(BF16)
    log = dot(stats, jnp.ones((8, HD), BF16), 0, 0)
    mixed, _ = combine((mixed_ref[...], log_ref[...]), (back_ref[:ROWS, :].astype(F32), log))
    attn = mixed.astype(BF16)
    attn_ref[...] = attn
    wide = attn.astype(F32)
    square = wide * wide
    total = square[:PAIRS]
    for h in range(1, HEADS):
        total = total + square[h * PAIRS : (h + 1) * PAIRS]
    total = jnp.sum(total, axis=-1, keepdims=True)
    line = jnp.sum(jnp.where(iota((PAIRS, HD), 0) == iota((PAIRS, HD), 1), total, 0.0), axis=0, keepdims=True)
    square_ref[...] = jnp.broadcast_to(line[None], square_ref.shape)


def merge(mixed, log, back, ways):
    return pl.pallas_call(
        merge_kernel,
        out_shape=(jax.ShapeDtypeStruct((ROWS, HD), BF16), jax.ShapeDtypeStruct((ways, 1, HD), F32)),
        in_specs=[VMEM] * 3,
        out_specs=(VMEM, VMEM),
        name="merge",
    )(mixed, log, back)


def norm_kernel(attn_ref, square_ref, gain_ref, out_ref):
    ways = square_ref.shape[0]
    line = square_ref[0]
    for i in range(1, ways):
        line = line + square_ref[i]
    line = jnp.broadcast_to(line, (PAIRS, HD))
    total = jnp.sum(jnp.where(iota((PAIRS, HD), 0) == iota((PAIRS, HD), 1), line, 0.0), axis=1, keepdims=True)
    scale = lax.rsqrt(total / (ways * HEADS * HD) + 1e-5)
    for h in range(HEADS):
        wide = attn_ref[h * PAIRS : (h + 1) * PAIRS, :].astype(F32)
        out = wide * scale * gain_ref[h : h + 1, :]
        for t in range(STEPS):
            out_ref[t, :, h * HD : (h + 1) * HD] = out[t * REQS : (t + 1) * REQS].astype(BF16)


def normalize(attn, square, gain):
    return pl.pallas_call(
        norm_kernel,
        out_shape=jax.ShapeDtypeStruct((STEPS, REQS, HEADS * HD), BF16),
        in_specs=[VMEM] * 3,
        out_specs=VMEM,
        name="normalize",
    )(attn, square, gain)


def body(
    lookup_vectors,
    fresh_token_memory,
    unfinished_block_memory,
    cache_block_store,
    sequence_block_index,
    sequence_history_count,
    unfinished_block_fill,
    migration_sender_block,
    migration_receiver_server,
    switch_moment,
    output_scaling_weights,
):
    ways = lax.axis_size("tp")
    half = lax.axis_index("zh").astype(I32).reshape(1)
    pool = cache_block_store.reshape(POOL, 2 * PAGE, HD)
    unfinished = unfinished_block_memory.reshape(REQS, 2 * PAGE, HD)
    fresh = fresh_token_memory.reshape(STEPS, REQS, 2, HD)
    gain = output_scaling_weights.reshape(HEADS, HD)
    fill, switch = unfinished_block_fill, switch_moment

    outgoing = send_tiles(
        half, migration_receiver_server.reshape(MIGS), migration_sender_block, fill, switch, pool, unfinished, fresh
    )
    tiles = lax.all_to_all(outgoing, ("y", "zl", "x"), split_axis=0, concat_axis=0, tiled=True)
    tiles = tiles.reshape(PEERS, 4, 2 * PAGE, HD)

    query = jnp.transpose(lookup_vectors, (2, 0, 1, 3)).reshape(ROWS, HD)
    pool_count, near_count, far_count = count_tokens(half, sequence_history_count, switch, sequence_block_index)
    far_rows = far_count.reshape(PAIRS, TOKENS // HD, HD).transpose(1, 0, 2).reshape(PAIRS * TOKENS // HD, HD)
    request = lax.ppermute(jnp.concatenate([query, far_rows], 0), "zh", [(0, 1), (1, 0)])
    mixed, log = local_part(fill, query, pool, unfinished, fresh, pool_count)

    back = lax.ppermute(far_part(request, tiles), "zh", [(0, 1), (1, 0)])
    mixed, log = near_part(query, near_count, tiles, mixed, log)
    attn, square = merge(mixed, log, back, ways)
    square = lax.all_to_all(square, "tp", split_axis=0, concat_axis=0, tiled=True)
    return normalize(attn, square, gain)


def solution(mesh):
    devices = mesh.devices.reshape(4, 2, 2, 4, mesh.devices.shape[1])
    fine = jax.sharding.Mesh(devices, ("y", "zh", "zl", "x", "tp"))
    rep = ("y", "zh", "zl", "x")
    placed = (
        P(None, rep, "tp", None),
        P(None, rep, None, "tp", None),
        P(rep, None, None, "tp", None),
        P(rep, None, None, "tp", None),
        P(rep, None),
        P(rep),
        P(rep),
        P(rep),
        P(rep, None),
        P(rep),
        P("tp"),
    )
    return jax.shard_map(body, mesh=fine, in_specs=placed, out_specs=P(None, rep, "tp"), check_vma=False)
```

time: 173 us -> 74.2 us (0.43); the launches traced: 171 us -> 73.6 us
  local copies, waits for them, and re-layouts: 68.6 us -> 2.4 us
  other arithmetic: 22.2 us -> 0.01 us
  waiting for transfers between devices: 29.4 us -> 8.85 us
  Pallas kernels: 0 us -> 17.3 us
  matrix products: 7.86 us -> 0 us
  blocking collectives: 22.2 us -> 27.4 us
  starting transfers between devices: 19.7 us -> 17.7 us
    gather x6 -> x0, local copies, waits for them, and re-layouts: 53.4 us -> none  [the longest x4 50.5 us: token_validity(): arrival_length[jnp.clip(entry - pool_page_tiles, 0, arrival_length.shape[...]
    all_to_all x0 -> x1, blocking collectives: none -> 27.4 us  [body(): lax.all_to_all(square, 'tp', split_axis=0, concat_axis=0, tiled=True)]
    all_to_all x2 -> x1, waiting for transfers between devices: 29.4 us -> 4.99 us  [body(): lax.all_to_all(outgoing, ('y', 'zl', 'x'), split_axis=0, concat_axis=0, t...]
    psum x1 -> x0, blocking collectives: 22.2 us -> none  [body(): squared = lax.psum(jnp.sum(wide * wide, axis=-1, keepdims=True), 'tp')]
    pallas_call x0 -> x7, Pallas kernels: none -> 17.3 us  [the longest x1 2.89 us: local_part(): pl.pallas_call(local_kernel, out_shape=(shape, shape), in_specs=[SMEM] +...]
    all_to_all x2 -> x1, starting transfers between devices: 19.7 us -> 9.35 us  [body(): lax.all_to_all(outgoing, ('y', 'zl', 'x'), split_axis=0, concat_axis=0, t...]
    ppermute x0 -> x2, starting transfers between devices: none -> 8.32 us  [the longest x1 4.9 us: body(): lax.ppermute(jnp.concatenate([query, far_rows], 0), 'zh', [(0, 1), (1, 0)])]
    dot_general x15 -> x0, matrix products: 7.86 us -> none  [the longest x6 3.94 us: pick_rows(): jnp.dot(selector.astype(jnp.bfloat16), flat, preferred_element_type=jnp.f...]
  transfers between devices with their start and end apart: 2 -> 3, of which waited for: 2 -> 2; matrix products, arithmetic and copies ran while one was open for 4% -> 1% of each run, Pallas kernels for 0% -> 11%
where the time goes in v1:
time: 74.2 us; the launch traced here: 73.6 us
  blocking collectives  27.4 us (37%)
  starting transfers between devices  17.7 us (24%)
  Pallas kernels  17.3 us (23%)
  waiting for transfers between devices  8.85 us (12%)
  local copies, waits for them, and re-layouts  2.4 us (3%)
    all_to_all x1, blocking collectives, body(): lax.all_to_all(square, 'tp', split_axis=0, concat_axis=0, tiled=True)  27.4 us
    all_to_all x1, starting transfers between devices, body(): lax.all_to_all(outgoing, ('y', 'zl', 'x'), split_axis=0, concat_axis=0, t...  9.35 us
    all_to_all x1, waiting for transfers between devices, body(): lax.all_to_all(outgoing, ('y', 'zl', 'x'), split_axis=0, concat_axis=0, t...  4.99 us
    ppermute x1, starting transfers between devices, body(): lax.ppermute(jnp.concatenate([query, far_rows], 0), 'zh', [(0, 1), (1, 0)])  4.9 us
    ppermute x1, waiting for transfers between devices, body(): lax.ppermute(jnp.concatenate([query, far_rows], 0), 'zh', [(0, 1), (1, 0)])  3.86 us
    ppermute x1, starting transfers between devices, body(): back = lax.ppermute(far_part(request, tiles), 'zh', [(0, 1), (1, 0)])  3.42 us
    pallas_call x1, Pallas kernels, local_part(): pl.pallas_call(local_kernel, out_shape=(shape, shape), in_specs=[SMEM] +...  2.89 us
    pallas_call x1, Pallas kernels, send_tiles(): pl.pallas_call(send_kernel, out_shape=jax.ShapeDtypeStruct((PEERS * 4, 2...  2.87 us
  transfers between devices with their start and end apart: 3, of which 2 were waited for; matrix products, arithmetic and copies ran while one was open for 1% of the time, Pallas kernels for 11%

profile of v1, /device:TPU:1, one launch (start us, length us, event | category | flops | bytes accessed | tf_op | source)
XLA Modules:
  0.0 73.6 jit_solution(4857031722424757025)
XLA Ops:
  0.0 2.9 %send_tiles.1 = bf16[128,32,128]{2,1,0:T(8,128)(2,1)} custom-call(s32[1]{0:T(128)} %bitcast.2.half_ref, s32[64]{0:T(128)} %bitcast.31, s32[64]{0:T(128)} %source_ref.1, s32[4]{0:T(128)} %fill_ref.3, s32[4]{0:T(128)} %switch_ref.3, bf16[64,32,128]{2,1,0:T(8,128)(2,1)} %bitcast.22, bf16[4,32,128]{2,1,0:T(8,128)(2,1)} %bitcast.26, bf16[4,4,2,128]{3,2,1,0:T(2,128)(2,1)} %bitcast.28), custom_call_target="tpu_custom_call" | custom-call | flops 1000 | bytes 2097152 | tf_op jit(solution)/shard_map/send_tiles/pallas_call | solution.py:73
  2.9 0.0 copy-start.4
  2.9 9.4 %all-to-all-start = ((bf16[128,32,128]{2,1,0:T(8,128)(2,1)}), bf16[128,32,128]{2,1,0:T(8,128)(2,1)S(1)}, u32[]{:S(2)}, u32[]{:S(2)}) async-start(bf16[128,32,128]{2,1,0:T(8,128)(2,1)} %send_tiles.1), calls=%async_computation | async-start | bytes 2097152 | tf_op jit(solution)/shard_map/all_to_all | solution.py:327
  12.2 0.0 copy-done.4
  12.3 0.0 copy-start.1
  12.3 2.4 %count_tokens.1 = (bf16[16,1024]{1,0:T(8,128)(2,1)}, bf16[16,1024]{1,0:T(8,128)(2,1)}, bf16[16,1024]{1,0:T(8,128)(2,1)}) custom-call(s32[1]{0:T(128)} %bitcast.2.half_ref, s32[4]{0:T(128)} %length_ref.1, s32[4]{0:T(128)} %switch_ref.3, s32[4,128]{1,0:T(4,128)} %table_ref.1), custom_call_target="tpu_custom_call" | custom-call | flops 134217728 | bytes 262144 | tf_op jit(solution)/shard_map/count_tokens/pallas_call | solution.py:118
  14.7 0.8 %copy_bitcast_fusion = bf16[16,8,128]{2,0,1:T(8,128)(2,1)S(1)} fusion(bf16[16,1024]{1,0:T(8,128)(2,1)} %get-tuple-element.20), kind=kLoop, calls=%fused_computation.1 | loop fusion | bytes 65536 | tf_op jit(solution)/shard_map/reshape | solution.py:332
  15.4 0.0 copy-done.1
  15.5 4.9 %collective-permute-start = (bf16[384,128]{1,0:T(8,128)(2,1)S(1)}, bf16[384,128]{1,0:T(8,128)(2,1)S(1)}, u32[]{:S(2)}, u32[]{:S(2)}) collective-permute-start(bf16[384,128]{1,0:T(8,128)(2,1)S(1)} %pad_maximum_fusion), channel_id=1, source_target_pairs={{0,64},{64,0},{1,65},{65,1},{2,66},{66,2},{3,67},{67,3},{4,68},{68... | collective-permute-start | bytes 294920 | tf_op jit(solution)/shard_map/ppermute | solution.py:333
  20.4 3.9 %collective-permute-done.request_ref = bf16[384,128]{1,0:T(8,128)(2,1)S(1)} collective-permute-done((bf16[384,128]{1,0:T(8,128)(2,1)S(1)}, bf16[384,128]{1,0:T(8,128)(2,1)S(1)}, u32[]{:S(2)}, u32[]{:S(2)}) %collective-permute-start) | collective-permute-done | bytes 98336 | tf_op jit(solution)/shard_map/ppermute | solution.py:333
  24.2 0.0 copy-start.2
  24.2 5.0 %all-to-all-done = bf16[128,32,128]{2,1,0:T(8,128)(2,1)S(1)} async-done(((bf16[128,32,128]{2,1,0:T(8,128)(2,1)}), bf16[128,32,128]{2,1,0:T(8,128)(2,1)S(1)}, u32[]{:S(2)}, u32[]{:S(2)}) %all-to-all-start) | async-done | bytes 1048608 | tf_op jit(solution)/shard_map/all_to_all | solution.py:327
  29.2 0.0 copy-start
  29.2 0.0 copy-done.2
  29.2 1.0 %copy-done = bf16[128,32,128]{2,1,0:T(8,128)(2,1)} copy-done((bf16[128,32,128]{2,1,0:T(8,128)(2,1)}, bf16[128,32,128]{2,1,0:T(8,128)(2,1)S(1)}, u32[]{:S(2)}) %copy-start) | copy-done | bytes 1048600
  30.2 2.8 %far_part.1 = bf16[272,128]{1,0:T(8,128)(2,1)} custom-call(bf16[384,128]{1,0:T(8,128)(2,1)} %copy-done.2, bf16[32,4,32,128]{3,2,1,0:T(8,128)(2,1)} %bitcast.17), custom_call_target="tpu_custom_call" | custom-call | flops 268435456 | bytes 1048576 | tf_op jit(solution)/shard_map/far_part/pallas_call | solution.py:220
  33.0 3.4 %collective-permute-start.1 = (bf16[272,128]{1,0:T(8,128)(2,1)}, bf16[272,128]{1,0:T(8,128)(2,1)S(1)}, u32[]{:S(2)}, u32[]{:S(2)}) collective-permute-start(bf16[272,128]{1,0:T(8,128)(2,1)} %far_part.1), channel_id=1, source_target_pairs={{0,64},{64,0},{1,65},{65,1},{2,66},{66,2},{3,67},{67,3},{4,68},{68... | collective-permute-start | bytes 208904 | tf_op jit(solution)/shard_map/ppermute | solution.py:336
  36.4 2.9 %local_part.1 = (f32[256,128]{1,0:T(8,128)}, f32[256,128]{1,0:T(8,128)}) custom-call(s32[4]{0:T(128)} %fill_ref.3, bf16[256,128]{1,0:T(8,128)(2,1)} %bitcast.20, bf16[64,32,128]{2,1,0:T(8,128)(2,1)} %bitcast.23, bf16[4,32,128]{2,1,0:T(8,128)(2,1)} %bitcast.27, bf16[4,4,2,128]{3,2,1,0:T(2,128)(2,1)} %bitcast.29, bf16[16,1024]{1,0:T(8,128)(2,1)} %get-tuple-element.15.count_ref), custom_call_target="tpu_custom_call" | custom-call | flops 268435456 | bytes 1048576 | tf_op jit(solution)/shard_map/local_part/pallas_call | solution.py:183
  39.3 2.8 %near_part.1 = (f32[256,128]{1,0:T(8,128)}, f32[256,128]{1,0:T(8,128)}) custom-call(bf16[256,128]{1,0:T(8,128)(2,1)} %bitcast.21, bf16[16,1024]{1,0:T(8,128)(2,1)} %get-tuple-element.14.count_ref, bf16[32,4,32,128]{3,2,1,0:T(8,128)(2,1)} %bitcast.18, f32[256,128]{1,0:T(8,128)} %get-tuple-element.16.mixed_ref, f32[256,128]{1,0:T(8,128)} %get-tuple-element.17.log_ref), custom_call_target="tpu_custom_call" | custom-call | flops 268435456 | bytes 1048576 | tf_op jit(solution)/shard_map/near_part/pallas_call | solution.py:240
  42.1 0.0 collective-permute-done.1.back_ref
  42.1 0.0 copy-start.3
  42.1 0.6 copy-done.3
  42.8 1.9 %merge.1 = (bf16[256,128]{1,0:T(8,128)(2,1)}, f32[8,1,128]{2,1,0:T(1,128)}) custom-call(f32[256,128]{1,0:T(8,128)} %get-tuple-element.18.mixed_ref, f32[256,128]{1,0:T(8,128)} %get-tuple-element.19.log_ref, bf16[272,128]{1,0:T(8,128)(2,1)} %copy-done.3), custom_call_target="tpu_custom_call" | custom-call | tf_op jit(solution)/shard_map/merge/pallas_call | solution.py:269
  44.7 27.4 %all_to_all.10.square_ref = f32[8,1,128]{2,1,0:T(1,128)} all-to-all(f32[8,1,128]{2,1,0:T(1,128)} %get-tuple-element.22), channel_id=1, replica_groups=mesh['y'=4,'zh'=2,'zl'=2,'x'=4,'tp'=8] {'tp'}, dimensions={0} | all-to-all | bytes 8192 | tf_op jit(solution)/shard_map/all_to_all | solution.py:339
  72.1 1.6 %normalize.1 = bf16[4,4,2048]{2,1,0:T(4,128)(2,1)} custom-call(bf16[256,128]{1,0:T(8,128)(2,1)} %get-tuple-element.21.attn_ref, f32[8,1,128]{2,1,0:T(1,128)} %all_to_all.10.square_ref, f32[16,128]{1,0:T(8,128)} %bitcast.30), custom_call_target="tpu_custom_call" | custom-call | tf_op jit(solution)/shard_map/normalize/pallas_call | solution.py:294
  (2 shorter events, 0.0 us)
Async XLA Ops:
  2.9 9.4 %copy-start.4 = (bf16[4,4,16,128]{3,2,1,0:T(8,128)(2,1)S(1)}, bf16[4,4,16,128]{3,2,1,0:T(8,128)(2,1)}, u32[]{:S(2)}) copy-start(bf16[4,4,16,128]{3,2,1,0:T(8,128)(2,1)} %param.11) | copy-start | bytes 196612
  2.9 26.3 %all-to-all-start = ((bf16[128,32,128]{2,1,0:T(8,128)(2,1)}), bf16[128,32,128]{2,1,0:T(8,128)(2,1)S(1)}, u32[]{:S(2)}, u32[]{:S(2)}) async-start(bf16[128,32,128]{2,1,0:T(8,128)(2,1)} %send_tiles.1), calls=%async_computation | async-start | bytes 2097152 | tf_op jit(solution)/shard_map/all_to_all | solution.py:327
  12.3 3.2 %copy-start.1 = (bf16[16,4,4,128]{3,2,1,0:T(4,128)(2,1)}, bf16[16,4,4,128]{3,2,1,0:T(4,128)(2,1)S(1)}, u32[]{:S(2)}) copy-start(bf16[16,4,4,128]{3,2,1,0:T(4,128)(2,1)S(1)} %copy.12) | copy-start | bytes 196612
  15.5 8.8 %collective-permute-start = (bf16[384,128]{1,0:T(8,128)(2,1)S(1)}, bf16[384,128]{1,0:T(8,128)(2,1)S(1)}, u32[]{:S(2)}, u32[]{:S(2)}) collective-permute-start(bf16[384,128]{1,0:T(8,128)(2,1)S(1)} %pad_maximum_fusion), channel_id=1, source_target_pairs={{0,64},{64,0},{1,65},{65,1},{2,66},{66,2},{3,67},{67,3},{4,68},{68... | collective-permute-start | bytes 294920 | tf_op jit(solution)/shard_map/ppermute | solution.py:333
  24.2 5.0 %copy-start.2 = (bf16[384,128]{1,0:T(8,128)(2,1)}, bf16[384,128]{1,0:T(8,128)(2,1)S(1)}, u32[]{:S(2)}) copy-start(bf16[384,128]{1,0:T(8,128)(2,1)S(1)} %collective-permute-done.request_ref) | copy-start | bytes 294916
  29.2 1.0 %copy-start = (bf16[128,32,128]{2,1,0:T(8,128)(2,1)}, bf16[128,32,128]{2,1,0:T(8,128)(2,1)S(1)}, u32[]{:S(2)}) copy-start(bf16[128,32,128]{2,1,0:T(8,128)(2,1)S(1)} %all-to-all-done) | copy-start | bytes 3145732
  33.0 9.2 %collective-permute-start.1 = (bf16[272,128]{1,0:T(8,128)(2,1)}, bf16[272,128]{1,0:T(8,128)(2,1)S(1)}, u32[]{:S(2)}, u32[]{:S(2)}) collective-permute-start(bf16[272,128]{1,0:T(8,128)(2,1)} %far_part.1), channel_id=1, source_target_pairs={{0,64},{64,0},{1,65},{65,1},{2,66},{66,2},{3,67},{67,3},{4,68},{68... | collective-permute-start | bytes 208904 | tf_op jit(solution)/shard_map/ppermute | solution.py:336
  42.1 0.6 copy-start.3

commit v2 on v1

v2 whole, which is shorter than its diff:
```python
import jax
import jax.numpy as jnp
from jax import lax
from jax.experimental import pallas as pl
from jax.experimental.pallas import tpu as pltpu
from jax.sharding import PartitionSpec as P

STEPS, REQS, HEADS, HD = 4, 4, 16, 128
ROWS = STEPS * REQS * HEADS
PAIRS = STEPS * REQS
PAGE = 16
POOL = 64
MIGS = 64
PEERS = 32
TOKENS = POOL * PAGE
NEG = -1e30
MARK = 4096.0
SCALE = 1.4426950408889634 / HD**0.5
F32, BF16, I32 = jnp.float32, jnp.bfloat16, jnp.int32
VMEM = pl.BlockSpec(memory_space=pltpu.VMEM)
SMEM = pl.BlockSpec(memory_space=pltpu.SMEM)


def dot(a, b, ca, cb):
    return lax.dot_general(a, b, (((ca,), (cb,)), ((), ())), preferred_element_type=F32)


def iota(shape, axis):
    return lax.broadcasted_iota(I32, shape, axis)


def tail_tile(r, kv, fill, unfinished_ref, fresh_ref):
    rows = iota((PAGE, HD), 0)
    tile = unfinished_ref[r, kv * PAGE : (kv + 1) * PAGE, :].astype(F32)
    for s in range(STEPS):
        row = fresh_ref[s, r].astype(F32)[kv : kv + 1, :]
        tile = jnp.where(rows == fill + s, row, tile)
    return tile


def send_kernel(half_ref, target_ref, source_ref, fill_ref, switch_ref, pool_ref, unfinished_ref, fresh_ref, out_ref, cut_ref):
    rows = iota((PAGE, HD), 0)
    blank = jnp.concatenate([jnp.full((PAGE, HD), MARK, BF16), jnp.zeros((PAGE, HD), BF16)], 0)
    out_ref[...] = jnp.broadcast_to(blank[None], out_ref.shape)
    for r in range(REQS):
        fill = fill_ref[r]
        key = tail_tile(r, 0, fill, unfinished_ref, fresh_ref)
        value = tail_tile(r, 1, fill, unfinished_ref, fresh_ref)
        key = jnp.where(rows < fill + switch_ref[r], key, MARK)
        cut_ref[r] = jnp.concatenate([key, value], 0).astype(BF16)
    half = half_ref[0]
    low = jnp.int32(0)
    high = jnp.int32(0)
    for e in range(MIGS):
        t = target_ref[e]
        m = source_ref[e]
        first = t < 32
        shift = t & 31
        word = jnp.where(first, low, high)
        rank = (word >> shift) & 1
        word = word | (jnp.int32(1) << shift)
        low = jnp.where(first, word, low)
        high = jnp.where(first, high, word)
        peer = ((t >> 4) << 3) | (t & 7)
        which = ((t >> 3) & 1) ^ half
        slot = peer * 4 + which * 2 + rank
        pooled = pool_ref[jnp.minimum(m, POOL - 1)]
        cut = cut_ref[jnp.maximum(m - POOL, 0)]
        out_ref[slot] = jnp.where(m < POOL, pooled, cut)


def keep(*arrays):
    return tuple(pltpu.with_memory_space_constraint(x, pltpu.VMEM) for x in arrays)


def send_tiles(half, target, source, fill, switch, pool, unfinished, fresh):
    return pl.pallas_call(
        send_kernel,
        out_shape=pltpu.VMEM((PEERS * 4, 2 * PAGE, HD), BF16),
        in_specs=[SMEM] * 5 + [VMEM] * 3,
        out_specs=VMEM,
        scratch_shapes=[pltpu.VMEM((REQS, 2 * PAGE, HD), BF16)],
        cost_estimate=pl.CostEstimate(flops=1000, bytes_accessed=2**21, transcendentals=0),
        name="send_tiles",
    )(half, target, source, fill, switch, pool, unfinished, fresh)


def request_kernel(length_ref, switch_ref, query_ref, table_ref, out_ref):
    out_ref[:ROWS, :] = query_ref[...]
    row, lane = iota((16, HD), 0), iota((16, HD), 1)
    info = jnp.concatenate([table_ref[...], jnp.zeros((16 - REQS, HD), I32)], 0)
    for g in range(REQS):
        length = length_ref[g]
        at = row - REQS
        fact = jnp.where(at == 0, length >> 4, jnp.where(at == 1, length & 15, switch_ref[g]))
        info = jnp.where((lane == g) & (at >= 0) & (at < 3), fact, info)
    out_ref[ROWS:, :] = info.astype(F32).astype(BF16)


def request_rows(length, switch, query, table):
    return pl.pallas_call(
        request_kernel,
        out_shape=pltpu.VMEM((ROWS + 16, HD), BF16),
        in_specs=[SMEM] * 2 + [VMEM] * 2,
        out_specs=VMEM,
        cost_estimate=pl.CostEstimate(flops=1000, bytes_accessed=2**17, transcendentals=0),
        name="request_rows",
    )(length, switch, query, table)


def bias_kernel(sections, half_ref, request_ref, *refs):
    info = request_ref[ROWS:, :].astype(F32).astype(I32)
    half = half_ref[0]
    token = iota((TOKENS, HD), 0)
    entry = iota((TOKENS, HD), 1)
    place, offset = token // PAGE, token % PAGE
    lane = iota((1, HD), 1)
    pair, part = lane % PAIRS, lane // PAIRS
    step, req = pair // REQS, pair % REQS
    inside, weights = [], []
    late = jnp.zeros((1, HD), jnp.bool_)
    for g in range(REQS):
        pages, rest, moment = (info[REQS + i : REQS + i + 1, g : g + 1] for i in range(3))
        inside.append(entry * PAGE + offset < pages * PAGE + rest)
        late = late | ((req == g) & (step < moment))
        spread = iota((HD, HD), 1)
        weights.append(((spread % REQS == g) & (spread < 3 * PAIRS)).astype(BF16))
    weights = jnp.concatenate(weights, 0)
    for section, ref in zip(sections, refs, strict=True):
        if section == "pool":
            page = place
        else:
            page = POOL + (place // 16) * 32 + half * 16 + place % 16
        hits = [jnp.where((info[g : g + 1, :] == page) & inside[g], 1.0, 0.0).astype(BF16) for g in range(REQS)]
        count = dot(jnp.concatenate(hits, 1), weights, 1, 0)
        log = jnp.log2(jnp.maximum(count, 1.0)) / SCALE
        high = log.astype(BF16).astype(F32)
        middle = (log - high).astype(BF16).astype(F32)
        parts = jnp.where(part == 0, high, jnp.where(part == 1, middle, log - high - middle))
        gone = count == 0
        if section != "pool":
            gone = gone | late
        ref[...] = jnp.where(gone, jnp.where(part == 0, NEG, 0.0), parts).astype(BF16)


def token_bias(sections, half, request):
    out = pltpu.VMEM((TOKENS, HD), BF16)
    return pl.pallas_call(
        lambda *refs: bias_kernel(sections, *refs),
        out_shape=(out,) * len(sections),
        in_specs=[SMEM, VMEM],
        out_specs=(VMEM,) * len(sections),
        cost_estimate=pl.CostEstimate(flops=2**27, bytes_accessed=2**18, transcendentals=0),
        name="token_bias",
    )(half, *keep(request))


def attend(query, key, value, bias):
    lane, row = iota((ROWS, HD), 1), iota((ROWS, HD), 0)
    reads = ((lane % PAIRS == row % PAIRS) & (lane < 3 * PAIRS)).astype(BF16)
    scores = dot(jnp.concatenate([query, reads], 1), jnp.concatenate([key, bias], 1), 1, 1)
    top = jnp.max(scores, axis=-1, keepdims=True)
    probs = jnp.exp2((scores - top) * SCALE).astype(BF16)
    mixed = dot(probs, jnp.concatenate([value, jnp.ones(value.shape, BF16)], 1), 1, 0)
    total = mixed[:, HD:]
    return mixed[:, :HD] / total, top * SCALE + jnp.log2(total)


def combine(a, b):
    (x, p), (y, q) = a, b
    top = jnp.maximum(p, q)
    u, v = jnp.exp2(p - top), jnp.exp2(q - top)
    return (x * u + y * v) / (u + v), top + jnp.log2(u + v)


def local_kernel(fill_ref, request_ref, pool_ref, unfinished_ref, fresh_ref, bias_ref, mixed_ref, log_ref):
    tail = 2 * REQS * PAGE
    keys = [pool_ref[:, :PAGE, :].reshape(TOKENS, HD)]
    values = [pool_ref[:, PAGE:, :].reshape(TOKENS, HD)]
    token, lane = iota((tail, HD), 0), iota((tail, HD), 1)
    step, req = lane % PAIRS // REQS, lane % REQS
    held = jnp.zeros((tail, HD), I32)
    for r in range(REQS):
        fill = fill_ref[r]
        keys.append(tail_tile(r, 0, fill, unfinished_ref, fresh_ref).astype(BF16))
        values.append(tail_tile(r, 1, fill, unfinished_ref, fresh_ref).astype(BF16))
        held = jnp.where(req == r, fill, held)
    keys.append(jnp.zeros((tail // 2, HD), BF16))
    values.append(jnp.zeros((tail // 2, HD), BF16))
    valid = (token // PAGE == req) & (token % PAGE < held + step + 1)
    bias = jnp.where((lane >= PAIRS) | valid, 0.0, NEG).astype(BF16)
    bias = jnp.concatenate([bias_ref[...], bias], 0)
    mixed, log = attend(request_ref[:ROWS, :], jnp.concatenate(keys, 0), jnp.concatenate(values, 0), bias)
    mixed_ref[...] = mixed
    log_ref[...] = log


def local_part(fill, request, pool, unfinished, fresh, bias):
    out = pltpu.VMEM((ROWS, HD), F32)
    request, bias = keep(request, bias)
    return pl.pallas_call(
        local_kernel,
        out_shape=(out, out),
        in_specs=[SMEM] + [VMEM] * 5,
        out_specs=(VMEM, VMEM),
        cost_estimate=pl.CostEstimate(flops=2**28, bytes_accessed=2**20, transcendentals=2**18),
        name="local_part",
    )(fill, request, pool, unfinished, fresh, bias)


def arrived_part(request_ref, bias_ref, tiles_ref, which):
    tiles = tiles_ref[:, 2 * which : 2 * which + 2]
    key = tiles[:, :, :PAGE, :].reshape(TOKENS, HD)
    value = tiles[:, :, PAGE:, :].reshape(TOKENS, HD)
    bias = jnp.where(key > MARK / 2, jnp.asarray(NEG, BF16), bias_ref[...])
    return attend(request_ref[:ROWS, :], key, value, bias)


def far_kernel(request_ref, bias_ref, tiles_ref, after_ref, out_ref):
    mixed, log = arrived_part(request_ref, bias_ref, tiles_ref, 1)
    out_ref[:ROWS, :] = mixed.astype(BF16)
    lane = iota((ROWS, HD), 1)
    high = log.astype(BF16).astype(F32)
    middle = (log - high).astype(BF16).astype(F32)
    least = log - high - middle
    parts = jnp.where(lane == 0, high, jnp.where(lane == 1, middle, jnp.where(lane == 2, least, 0.0)))
    eye = (iota((8, HD), 0) == iota((8, HD), 1)).astype(BF16)
    across = dot(eye, parts.astype(BF16), 1, 1)
    out_ref[ROWS:, :] = jnp.concatenate([across[:, :HD], across[:, HD:]], 0).astype(BF16)


def far_part(request, bias, tiles, after):
    return pl.pallas_call(
        far_kernel,
        out_shape=pltpu.VMEM((ROWS + 16, HD), BF16),
        in_specs=[VMEM] * 3 + [pl.BlockSpec(memory_space=pl.ANY)],
        out_specs=VMEM,
        cost_estimate=pl.CostEstimate(flops=2**28, bytes_accessed=2**20, transcendentals=2**18),
        name="far_part",
    )(*keep(request, bias, tiles, after))


def near_kernel(request_ref, bias_ref, tiles_ref, mixed_ref, log_ref, out_ref, sum_ref):
    part = arrived_part(request_ref, bias_ref, tiles_ref, 0)
    mixed, log = combine((mixed_ref[...], log_ref[...]), part)
    out_ref[...] = mixed
    sum_ref[...] = log


def near_part(request, bias, tiles, mixed, log):
    out = pltpu.VMEM((ROWS, HD), F32)
    return pl.pallas_call(
        near_kernel,
        out_shape=(out, out),
        in_specs=[VMEM] * 5,
        out_specs=(VMEM, VMEM),
        cost_estimate=pl.CostEstimate(flops=2**28, bytes_accessed=2**20, transcendentals=2**18),
        name="near_part",
    )(*keep(request, bias, tiles, mixed, log))


def merge_kernel(mixed_ref, log_ref, back_ref, attn_ref, square_ref):
    stats = back_ref[ROWS:, :].astype(F32)
    stats = jnp.concatenate([stats[:8], stats[8:]], 1).astype(BF16)
    log = dot(stats, jnp.ones((8, HD), BF16), 0, 0)
    mixed, _ = combine((mixed_ref[...], log_ref[...]), (back_ref[:ROWS, :].astype(F32), log))
    attn = mixed.astype(BF16)
    attn_ref[...] = attn
    wide = attn.astype(F32)
    square = wide * wide
    total = square[:PAIRS]
    for h in range(1, HEADS):
        total = total + square[h * PAIRS : (h + 1) * PAIRS]
    total = jnp.sum(total, axis=-1, keepdims=True)
    line = jnp.sum(jnp.where(iota((PAIRS, HD), 0) == iota((PAIRS, HD), 1), total, 0.0), axis=0, keepdims=True)
    square_ref[...] = jnp.broadcast_to(line[None], square_ref.shape)


def merge(mixed, log, back, ways):
    return pl.pallas_call(
        merge_kernel,
        out_shape=(pltpu.VMEM((ROWS, HD), BF16), pltpu.VMEM((ways, 1, HD), F32)),
        in_specs=[VMEM] * 3,
        out_specs=(VMEM, VMEM),
        name="merge",
    )(*keep(mixed, log, back))


def norm_kernel(attn_ref, square_ref, gain_ref, out_ref):
    ways = square_ref.shape[0]
    line = square_ref[0]
    for i in range(1, ways):
        line = line + square_ref[i]
    line = jnp.broadcast_to(line, (PAIRS, HD))
    total = jnp.sum(jnp.where(iota((PAIRS, HD), 0) == iota((PAIRS, HD), 1), line, 0.0), axis=1, keepdims=True)
    scale = lax.rsqrt(total / (ways * HEADS * HD) + 1e-5)
    for h in range(HEADS):
        wide = attn_ref[h * PAIRS : (h + 1) * PAIRS, :].astype(F32)
        out = wide * scale * gain_ref[h : h + 1, :]
        for t in range(STEPS):
            out_ref[t, :, h * HD : (h + 1) * HD] = out[t * REQS : (t + 1) * REQS].astype(BF16)


def normalize(attn, square, gain):
    return pl.pallas_call(
        norm_kernel,
        out_shape=jax.ShapeDtypeStruct((STEPS, REQS, HEADS * HD), BF16),
        in_specs=[VMEM] * 3,
        out_specs=VMEM,
        name="normalize",
    )(*keep(attn, square, gain))


def body(
    lookup_vectors,
    fresh_token_memory,
    unfinished_block_memory,
    cache_block_store,
    sequence_block_index,
    sequence_history_count,
    unfinished_block_fill,
    migration_sender_block,
    migration_receiver_server,
    switch_moment,
    output_scaling_weights,
):
    ways = lax.axis_size("tp")
    half = lax.axis_index("zh").astype(I32).reshape(1)
    pool = cache_block_store.reshape(POOL, 2 * PAGE, HD)
    unfinished = unfinished_block_memory.reshape(REQS, 2 * PAGE, HD)
    fresh = fresh_token_memory.reshape(STEPS, REQS, 2, HD)
    gain = output_scaling_weights.reshape(HEADS, HD)
    fill, switch = unfinished_block_fill, switch_moment

    outgoing = send_tiles(
        half, migration_receiver_server.reshape(MIGS), migration_sender_block, fill, switch, pool, unfinished, fresh
    )
    tiles = lax.all_to_all(outgoing, ("y", "zl", "x"), split_axis=0, concat_axis=0, tiled=True)
    tiles = tiles.reshape(PEERS, 4, 2 * PAGE, HD)

    query = jnp.transpose(lookup_vectors, (2, 0, 1, 3)).reshape(ROWS, HD)
    request = request_rows(sequence_history_count, switch, query, sequence_block_index)
    asked = lax.ppermute(request, "zh", [(0, 1), (1, 0)])
    pool_bias, near_bias = token_bias(("pool", "arrived"), half, request)
    mixed, log = local_part(fill, request, pool, unfinished, fresh, pool_bias)
    (far_bias,) = token_bias(("arrived",), half, asked)

    back = lax.ppermute(far_part(asked, far_bias, tiles, log), "zh", [(0, 1), (1, 0)])
    mixed, log = near_part(request, near_bias, tiles, mixed, log)
    attn, square = merge(mixed, log, back, ways)
    square = lax.all_to_all(square, "tp", split_axis=0, concat_axis=0, tiled=True)
    return normalize(attn, square, gain)


def solution(mesh):
    devices = mesh.devices.reshape(4, 2, 2, 4, mesh.devices.shape[1])
    fine = jax.sharding.Mesh(devices, ("y", "zh", "zl", "x", "tp"))
    rep = ("y", "zh", "zl", "x")
    placed = (
        P(None, rep, "tp", None),
        P(None, rep, None, "tp", None),
        P(rep, None, None, "tp", None),
        P(rep, None, None, "tp", None),
        P(rep, None),
        P(rep),
        P(rep),
        P(rep),
        P(rep, None),
        P(rep),
        P("tp"),
    )
    return jax.shard_map(body, mesh=fine, in_specs=placed, out_specs=P(None, rep, "tp"), check_vma=False)
```

time: 74.2 us -> 66.6 us (0.90)
  Pallas kernels: 17.3 us -> 10.7 us
  blocking collectives: 27.4 us -> 29.5 us
  waiting for transfers between devices: 8.85 us -> 6.89 us
  local copies, waits for them, and re-layouts: 2.4 us -> 0.66 us
    pallas_call x6 -> x8, Pallas kernels: 15.7 us -> 9.94 us  [the longest x1 2.86 us: send_tiles(): pl.pallas_call(send_kernel, out_shape=pltpu.VMEM((PEERS * 4, 2 * PAGE, HD...]
    all_to_all x1, blocking collectives: 27.4 us -> 29.5 us  [body(): lax.all_to_all(square, 'tp', split_axis=0, concat_axis=0, tiled=True)]
    unnamed x10 -> x4, local copies, waits for them, and re-layouts: 1.61 us -> 0.01 us
    ppermute x2, waiting for transfers between devices: 3.86 us -> 2.66 us  [the longest x1 1.7 us: body(): asked = lax.ppermute(request, 'zh', [(0, 1), (1, 0)])]
    pallas_call x1, Pallas kernels: 1.59 us -> 0.75 us  [normalize(): pl.pallas_call(norm_kernel, out_shape=jax.ShapeDtypeStruct((STEPS, REQS,...]
    all_to_all x1, waiting for transfers between devices: 4.99 us -> 4.22 us  [body(): lax.all_to_all(outgoing, ('y', 'zl', 'x'), split_axis=0, concat_axis=0, t...]
    reshape x1 -> x0, local copies, waits for them, and re-layouts: 0.76 us -> none  [body(): far_count.reshape(PAIRS, TOKENS // HD, HD).transpose(1, 0, 2)]
  transfers between devices with their start and end apart: 3 -> 3, of which waited for: 2 -> 3; matrix products, arithmetic and copies ran while one was open for 1% -> 1% of each run, Pallas kernels for 11% -> 9%
where the time goes in v2:
time: 66.6 us; the launch traced here: 66.1 us
  blocking collectives  29.5 us (44%)
  starting transfers between devices  18.3 us (27%)
  Pallas kernels  10.7 us (16%)
  waiting for transfers between devices  6.89 us (10%)
    all_to_all x1, blocking collectives, body(): lax.all_to_all(square, 'tp', split_axis=0, concat_axis=0, tiled=True)  29.5 us
    all_to_all x1, starting transfers between devices, body(): lax.all_to_all(outgoing, ('y', 'zl', 'x'), split_axis=0, concat_axis=0, t...  9.35 us
    ppermute x1, starting transfers between devices, body(): asked = lax.ppermute(request, 'zh', [(0, 1), (1, 0)])  4.9 us
    all_to_all x1, waiting for transfers between devices, body(): lax.all_to_all(outgoing, ('y', 'zl', 'x'), split_axis=0, concat_axis=0, t...  4.22 us
    ppermute x1, starting transfers between devices, body(): lax.ppermute(far_part(asked, far_bias, tiles, log), 'zh', [(0, 1), (1, 0)])  4.05 us
    pallas_call x1, Pallas kernels, send_tiles(): pl.pallas_call(send_kernel, out_shape=pltpu.VMEM((PEERS * 4, 2 * PAGE, HD...  2.86 us
    pallas_call x1, Pallas kernels, local_part(): pl.pallas_call(local_kernel, out_shape=(out, out), in_specs=[SMEM] + [VME...  2.08 us
    pallas_call x2, Pallas kernels, token_bias(): pl.pallas_call(lambda *refs: bias_kernel(sections, *refs), out_shape=(out...  1.89 us
  transfers between devices with their start and end apart: 3, of which 3 were waited for; matrix products, arithmetic and copies ran while one was open for 1% of the time, Pallas kernels for 9%

profile of v2, /device:TPU:1, one launch (start us, length us, event | category | flops | bytes accessed | tf_op | source)
XLA Modules:
  0.0 66.1 jit_solution(8611142311943501721)
XLA Ops:
  0.0 2.9 %send_tiles.1 = bf16[128,32,128]{2,1,0:T(8,128)(2,1)} custom-call(s32[1]{0:T(128)} %bitcast.2.refs_0_.half_ref, s32[64]{0:T(128)} %bitcast.20, s32[64]{0:T(128)} %source_ref.1, s32[4]{0:T(128)} %fill_ref.3, s32[4]{0:T(128)} %switch_ref.3, bf16[64,32,128]{2,1,0:T(8,128)(2,1)} %bitcast.12, bf16[4,32,128]{2,1,0:T(8,128)(2,1)} %bitcast.16, ...), custom_call_target="tpu_custom_call" | custom-call | flops 1000 | bytes 2097152 | tf_op jit(solution)/shard_map/send_tiles/pallas_call | solution.py:77
  2.9 0.0 copy-start.1
  2.9 9.4 %all-to-all-start = ((bf16[128,32,128]{2,1,0:T(8,128)(2,1)}), bf16[128,32,128]{2,1,0:T(8,128)(2,1)S(1)}, u32[]{:S(2)}, u32[]{:S(2)}) async-start(bf16[128,32,128]{2,1,0:T(8,128)(2,1)} %send_tiles.1), calls=%async_computation | async-start | bytes 2097152 | tf_op jit(solution)/shard_map/all_to_all | solution.py:338
  12.2 0.0 copy-done.1
  12.2 0.7 copy.12
  12.9 0.9 %request_rows.1.refs_1_.request_ref = bf16[272,128]{1,0:T(8,128)(2,1)S(1)} custom-call(s32[4]{0:T(128)} %length_ref.1, s32[4]{0:T(128)} %switch_ref.3, bf16[256,128]{1,0:T(8,128)(2,1)} %bitcast.14, s32[4,128]{1,0:T(4,128)} %table_ref.1), custom_call_target="tpu_custom_call" | custom-call | flops 1000 | bytes 131072 | tf_op jit(solution)/shard_map/request_rows/pallas_call | solution.py:101
  13.8 4.9 %collective-permute-start = (bf16[272,128]{1,0:T(8,128)(2,1)S(1)}, bf16[272,128]{1,0:T(8,128)(2,1)S(1)}, u32[]{:S(2)}, u32[]{:S(2)}) collective-permute-start(bf16[272,128]{1,0:T(8,128)(2,1)S(1)} %request_rows.1.refs_1_.request_ref), channel_id=1, source_target_pairs={{0,64},{64,0},{1,65},{65,1},{2,66},{66,2},{3,67},{67,3},{4,68},{68... | collective-permute-start | bytes 208904 | tf_op jit(solution)/shard_map/ppermute | solution.py:343
  18.7 1.1 %token_bias.2 = (bf16[1024,128]{1,0:T(8,128)(2,1)S(1)}, bf16[1024,128]{1,0:T(8,128)(2,1)S(1)}) custom-call(s32[1]{0:T(128)} %bitcast.2.refs_0_.half_ref, bf16[272,128]{1,0:T(8,128)(2,1)S(1)} %request_rows.1.refs_1_.request_ref), custom_call_target="tpu_custom_call" | custom-call | flops 134217728 | bytes 262144 | tf_op jit(solution)/shard_map/token_bias/pallas_call | solution.py:148
  19.8 2.1 %local_part.1 = (f32[256,128]{1,0:T(8,128)S(1)}, f32[256,128]{1,0:T(8,128)S(1)}) custom-call(s32[4]{0:T(128)} %fill_ref.3, bf16[272,128]{1,0:T(8,128)(2,1)S(1)} %request_rows.1.refs_1_.request_ref, bf16[64,32,128]{2,1,0:T(8,128)(2,1)} %bitcast.13, bf16[4,32,128]{2,1,0:T(8,128)(2,1)} %bitcast.17, bf16[4,4,2,128]{3,2,1,0:T(2,128)(2,1)} %bitcast.19, ...), custom_call_target="tpu_custom_call" | custom-call | flops 268435456 | bytes 1048576 | tf_op jit(solution)/shard_map/local_part/pallas_call | solution.py:201
  21.9 1.7 %collective-permute-done.refs_1_.request_ref = bf16[272,128]{1,0:T(8,128)(2,1)S(1)} collective-permute-done((bf16[272,128]{1,0:T(8,128)(2,1)S(1)}, bf16[272,128]{1,0:T(8,128)(2,1)S(1)}, u32[]{:S(2)}, u32[]{:S(2)}) %collective-permute-start) | collective-permute-done | bytes 69664 | tf_op jit(solution)/shard_map/ppermute | solution.py:343
  23.6 0.8 %token_bias.3.bias_ref = bf16[1024,128]{1,0:T(8,128)(2,1)S(1)} custom-call(s32[1]{0:T(128)} %bitcast.2.refs_0_.half_ref, bf16[272,128]{1,0:T(8,128)(2,1)S(1)} %collective-permute-done.refs_1_.request_ref), custom_call_target="tpu_custom_call" | custom-call | flops 134217728 | bytes 262144 | tf_op jit(solution)/shard_map/token_bias/pallas_call | solution.py:148
  24.4 4.2 %all-to-all-done = bf16[128,32,128]{2,1,0:T(8,128)(2,1)S(1)} async-done(((bf16[128,32,128]{2,1,0:T(8,128)(2,1)}), bf16[128,32,128]{2,1,0:T(8,128)(2,1)S(1)}, u32[]{:S(2)}, u32[]{:S(2)}) %all-to-all-start) | async-done | bytes 1048608 | tf_op jit(solution)/shard_map/all_to_all | solution.py:338
  28.6 1.0 %far_part.1 = bf16[272,128]{1,0:T(8,128)(2,1)S(1)} custom-call(bf16[272,128]{1,0:T(8,128)(2,1)S(1)} %collective-permute-done.refs_1_.request_ref, bf16[1024,128]{1,0:T(8,128)(2,1)S(1)} %token_bias.3.bias_ref, bf16[32,4,32,128]{3,2,1,0:T(8,128)(2,1)S(1)} %bitcast.9, f32[256,128]{1,0:T(8,128)S(1)} %get-tuple-element.16.log_ref.after_ref), custom_call_target="tpu_custom_call" | custom-call | flops 268435456 | bytes 1048576 | tf_op jit(solution)/shard_map/far_part/pallas_call | solution.py:233
  29.6 4.0 %collective-permute-start.1 = (bf16[272,128]{1,0:T(8,128)(2,1)S(1)}, bf16[272,128]{1,0:T(8,128)(2,1)S(1)}, u32[]{:S(2)}, u32[]{:S(2)}) collective-permute-start(bf16[272,128]{1,0:T(8,128)(2,1)S(1)} %far_part.1), channel_id=1, source_target_pairs={{0,64},{64,0},{1,65},{65,1},{2,66},{66,2},{3,67},{67,3},{4,68},{68... | collective-permute-start | bytes 208904 | tf_op jit(solution)/shard_map/ppermute | solution.py:348
  33.6 0.9 %near_part.1 = (f32[256,128]{1,0:T(8,128)S(1)}, f32[256,128]{1,0:T(8,128)S(1)}) custom-call(bf16[272,128]{1,0:T(8,128)(2,1)S(1)} %request_rows.1.refs_1_.request_ref, bf16[1024,128]{1,0:T(8,128)(2,1)S(1)} %get-tuple-element.13.bias_ref, bf16[32,4,32,128]{3,2,1,0:T(8,128)(2,1)S(1)} %bitcast.10, f32[256,128]{1,0:T(8,128)S(1)} %get-tuple-element.15.mixed_ref, ...), custom_call_target="tpu_custom_call" | custom-call | flops 268435456 | bytes 1048576 | tf_op jit(solution)/shard_map/near_part/pallas_call | solution.py:252
  34.6 1.0 %collective-permute-done.1.back_ref = bf16[272,128]{1,0:T(8,128)(2,1)S(1)} collective-permute-done((bf16[272,128]{1,0:T(8,128)(2,1)S(1)}, bf16[272,128]{1,0:T(8,128)(2,1)S(1)}, u32[]{:S(2)}, u32[]{:S(2)}) %collective-permute-start.1) | collective-permute-done | bytes 69664 | tf_op jit(solution)/shard_map/ppermute | solution.py:348
  35.5 0.3 merge.1
  35.9 0.0 copy-start
  35.9 29.5 %all_to_all.10.square_ref = f32[8,1,128]{2,1,0:T(1,128)S(1)} all-to-all(f32[8,1,128]{2,1,0:T(1,128)S(1)} %get-tuple-element.20), channel_id=1, replica_groups=mesh['y'=4,'zh'=2,'zl'=2,'x'=4,'tp'=8] {'tp'}, dimensions={0} | all-to-all | bytes 8192 | tf_op jit(solution)/shard_map/all_to_all | solution.py:351
  65.4 0.0 copy-done
  65.4 0.7 %normalize.1 = bf16[4,4,2048]{2,1,0:T(4,128)(2,1)} custom-call(bf16[256,128]{1,0:T(8,128)(2,1)S(1)} %get-tuple-element.19.attn_ref, f32[8,1,128]{2,1,0:T(1,128)S(1)} %all_to_all.10.square_ref, f32[16,128]{1,0:T(8,128)S(1)} %bitcast.11), custom_call_target="tpu_custom_call" | custom-call | tf_op jit(solution)/shard_map/normalize/pallas_call | solution.py:305
Async XLA Ops:
  2.9 9.4 %copy-start.1 = (bf16[4,4,16,128]{3,2,1,0:T(8,128)(2,1)S(1)}, bf16[4,4,16,128]{3,2,1,0:T(8,128)(2,1)}, u32[]{:S(2)}) copy-start(bf16[4,4,16,128]{3,2,1,0:T(8,128)(2,1)} %param.11) | copy-start | bytes 196612
  2.9 25.7 %all-to-all-start = ((bf16[128,32,128]{2,1,0:T(8,128)(2,1)}), bf16[128,32,128]{2,1,0:T(8,128)(2,1)S(1)}, u32[]{:S(2)}, u32[]{:S(2)}) async-start(bf16[128,32,128]{2,1,0:T(8,128)(2,1)} %send_tiles.1), calls=%async_computation | async-start | bytes 2097152 | tf_op jit(solution)/shard_map/all_to_all | solution.py:338
  13.8 9.8 %collective-permute-start = (bf16[272,128]{1,0:T(8,128)(2,1)S(1)}, bf16[272,128]{1,0:T(8,128)(2,1)S(1)}, u32[]{:S(2)}, u32[]{:S(2)}) collective-permute-start(bf16[272,128]{1,0:T(8,128)(2,1)S(1)} %request_rows.1.refs_1_.request_ref), channel_id=1, source_target_pairs={{0,64},{64,0},{1,65},{65,1},{2,66},{66,2},{3,67},{67,3},{4,68},{68... | collective-permute-start | bytes 208904 | tf_op jit(solution)/shard_map/ppermute | solution.py:343
  29.6 6.0 %collective-permute-start.1 = (bf16[272,128]{1,0:T(8,128)(2,1)S(1)}, bf16[272,128]{1,0:T(8,128)(2,1)S(1)}, u32[]{:S(2)}, u32[]{:S(2)}) collective-permute-start(bf16[272,128]{1,0:T(8,128)(2,1)S(1)} %far_part.1), channel_id=1, source_target_pairs={{0,64},{64,0},{1,65},{65,1},{2,66},{66,2},{3,67},{67,3},{4,68},{68... | collective-permute-start | bytes 208904 | tf_op jit(solution)/shard_map/ppermute | solution.py:348
  35.9 29.5 %copy-start = (f32[2048]{0:T(1024)S(1)}, f32[2048]{0:T(1024)}, u32[]{:S(2)}) copy-start(f32[2048]{0:T(1024)} %param.21) | copy-start | bytes 24580

commit v3 on v2

--- a/solution.py
+++ b/solution.py
@@ -16,6 +16,9 @@
 NEG = -1e30
 MARK = 4096.0
 SCALE = 1.4426950408889634 / HD**0.5
+HALVES = [[p for p in reversed(range(64)) if (p >> 3) & 1 == half] for half in range(2)]
+PARTNERS = [(p, p ^ 8) for p in range(64)]
+SUMMED = [[4, 5, 2, 3, 6, 7, 0, 1]]
 F32, BF16, I32 = jnp.float32, jnp.bfloat16, jnp.int32
 VMEM = pl.BlockSpec(memory_space=pltpu.VMEM)
 SMEM = pl.BlockSpec(memory_space=pltpu.SMEM)
@@ -61,7 +64,7 @@
         word = word | (jnp.int32(1) << shift)
         low = jnp.where(first, word, low)
         high = jnp.where(first, high, word)
-        peer = ((t >> 4) << 3) | (t & 7)
+        peer = (((t >> 4) << 3) | (t & 7)) ^ (PEERS - 1)
         which = ((t >> 3) & 1) ^ half
         slot = peer * 4 + which * 2 + rank
         pooled = pool_ref[jnp.minimum(m, POOL - 1)]
@@ -130,7 +133,8 @@
         if section == "pool":
             page = place
         else:
-            page = POOL + (place // 16) * 32 + half * 16 + place % 16
+            from_end = place ^ (2 * PEERS - 2)
+            page = POOL + (from_end // 16) * 32 + half * 16 + from_end % 16
         hits = [jnp.where((info[g : g + 1, :] == page) & inside[g], 1.0, 0.0).astype(BF16) for g in range(REQS)]
         count = dot(jnp.concatenate(hits, 1), weights, 1, 0)
         log = jnp.log2(jnp.maximum(count, 1.0)) / SCALE
@@ -325,7 +329,7 @@
     output_scaling_weights,
 ):
     ways = lax.axis_size("tp")
-    half = lax.axis_index("zh").astype(I32).reshape(1)
+    half = ((lax.axis_index("rep") >> 3) & 1).astype(I32).reshape(1)
     pool = cache_block_store.reshape(POOL, 2 * PAGE, HD)
     unfinished = unfinished_block_memory.reshape(REQS, 2 * PAGE, HD)
     fresh = fresh_token_memory.reshape(STEPS, REQS, 2, HD)
@@ -335,27 +339,25 @@
     outgoing = send_tiles(
         half, migration_receiver_server.reshape(MIGS), migration_sender_block, fill, switch, pool, unfinished, fresh
     )
-    tiles = lax.all_to_all(outgoing, ("y", "zl", "x"), split_axis=0, concat_axis=0, tiled=True)
+    tiles = lax.all_to_all(outgoing, "rep", split_axis=0, concat_axis=0, axis_index_groups=HALVES, tiled=True)
     tiles = tiles.reshape(PEERS, 4, 2 * PAGE, HD)
 
     query = jnp.transpose(lookup_vectors, (2, 0, 1, 3)).reshape(ROWS, HD)
     request = request_rows(sequence_history_count, switch, query, sequence_block_index)
-    asked = lax.ppermute(request, "zh", [(0, 1), (1, 0)])
+    asked = lax.ppermute(request, "rep", PARTNERS)
     pool_bias, near_bias = token_bias(("pool", "arrived"), half, request)
     mixed, log = local_part(fill, request, pool, unfinished, fresh, pool_bias)
     (far_bias,) = token_bias(("arrived",), half, asked)
 
-    back = lax.ppermute(far_part(asked, far_bias, tiles, log), "zh", [(0, 1), (1, 0)])
+    back = lax.ppermute(far_part(asked, far_bias, tiles, log), "rep", PARTNERS)
     mixed, log = near_part(request, near_bias, tiles, mixed, log)
     attn, square = merge(mixed, log, back, ways)
-    square = lax.all_to_all(square, "tp", split_axis=0, concat_axis=0, tiled=True)
+    square = lax.all_to_all(square, "tp", split_axis=0, concat_axis=0, axis_index_groups=SUMMED, tiled=True)
     return normalize(attn, square, gain)
 
 
 def solution(mesh):
-    devices = mesh.devices.reshape(4, 2, 2, 4, mesh.devices.shape[1])
-    fine = jax.sharding.Mesh(devices, ("y", "zh", "zl", "x", "tp"))
-    rep = ("y", "zh", "zl", "x")
+    rep = "rep"
     placed = (
         P(None, rep, "tp", None),
         P(None, rep, None, "tp", None),
@@ -369,4 +371,4 @@
         P(rep),
         P("tp"),
     )
-    return jax.shard_map(body, mesh=fine, in_specs=placed, out_specs=P(None, rep, "tp"), check_vma=False)
+    return jax.shard_map(body, mesh=mesh, in_specs=placed, out_specs=P(None, rep, "tp"), check_vma=False)

time: 66.6 us -> 58.3 us (0.88)
  blocking collectives: 29.5 us -> 21.8 us
  waiting for transfers between devices: 6.89 us -> 0.76 us
  starting transfers between devices: 18.3 us -> 23.7 us
    all_to_all x1, blocking collectives: 29.5 us -> 21.8 us  [body(): lax.all_to_all(square, 'tp', split_axis=0, concat_axis=0, axis_index_grou...]
    all_to_all x1, waiting for transfers between devices: 4.22 us -> 0.01 us  [body(): lax.all_to_all(outgoing, 'rep', split_axis=0, concat_axis=0, axis_index_g...]
    ppermute x2, starting transfers between devices: 8.95 us -> 12.7 us  [the longest x1 7.79 us: body(): back = lax.ppermute(far_part(asked, far_bias, tiles, log), 'rep', PARTNERS)]
    ppermute x2, waiting for transfers between devices: 2.66 us -> 0.75 us  [the longest x1 0.75 us: body(): back = lax.ppermute(far_part(asked, far_bias, tiles, log), 'rep', PARTNERS)]
    all_to_all x1, starting transfers between devices: 9.35 us -> 11 us  [body(): lax.all_to_all(outgoing, 'rep', split_axis=0, concat_axis=0, axis_index_g...]
  transfers between devices with their start and end apart: 3 -> 3, of which waited for: 3 -> 1; matrix products, arithmetic and copies ran while one was open for 1% -> 1% of each run, Pallas kernels for 9% -> 10%
where the time goes in v3:
time: 58.3 us; the launch traced here: 57.9 us
  starting transfers between devices  23.7 us (41%)
  blocking collectives  21.8 us (37%)
  Pallas kernels  10.9 us (19%)
  waiting for transfers between devices  0.76 us (1%)
  local copies, waits for them, and re-layouts  0.66 us (1%)
    all_to_all x1, blocking collectives, body(): lax.all_to_all(square, 'tp', split_axis=0, concat_axis=0, axis_index_grou...  21.8 us
    all_to_all x1, starting transfers between devices, body(): lax.all_to_all(outgoing, 'rep', split_axis=0, concat_axis=0, axis_index_g...  11 us
    ppermute x1, starting transfers between devices, body(): back = lax.ppermute(far_part(asked, far_bias, tiles, log), 'rep', PARTNERS)  7.79 us
    ppermute x1, starting transfers between devices, body(): asked = lax.ppermute(request, 'rep', PARTNERS)  4.9 us
    pallas_call x1, Pallas kernels, send_tiles(): pl.pallas_call(send_kernel, out_shape=pltpu.VMEM((PEERS * 4, 2 * PAGE, HD...  2.9 us
    pallas_call x1, Pallas kernels, local_part(): pl.pallas_call(local_kernel, out_shape=(out, out), in_specs=[SMEM] + [VME...  2.08 us
    pallas_call x2, Pallas kernels, token_bias(): pl.pallas_call(lambda *refs: bias_kernel(sections, *refs), out_shape=(out...  2.05 us
  transfers between devices with their start and end apart: 3, of which 1 were waited for; matrix products, arithmetic and copies ran while one was open for 1% of the time, Pallas kernels for 10%

profile of v3, /device:TPU:1, one launch (start us, length us, event | category | flops | bytes accessed | tf_op | source)
XLA Modules:
  0.0 57.9 jit_solution(18282575875800483610)
XLA Ops:
  0.0 2.9 %send_tiles.1 = bf16[128,32,128]{2,1,0:T(8,128)(2,1)} custom-call(s32[1]{0:T(128)} %bitcast.2.refs_0_.half_ref, s32[64]{0:T(128)} %bitcast.20, s32[64]{0:T(128)} %source_ref.1, s32[4]{0:T(128)} %fill_ref.3, s32[4]{0:T(128)} %switch_ref.3, bf16[64,32,128]{2,1,0:T(8,128)(2,1)} %bitcast.12, bf16[4,32,128]{2,1,0:T(8,128)(2,1)} %bitcast.16, ...), custom_call_target="tpu_custom_call" | custom-call | flops 1000 | bytes 2097152 | tf_op jit(solution)/shard_map/send_tiles/pallas_call | solution.py:80
  2.9 0.0 copy-start.1
  2.9 11.0 %all-to-all-start = ((bf16[128,32,128]{2,1,0:T(8,128)(2,1)}), bf16[128,32,128]{2,1,0:T(8,128)(2,1)S(1)}, u32[]{:S(2)}, u32[]{:S(2)}) async-start(bf16[128,32,128]{2,1,0:T(8,128)(2,1)} %send_tiles.1), calls=%async_computation | async-start | bytes 2097152 | tf_op jit(solution)/shard_map/all_to_all | solution.py:342
  13.9 0.0 copy-done.1
  13.9 0.7 %copy.12 = bf16[16,4,4,128]{3,2,1,0:T(4,128)(2,1)} copy(bf16[16,4,4,128]{3,0,2,1:T(8,128)(2,1)S(1)} %bitcast.15) | data formatting | bytes 131072 | tf_op jit(solution)/shard_map/transpose | solution.py:345
  14.6 0.9 %request_rows.1.refs_1_.request_ref = bf16[272,128]{1,0:T(8,128)(2,1)S(1)} custom-call(s32[4]{0:T(128)} %length_ref.1, s32[4]{0:T(128)} %switch_ref.3, bf16[256,128]{1,0:T(8,128)(2,1)} %bitcast.14, s32[4,128]{1,0:T(4,128)} %table_ref.1), custom_call_target="tpu_custom_call" | custom-call | flops 1000 | bytes 131072 | tf_op jit(solution)/shard_map/request_rows/pallas_call | solution.py:104
  15.5 4.9 %collective-permute-start = (bf16[272,128]{1,0:T(8,128)(2,1)S(1)}, bf16[272,128]{1,0:T(8,128)(2,1)S(1)}, u32[]{:S(2)}, u32[]{:S(2)}) collective-permute-start(bf16[272,128]{1,0:T(8,128)(2,1)S(1)} %request_rows.1.refs_1_.request_ref), channel_id=1, source_target_pairs={{0,64},{8,72},{16,80},{24,88},{32,96},{40,104},{48,112},{56,120},{... | collective-permute-start | bytes 208904 | tf_op jit(solution)/shard_map/ppermute | solution.py:347
  20.4 1.2 %token_bias.2 = (bf16[1024,128]{1,0:T(8,128)(2,1)S(1)}, bf16[1024,128]{1,0:T(8,128)(2,1)S(1)}) custom-call(s32[1]{0:T(128)} %bitcast.2.refs_0_.half_ref, bf16[272,128]{1,0:T(8,128)(2,1)S(1)} %request_rows.1.refs_1_.request_ref), custom_call_target="tpu_custom_call" | custom-call | flops 134217728 | bytes 262144 | tf_op jit(solution)/shard_map/token_bias/pallas_call | solution.py:152
  21.6 2.1 %local_part.1 = (f32[256,128]{1,0:T(8,128)S(1)}, f32[256,128]{1,0:T(8,128)S(1)}) custom-call(s32[4]{0:T(128)} %fill_ref.3, bf16[272,128]{1,0:T(8,128)(2,1)S(1)} %request_rows.1.refs_1_.request_ref, bf16[64,32,128]{2,1,0:T(8,128)(2,1)} %bitcast.13, bf16[4,32,128]{2,1,0:T(8,128)(2,1)} %bitcast.17, bf16[4,4,2,128]{3,2,1,0:T(2,128)(2,1)} %bitcast.19, ...), custom_call_target="tpu_custom_call" | custom-call | flops 268435456 | bytes 1048576 | tf_op jit(solution)/shard_map/local_part/pallas_call | solution.py:205
  23.7 0.0 collective-permute-done.refs_1_.request_ref
  23.7 0.9 %token_bias.3.bias_ref = bf16[1024,128]{1,0:T(8,128)(2,1)S(1)} custom-call(s32[1]{0:T(128)} %bitcast.2.refs_0_.half_ref, bf16[272,128]{1,0:T(8,128)(2,1)S(1)} %collective-permute-done.refs_1_.request_ref), custom_call_target="tpu_custom_call" | custom-call | flops 134217728 | bytes 262144 | tf_op jit(solution)/shard_map/token_bias/pallas_call | solution.py:152
  24.5 0.0 all-to-all-done
  24.6 1.0 %far_part.1 = bf16[272,128]{1,0:T(8,128)(2,1)S(1)} custom-call(bf16[272,128]{1,0:T(8,128)(2,1)S(1)} %collective-permute-done.refs_1_.request_ref, bf16[1024,128]{1,0:T(8,128)(2,1)S(1)} %token_bias.3.bias_ref, bf16[32,4,32,128]{3,2,1,0:T(8,128)(2,1)S(1)} %bitcast.9, f32[256,128]{1,0:T(8,128)S(1)} %get-tuple-element.16.log_ref.after_ref), custom_call_target="tpu_custom_call" | custom-call | flops 268435456 | bytes 1048576 | tf_op jit(solution)/shard_map/far_part/pallas_call | solution.py:237
  25.6 7.8 %collective-permute-start.1 = (bf16[272,128]{1,0:T(8,128)(2,1)S(1)}, bf16[272,128]{1,0:T(8,128)(2,1)S(1)}, u32[]{:S(2)}, u32[]{:S(2)}) collective-permute-start(bf16[272,128]{1,0:T(8,128)(2,1)S(1)} %far_part.1), channel_id=1, source_target_pairs={{0,64},{8,72},{16,80},{24,88},{32,96},{40,104},{48,112},{56,120},{... | collective-permute-start | bytes 208904 | tf_op jit(solution)/shard_map/ppermute | solution.py:352
  33.3 0.9 %near_part.1 = (f32[256,128]{1,0:T(8,128)S(1)}, f32[256,128]{1,0:T(8,128)S(1)}) custom-call(bf16[272,128]{1,0:T(8,128)(2,1)S(1)} %request_rows.1.refs_1_.request_ref, bf16[1024,128]{1,0:T(8,128)(2,1)S(1)} %get-tuple-element.13.bias_ref, bf16[32,4,32,128]{3,2,1,0:T(8,128)(2,1)S(1)} %bitcast.10, f32[256,128]{1,0:T(8,128)S(1)} %get-tuple-element.15.mixed_ref, ...), custom_call_target="tpu_custom_call" | custom-call | flops 268435456 | bytes 1048576 | tf_op jit(solution)/shard_map/near_part/pallas_call | solution.py:256
  34.3 0.8 %collective-permute-done.1.back_ref = bf16[272,128]{1,0:T(8,128)(2,1)S(1)} collective-permute-done((bf16[272,128]{1,0:T(8,128)(2,1)S(1)}, bf16[272,128]{1,0:T(8,128)(2,1)S(1)}, u32[]{:S(2)}, u32[]{:S(2)}) %collective-permute-start.1) | collective-permute-done | bytes 69664 | tf_op jit(solution)/shard_map/ppermute | solution.py:352
  35.0 0.3 merge.1
  35.4 0.0 copy-start
  35.4 21.8 %all_to_all.10.square_ref = f32[8,1,128]{2,1,0:T(1,128)S(1)} all-to-all(f32[8,1,128]{2,1,0:T(1,128)S(1)} %get-tuple-element.20), channel_id=1, replica_groups={{4,5,2,3,6,7,0,1},{12,13,10,11,14,15,8,9},{20,21,18,19,22,23,16,17},{28..., dimensions={0} | all-to-all | bytes 8192 | tf_op jit(solution)/shard_map/all_to_all | solution.py:355
  57.1 0.0 copy-done
  57.1 0.7 %normalize.1 = bf16[4,4,2048]{2,1,0:T(4,128)(2,1)} custom-call(bf16[256,128]{1,0:T(8,128)(2,1)S(1)} %get-tuple-element.19.attn_ref, f32[8,1,128]{2,1,0:T(1,128)S(1)} %all_to_all.10.square_ref, f32[16,128]{1,0:T(8,128)S(1)} %bitcast.11), custom_call_target="tpu_custom_call" | custom-call | tf_op jit(solution)/shard_map/normalize/pallas_call | solution.py:309
Async XLA Ops:
  2.9 11.0 %copy-start.1 = (bf16[4,4,16,128]{3,2,1,0:T(8,128)(2,1)S(1)}, bf16[4,4,16,128]{3,2,1,0:T(8,128)(2,1)}, u32[]{:S(2)}) copy-start(bf16[4,4,16,128]{3,2,1,0:T(8,128)(2,1)} %param.11) | copy-start | bytes 196612
  2.9 21.6 %all-to-all-start = ((bf16[128,32,128]{2,1,0:T(8,128)(2,1)}), bf16[128,32,128]{2,1,0:T(8,128)(2,1)S(1)}, u32[]{:S(2)}, u32[]{:S(2)}) async-start(bf16[128,32,128]{2,1,0:T(8,128)(2,1)} %send_tiles.1), calls=%async_computation | async-start | bytes 2097152 | tf_op jit(solution)/shard_map/all_to_all | solution.py:342
  15.5 8.2 %collective-permute-start = (bf16[272,128]{1,0:T(8,128)(2,1)S(1)}, bf16[272,128]{1,0:T(8,128)(2,1)S(1)}, u32[]{:S(2)}, u32[]{:S(2)}) collective-permute-start(bf16[272,128]{1,0:T(8,128)(2,1)S(1)} %request_rows.1.refs_1_.request_ref), channel_id=1, source_target_pairs={{0,64},{8,72},{16,80},{24,88},{32,96},{40,104},{48,112},{56,120},{... | collective-permute-start | bytes 208904 | tf_op jit(solution)/shard_map/ppermute | solution.py:347
  25.6 9.5 %collective-permute-start.1 = (bf16[272,128]{1,0:T(8,128)(2,1)S(1)}, bf16[272,128]{1,0:T(8,128)(2,1)S(1)}, u32[]{:S(2)}, u32[]{:S(2)}) collective-permute-start(bf16[272,128]{1,0:T(8,128)(2,1)S(1)} %far_part.1), channel_id=1, source_target_pairs={{0,64},{8,72},{16,80},{24,88},{32,96},{40,104},{48,112},{56,120},{... | collective-permute-start | bytes 208904 | tf_op jit(solution)/shard_map/ppermute | solution.py:352
  35.4 21.8 %copy-start = (f32[2048]{0:T(1024)S(1)}, f32[2048]{0:T(1024)}, u32[]{:S(2)}) copy-start(f32[2048]{0:T(1024)} %param.21) | copy-start | bytes 24580

commit v4 on v3

--- a/solution.py
+++ b/solution.py
@@ -16,7 +16,10 @@
 NEG = -1e30
 MARK = 4096.0
 SCALE = 1.4426950408889634 / HD**0.5
-HALVES = [[p for p in reversed(range(64)) if (p >> 3) & 1 == half] for half in range(2)]
+FIRST = 27
+ORDER = [k ^ FIRST for k in range(PEERS)]
+HALVES = [[((j >> 3) << 4) | (half << 3) | (j & 7) for j in ORDER] for half in range(2)]
+STANDS = [ORDER.index(((t >> 4) << 3) | (t & 7)) * 4 + ((t >> 3) & 1) * 2 for t in range(64)]
 PARTNERS = [(p, p ^ 8) for p in range(64)]
 SUMMED = [[4, 5, 2, 3, 6, 7, 0, 1]]
 F32, BF16, I32 = jnp.float32, jnp.bfloat16, jnp.int32
@@ -41,7 +44,10 @@
     return tile
 
 
-def send_kernel(half_ref, target_ref, source_ref, fill_ref, switch_ref, pool_ref, unfinished_ref, fresh_ref, out_ref, cut_ref):
+def send_kernel(
+    half_ref, target_ref, source_ref, stand_ref, length_ref, fill_ref, switch_ref,
+    pool_ref, unfinished_ref, fresh_ref, query_ref, table_ref, out_ref, request_ref, cut_ref
+):
     rows = iota((PAGE, HD), 0)
     blank = jnp.concatenate([jnp.full((PAGE, HD), MARK, BF16), jnp.zeros((PAGE, HD), BF16)], 0)
     out_ref[...] = jnp.broadcast_to(blank[None], out_ref.shape)
@@ -51,7 +57,7 @@
         value = tail_tile(r, 1, fill, unfinished_ref, fresh_ref)
         key = jnp.where(rows < fill + switch_ref[r], key, MARK)
         cut_ref[r] = jnp.concatenate([key, value], 0).astype(BF16)
-    half = half_ref[0]
+    flip = half_ref[0] * 2
     low = jnp.int32(0)
     high = jnp.int32(0)
     for e in range(MIGS):
@@ -64,32 +70,11 @@
         word = word | (jnp.int32(1) << shift)
         low = jnp.where(first, word, low)
         high = jnp.where(first, high, word)
-        peer = (((t >> 4) << 3) | (t & 7)) ^ (PEERS - 1)
-        which = ((t >> 3) & 1) ^ half
-        slot = peer * 4 + which * 2 + rank
         pooled = pool_ref[jnp.minimum(m, POOL - 1)]
         cut = cut_ref[jnp.maximum(m - POOL, 0)]
-        out_ref[slot] = jnp.where(m < POOL, pooled, cut)
-
-
-def keep(*arrays):
-    return tuple(pltpu.with_memory_space_constraint(x, pltpu.VMEM) for x in arrays)
-
-
-def send_tiles(half, target, source, fill, switch, pool, unfinished, fresh):
-    return pl.pallas_call(
-        send_kernel,
-        out_shape=pltpu.VMEM((PEERS * 4, 2 * PAGE, HD), BF16),
-        in_specs=[SMEM] * 5 + [VMEM] * 3,
-        out_specs=VMEM,
-        scratch_shapes=[pltpu.VMEM((REQS, 2 * PAGE, HD), BF16)],
-        cost_estimate=pl.CostEstimate(flops=1000, bytes_accessed=2**21, transcendentals=0),
-        name="send_tiles",
-    )(half, target, source, fill, switch, pool, unfinished, fresh)
-
-
-def request_kernel(length_ref, switch_ref, query_ref, table_ref, out_ref):
-    out_ref[:ROWS, :] = query_ref[...]
+        out_ref[(stand_ref[t] ^ flip) + rank] = jnp.where(m < POOL, pooled, cut)
+    query = jnp.transpose(query_ref[...].astype(F32), (1, 0, 2))
+    request_ref[:ROWS, :] = query.reshape(ROWS, HD).astype(BF16)
     row, lane = iota((16, HD), 0), iota((16, HD), 1)
     info = jnp.concatenate([table_ref[...], jnp.zeros((16 - REQS, HD), I32)], 0)
     for g in range(REQS):
@@ -97,18 +82,23 @@
         at = row - REQS
         fact = jnp.where(at == 0, length >> 4, jnp.where(at == 1, length & 15, switch_ref[g]))
         info = jnp.where((lane == g) & (at >= 0) & (at < 3), fact, info)
-    out_ref[ROWS:, :] = info.astype(F32).astype(BF16)
-
-
-def request_rows(length, switch, query, table):
-    return pl.pallas_call(
-        request_kernel,
-        out_shape=pltpu.VMEM((ROWS + 16, HD), BF16),
-        in_specs=[SMEM] * 2 + [VMEM] * 2,
-        out_specs=VMEM,
-        cost_estimate=pl.CostEstimate(flops=1000, bytes_accessed=2**17, transcendentals=0),
-        name="request_rows",
-    )(length, switch, query, table)
+    request_ref[ROWS:, :] = info.astype(F32).astype(BF16)
+
+
+def keep(*arrays):
+    return tuple(pltpu.with_memory_space_constraint(x, pltpu.VMEM) for x in arrays)
+
+
+def send_tiles(half, target, source, length, fill, switch, pool, unfinished, fresh, query, table):
+    return pl.pallas_call(
+        send_kernel,
+        out_shape=(pltpu.VMEM((PEERS * 4, 2 * PAGE, HD), BF16), pltpu.VMEM((ROWS + 16, HD), BF16)),
+        in_specs=[SMEM] * 7 + [VMEM] * 5,
+        out_specs=(VMEM, VMEM),
+        scratch_shapes=[pltpu.VMEM((REQS, 2 * PAGE, HD), BF16)],
+        cost_estimate=pl.CostEstimate(flops=1000, bytes_accessed=2**21, transcendentals=0),
+        name="send_tiles",
+    )(half, target, source, jnp.array(STANDS, I32), length, fill, switch, pool, unfinished, fresh, query, table)
 
 
 def bias_kernel(sections, half_ref, request_ref, *refs):
@@ -130,12 +120,14 @@
         weights.append(((spread % REQS == g) & (spread < 3 * PAIRS)).astype(BF16))
     weights = jnp.concatenate(weights, 0)
     for section, ref in zip(sections, refs, strict=True):
-        if section == "pool":
-            page = place
-        else:
-            from_end = place ^ (2 * PEERS - 2)
-            page = POOL + (from_end // 16) * 32 + half * 16 + from_end % 16
-        hits = [jnp.where((info[g : g + 1, :] == page) & inside[g], 1.0, 0.0).astype(BF16) for g in range(REQS)]
+        spot = info[:REQS]
+        if section != "pool":
+            slot = spot - POOL
+            peer = slot >> 1
+            here = (slot >= 0) & (((peer >> 3) & 1) == half)
+            peer = (((peer >> 4) << 3) | (peer & 7)) ^ FIRST
+            spot = jnp.where(here, peer * 2 + (slot & 1), -1)
+        hits = [jnp.where((spot[g : g + 1, :] == place) & inside[g], 1.0, 0.0).astype(BF16) for g in range(REQS)]
         count = dot(jnp.concatenate(hits, 1), weights, 1, 0)
         log = jnp.log2(jnp.maximum(count, 1.0)) / SCALE
         high = log.astype(BF16).astype(F32)
@@ -336,14 +328,14 @@
     gain = output_scaling_weights.reshape(HEADS, HD)
     fill, switch = unfinished_block_fill, switch_moment
 
-    outgoing = send_tiles(
-        half, migration_receiver_server.reshape(MIGS), migration_sender_block, fill, switch, pool, unfinished, fresh
+    query = lookup_vectors.reshape(PAIRS, HEADS, HD)
+    outgoing, request = send_tiles(
+        half, migration_receiver_server.reshape(MIGS), migration_sender_block, sequence_history_count, fill, switch,
+        pool, unfinished, fresh, query, sequence_block_index
     )
     tiles = lax.all_to_all(outgoing, "rep", split_axis=0, concat_axis=0, axis_index_groups=HALVES, tiled=True)
     tiles = tiles.reshape(PEERS, 4, 2 * PAGE, HD)
 
-    query = jnp.transpose(lookup_vectors, (2, 0, 1, 3)).reshape(ROWS, HD)
-    request = request_rows(sequence_history_count, switch, query, sequence_block_index)
     asked = lax.ppermute(request, "rep", PARTNERS)
     pool_bias, near_bias = token_bias(("pool", "arrived"), half, request)
     mixed, log = local_part(fill, request, pool, unfinished, fresh, pool_bias)

time: 58.3 us -> 56.8 us (0.974)
  waiting for transfers between devices: 0.76 us -> 3.43 us
  starting transfers between devices: 23.7 us -> 21.3 us
  Pallas kernels: 10.9 us -> 9.64 us
  local copies, waits for them, and re-layouts: 0.66 us -> 0.01 us
    ppermute x1, starting transfers between devices: 7.79 us -> 6.03 us  [body(): back = lax.ppermute(far_part(asked, far_bias, tiles, log), 'rep', PARTNERS)]
    ppermute x1, waiting for transfers between devices: 0.01 us -> 1.65 us  [body(): asked = lax.ppermute(request, 'rep', PARTNERS)]
    all_to_all x1, waiting for transfers between devices: 0.01 us -> 1.03 us  [body(): lax.all_to_all(outgoing, 'rep', split_axis=0, concat_axis=0, axis_index_g...]
    pallas_call x2 -> x1, Pallas kernels: 3.77 us -> 2.75 us  [send_tiles(): pl.pallas_call(send_kernel, out_shape=(pltpu.VMEM((PEERS * 4, 2 * PAGE, H...]
    transpose x1 -> x0, local copies, waits for them, and re-layouts: 0.66 us -> none  [body(): query = jnp.transpose(lookup_vectors, (2, 0, 1, 3)).reshape(ROWS, HD)]
    all_to_all x1, starting transfers between devices: 11 us -> 10.4 us  [body(): lax.all_to_all(outgoing, 'rep', split_axis=0, concat_axis=0, axis_index_g...]
  transfers between devices with their start and end apart: 3 -> 3, of which waited for: 1 -> 3; matrix products, arithmetic and copies ran while one was open for 1% -> 0% of each run, Pallas kernels for 10% -> 9%
where the time goes in v4:
time: 56.8 us; the launch traced here: 56.4 us
  blocking collectives  22 us (39%)
  starting transfers between devices  21.3 us (38%)
  Pallas kernels  9.64 us (17%)
  waiting for transfers between devices  3.43 us (6%)
    all_to_all x1, blocking collectives, body(): lax.all_to_all(square, 'tp', split_axis=0, concat_axis=0, axis_index_grou...  22 us
    all_to_all x1, starting transfers between devices, body(): lax.all_to_all(outgoing, 'rep', split_axis=0, concat_axis=0, axis_index_g...  10.4 us
    ppermute x1, starting transfers between devices, body(): back = lax.ppermute(far_part(asked, far_bias, tiles, log), 'rep', PARTNERS)  6.03 us
    ppermute x1, starting transfers between devices, body(): asked = lax.ppermute(request, 'rep', PARTNERS)  4.9 us
    pallas_call x1, Pallas kernels, send_tiles(): pl.pallas_call(send_kernel, out_shape=(pltpu.VMEM((PEERS * 4, 2 * PAGE, H...  2.75 us
    pallas_call x1, Pallas kernels, local_part(): pl.pallas_call(local_kernel, out_shape=(out, out), in_specs=[SMEM] + [VME...  2.09 us
    pallas_call x2, Pallas kernels, token_bias(): pl.pallas_call(lambda *refs: bias_kernel(sections, *refs), out_shape=(out...  1.81 us
    ppermute x1, waiting for transfers between devices, body(): asked = lax.ppermute(request, 'rep', PARTNERS)  1.65 us
  transfers between devices with their start and end apart: 3, of which 3 were waited for; matrix products, arithmetic and copies ran while one was open for 0% of the time, Pallas kernels for 9%

profile of v4, /device:TPU:1, one launch (start us, length us, event | category | flops | bytes accessed | tf_op | source)
XLA Modules:
  0.0 56.4 jit_solution(14070440238492445264)
XLA Ops:
  0.0 2.7 %send_tiles.1 = (bf16[128,32,128]{2,1,0:T(8,128)(2,1)}, bf16[272,128]{1,0:T(8,128)(2,1)S(1)}) custom-call(s32[1]{0:T(128)} %bitcast.half_ref.refs_0_, s32[64]{0:T(128)} %bitcast.18, s32[64]{0:T(128)} %source_ref.1, s32[64]{0:T(128)} %constant.12.clone.stand_ref, s32[4]{0:T(128)} %length_ref.1, s32[4]{0:T(128)} %fill_ref.3, s32[4]{0:T(128)} %switch_ref.1, ...), custom_call_target="tpu_custom_call" | custom-call | flops 1000 | bytes 2097152 | tf_op jit(solution)/shard_map/send_tiles/pallas_call | solution.py:93
  2.7 10.4 %all-to-all-start = ((bf16[128,32,128]{2,1,0:T(8,128)(2,1)}), bf16[128,32,128]{2,1,0:T(8,128)(2,1)S(1)}, u32[]{:S(2)}, u32[]{:S(2)}) async-start(bf16[128,32,128]{2,1,0:T(8,128)(2,1)} %get-tuple-element.17), calls=%async_computation | async-start | bytes 2097152 | tf_op jit(solution)/shard_map/all_to_all | solution.py:336
  13.2 4.9 %collective-permute-start = (bf16[272,128]{1,0:T(8,128)(2,1)S(1)}, bf16[272,128]{1,0:T(8,128)(2,1)S(1)}, u32[]{:S(2)}, u32[]{:S(2)}) collective-permute-start(bf16[272,128]{1,0:T(8,128)(2,1)S(1)} %get-tuple-element.15.refs_1_.request_ref), channel_id=1, source_target_pairs={{0,64},{8,72},{16,80},{24,88},{32,96},{40,104},{48,112},{56,120},{... | collective-permute-start | bytes 208904 | tf_op jit(solution)/shard_map/ppermute | solution.py:339
  18.1 1.1 %token_bias.2 = (bf16[1024,128]{1,0:T(8,128)(2,1)S(1)}, bf16[1024,128]{1,0:T(8,128)(2,1)S(1)}) custom-call(s32[1]{0:T(128)} %bitcast.half_ref.refs_0_, bf16[272,128]{1,0:T(8,128)(2,1)S(1)} %get-tuple-element.15.refs_1_.request_ref), custom_call_target="tpu_custom_call" | custom-call | flops 134217728 | bytes 262144 | tf_op jit(solution)/shard_map/token_bias/pallas_call | solution.py:144
  19.2 2.1 %local_part.1 = (f32[256,128]{1,0:T(8,128)S(1)}, f32[256,128]{1,0:T(8,128)S(1)}) custom-call(s32[4]{0:T(128)} %fill_ref.3, bf16[272,128]{1,0:T(8,128)(2,1)S(1)} %get-tuple-element.15.refs_1_.request_ref, bf16[64,32,128]{2,1,0:T(8,128)(2,1)} %bitcast.12, bf16[4,32,128]{2,1,0:T(8,128)(2,1)} %bitcast.15, bf16[4,4,2,128]{3,2,1,0:T(2,128)(2,1)} %bitcast.17, ...), custom_call_target="tpu_custom_call" | custom-call | flops 268435456 | bytes 1048576 | tf_op jit(solution)/shard_map/local_part/pallas_call | solution.py:197
  21.3 1.7 %collective-permute-done.refs_1_.request_ref = bf16[272,128]{1,0:T(8,128)(2,1)S(1)} collective-permute-done((bf16[272,128]{1,0:T(8,128)(2,1)S(1)}, bf16[272,128]{1,0:T(8,128)(2,1)S(1)}, u32[]{:S(2)}, u32[]{:S(2)}) %collective-permute-start) | collective-permute-done | bytes 69664 | tf_op jit(solution)/shard_map/ppermute | solution.py:339
  22.9 0.7 %token_bias.3.bias_ref = bf16[1024,128]{1,0:T(8,128)(2,1)S(1)} custom-call(s32[1]{0:T(128)} %bitcast.half_ref.refs_0_, bf16[272,128]{1,0:T(8,128)(2,1)S(1)} %collective-permute-done.refs_1_.request_ref), custom_call_target="tpu_custom_call" | custom-call | flops 134217728 | bytes 262144 | tf_op jit(solution)/shard_map/token_bias/pallas_call | solution.py:144
  23.6 1.0 %all-to-all-done = bf16[128,32,128]{2,1,0:T(8,128)(2,1)S(1)} async-done(((bf16[128,32,128]{2,1,0:T(8,128)(2,1)}), bf16[128,32,128]{2,1,0:T(8,128)(2,1)S(1)}, u32[]{:S(2)}, u32[]{:S(2)}) %all-to-all-start) | async-done | bytes 1048608 | tf_op jit(solution)/shard_map/all_to_all | solution.py:336
  24.7 1.0 %far_part.1 = bf16[272,128]{1,0:T(8,128)(2,1)S(1)} custom-call(bf16[272,128]{1,0:T(8,128)(2,1)S(1)} %collective-permute-done.refs_1_.request_ref, bf16[1024,128]{1,0:T(8,128)(2,1)S(1)} %token_bias.3.bias_ref, bf16[32,4,32,128]{3,2,1,0:T(8,128)(2,1)S(1)} %bitcast.8, f32[256,128]{1,0:T(8,128)S(1)} %get-tuple-element.20.log_ref.after_ref), custom_call_target="tpu_custom_call" | custom-call | flops 268435456 | bytes 1048576 | tf_op jit(solution)/shard_map/far_part/pallas_call | solution.py:229
  25.7 6.0 %collective-permute-start.1 = (bf16[272,128]{1,0:T(8,128)(2,1)S(1)}, bf16[272,128]{1,0:T(8,128)(2,1)S(1)}, u32[]{:S(2)}, u32[]{:S(2)}) collective-permute-start(bf16[272,128]{1,0:T(8,128)(2,1)S(1)} %far_part.1), channel_id=1, source_target_pairs={{0,64},{8,72},{16,80},{24,88},{32,96},{40,104},{48,112},{56,120},{... | collective-permute-start | bytes 208904 | tf_op jit(solution)/shard_map/ppermute | solution.py:344
  31.7 0.9 %near_part.1 = (f32[256,128]{1,0:T(8,128)S(1)}, f32[256,128]{1,0:T(8,128)S(1)}) custom-call(bf16[272,128]{1,0:T(8,128)(2,1)S(1)} %get-tuple-element.15.refs_1_.request_ref, bf16[1024,128]{1,0:T(8,128)(2,1)S(1)} %get-tuple-element.16.bias_ref, bf16[32,4,32,128]{3,2,1,0:T(8,128)(2,1)S(1)} %bitcast.9, f32[256,128]{1,0:T(8,128)S(1)} %get-tuple-element.19.mixed_ref, ...), custom_call_target="tpu_custom_call" | custom-call | flops 268435456 | bytes 1048576 | tf_op jit(solution)/shard_map/near_part/pallas_call | solution.py:248
  32.6 0.8 %collective-permute-done.1.back_ref = bf16[272,128]{1,0:T(8,128)(2,1)S(1)} collective-permute-done((bf16[272,128]{1,0:T(8,128)(2,1)S(1)}, bf16[272,128]{1,0:T(8,128)(2,1)S(1)}, u32[]{:S(2)}, u32[]{:S(2)}) %collective-permute-start.1) | collective-permute-done | bytes 69664 | tf_op jit(solution)/shard_map/ppermute | solution.py:344
  33.4 0.3 merge.1
  33.7 0.0 copy-start
  33.7 22.0 %all_to_all.10.square_ref = f32[8,1,128]{2,1,0:T(1,128)S(1)} all-to-all(f32[8,1,128]{2,1,0:T(1,128)S(1)} %get-tuple-element.24), channel_id=1, replica_groups={{4,5,2,3,6,7,0,1},{12,13,10,11,14,15,8,9},{20,21,18,19,22,23,16,17},{28..., dimensions={0} | all-to-all | bytes 8192 | tf_op jit(solution)/shard_map/all_to_all | solution.py:347
  55.7 0.0 copy-done
  55.7 0.7 %normalize.1 = bf16[4,4,2048]{2,1,0:T(4,128)(2,1)} custom-call(bf16[256,128]{1,0:T(8,128)(2,1)S(1)} %get-tuple-element.23.attn_ref, f32[8,1,128]{2,1,0:T(1,128)S(1)} %all_to_all.10.square_ref, f32[16,128]{1,0:T(8,128)S(1)} %bitcast.10), custom_call_target="tpu_custom_call" | custom-call | tf_op jit(solution)/shard_map/normalize/pallas_call | solution.py:301
Async XLA Ops:
  2.7 21.9 %all-to-all-start = ((bf16[128,32,128]{2,1,0:T(8,128)(2,1)}), bf16[128,32,128]{2,1,0:T(8,128)(2,1)S(1)}, u32[]{:S(2)}, u32[]{:S(2)}) async-start(bf16[128,32,128]{2,1,0:T(8,128)(2,1)} %get-tuple-element.17), calls=%async_computation | async-start | bytes 2097152 | tf_op jit(solution)/shard_map/all_to_all | solution.py:336
  13.2 9.8 %collective-permute-start = (bf16[272,128]{1,0:T(8,128)(2,1)S(1)}, bf16[272,128]{1,0:T(8,128)(2,1)S(1)}, u32[]{:S(2)}, u32[]{:S(2)}) collective-permute-start(bf16[272,128]{1,0:T(8,128)(2,1)S(1)} %get-tuple-element.15.refs_1_.request_ref), channel_id=1, source_target_pairs={{0,64},{8,72},{16,80},{24,88},{32,96},{40,104},{48,112},{56,120},{... | collective-permute-start | bytes 208904 | tf_op jit(solution)/shard_map/ppermute | solution.py:339
  25.7 7.7 %collective-permute-start.1 = (bf16[272,128]{1,0:T(8,128)(2,1)S(1)}, bf16[272,128]{1,0:T(8,128)(2,1)S(1)}, u32[]{:S(2)}, u32[]{:S(2)}) collective-permute-start(bf16[272,128]{1,0:T(8,128)(2,1)S(1)} %far_part.1), channel_id=1, source_target_pairs={{0,64},{8,72},{16,80},{24,88},{32,96},{40,104},{48,112},{56,120},{... | collective-permute-start | bytes 208904 | tf_op jit(solution)/shard_map/ppermute | solution.py:344
  33.7 22.0 %copy-start = (f32[2048]{0:T(1024)S(1)}, f32[2048]{0:T(1024)}, u32[]{:S(2)}) copy-start(f32[2048]{0:T(1024)} %param.22) | copy-start | bytes 24580

commit v5 on v4

--- a/solution.py
+++ b/solution.py
@@ -16,10 +16,19 @@
 NEG = -1e30
 MARK = 4096.0
 SCALE = 1.4426950408889634 / HD**0.5
-FIRST = 27
-ORDER = [k ^ FIRST for k in range(PEERS)]
-HALVES = [[((j >> 3) << 4) | (half << 3) | (j & 7) for j in ORDER] for half in range(2)]
-STANDS = [ORDER.index(((t >> 4) << 3) | (t & 7)) * 4 + ((t >> 3) & 1) * 2 for t in range(64)]
+def place_of(member, core):
+    if core == 0:
+        return member ^ 27
+    place = member ^ 31
+    return ((place & 3) << 3) | (place & 4) | (place >> 3)
+
+
+PLACES = [[place_of(j, core) for j in range(PEERS)] for core in range(2)]
+ORDERS = [[places.index(k) for k in range(PEERS)] for places in PLACES]
+HALVES = [
+    [(((j >> 3) << 4) | (half << 3) | (j & 7)) * 8 + tp for j in ORDERS[tp % 2]] for half in range(2) for tp in range(8)
+]
+STANDS = [PLACES[c][((t >> 4) << 3) | (t & 7)] * 4 + ((t >> 3) & 1) * 2 for c in range(2) for t in range(64)]
 PARTNERS = [(p, p ^ 8) for p in range(64)]
 SUMMED = [[4, 5, 2, 3, 6, 7, 0, 1]]
 F32, BF16, I32 = jnp.float32, jnp.bfloat16, jnp.int32
@@ -45,24 +54,25 @@
 
 
 def send_kernel(
-    half_ref, target_ref, source_ref, stand_ref, length_ref, fill_ref, switch_ref,
-    pool_ref, unfinished_ref, fresh_ref, query_ref, table_ref, out_ref, request_ref, cut_ref
+    half_ref, core_ref, target_ref, source_ref, stand_ref, length_ref, fill_ref, switch_ref,
+    pool_ref, unfinished_ref, fresh_ref, query_ref, table_ref, out_ref, request_ref, tiles_ref
 ):
     rows = iota((PAGE, HD), 0)
     blank = jnp.concatenate([jnp.full((PAGE, HD), MARK, BF16), jnp.zeros((PAGE, HD), BF16)], 0)
     out_ref[...] = jnp.broadcast_to(blank[None], out_ref.shape)
+    tiles_ref[:POOL] = pool_ref[...]
     for r in range(REQS):
         fill = fill_ref[r]
         key = tail_tile(r, 0, fill, unfinished_ref, fresh_ref)
         value = tail_tile(r, 1, fill, unfinished_ref, fresh_ref)
         key = jnp.where(rows < fill + switch_ref[r], key, MARK)
-        cut_ref[r] = jnp.concatenate([key, value], 0).astype(BF16)
+        tiles_ref[POOL + r] = jnp.concatenate([key, value], 0).astype(BF16)
     flip = half_ref[0] * 2
+    table = core_ref[0] * 64
     low = jnp.int32(0)
     high = jnp.int32(0)
     for e in range(MIGS):
         t = target_ref[e]
-        m = source_ref[e]
         first = t < 32
         shift = t & 31
         word = jnp.where(first, low, high)
@@ -70,9 +80,7 @@
         word = word | (jnp.int32(1) << shift)
         low = jnp.where(first, word, low)
         high = jnp.where(first, high, word)
-        pooled = pool_ref[jnp.minimum(m, POOL - 1)]
-        cut = cut_ref[jnp.maximum(m - POOL, 0)]
-        out_ref[(stand_ref[t] ^ flip) + rank] = jnp.where(m < POOL, pooled, cut)
+        out_ref[(stand_ref[table + t] ^ flip) + rank] = tiles_ref[source_ref[e]]
     query = jnp.transpose(query_ref[...].astype(F32), (1, 0, 2))
     request_ref[:ROWS, :] = query.reshape(ROWS, HD).astype(BF16)
     row, lane = iota((16, HD), 0), iota((16, HD), 1)
@@ -89,19 +97,19 @@
     return tuple(pltpu.with_memory_space_constraint(x, pltpu.VMEM) for x in arrays)
 
 
-def send_tiles(half, target, source, length, fill, switch, pool, unfinished, fresh, query, table):
+def send_tiles(half, core, target, source, length, fill, switch, pool, unfinished, fresh, query, table):
     return pl.pallas_call(
         send_kernel,
         out_shape=(pltpu.VMEM((PEERS * 4, 2 * PAGE, HD), BF16), pltpu.VMEM((ROWS + 16, HD), BF16)),
-        in_specs=[SMEM] * 7 + [VMEM] * 5,
+        in_specs=[SMEM] * 8 + [VMEM] * 5,
         out_specs=(VMEM, VMEM),
-        scratch_shapes=[pltpu.VMEM((REQS, 2 * PAGE, HD), BF16)],
+        scratch_shapes=[pltpu.VMEM((POOL + REQS, 2 * PAGE, HD), BF16)],
         cost_estimate=pl.CostEstimate(flops=1000, bytes_accessed=2**21, transcendentals=0),
         name="send_tiles",
-    )(half, target, source, jnp.array(STANDS, I32), length, fill, switch, pool, unfinished, fresh, query, table)
-
-
-def bias_kernel(sections, half_ref, request_ref, *refs):
+    )(half, core, target, source, jnp.array(STANDS, I32), length, fill, switch, pool, unfinished, fresh, query, table)
+
+
+def bias_kernel(sections, half_ref, core_ref, request_ref, *refs):
     info = request_ref[ROWS:, :].astype(F32).astype(I32)
     half = half_ref[0]
     token = iota((TOKENS, HD), 0)
@@ -125,7 +133,8 @@
             slot = spot - POOL
             peer = slot >> 1
             here = (slot >= 0) & (((peer >> 3) & 1) == half)
-            peer = (((peer >> 4) << 3) | (peer & 7)) ^ FIRST
+            peer = ((peer >> 4) << 3) | (peer & 7)
+            peer = jnp.where(core_ref[0] == 1, place_of(peer, 1), place_of(peer, 0))
             spot = jnp.where(here, peer * 2 + (slot & 1), -1)
         hits = [jnp.where((spot[g : g + 1, :] == place) & inside[g], 1.0, 0.0).astype(BF16) for g in range(REQS)]
         count = dot(jnp.concatenate(hits, 1), weights, 1, 0)
@@ -139,16 +148,16 @@
         ref[...] = jnp.where(gone, jnp.where(part == 0, NEG, 0.0), parts).astype(BF16)
 
 
-def token_bias(sections, half, request):
+def token_bias(sections, half, core, request):
     out = pltpu.VMEM((TOKENS, HD), BF16)
     return pl.pallas_call(
         lambda *refs: bias_kernel(sections, *refs),
         out_shape=(out,) * len(sections),
-        in_specs=[SMEM, VMEM],
+        in_specs=[SMEM, SMEM, VMEM],
         out_specs=(VMEM,) * len(sections),
         cost_estimate=pl.CostEstimate(flops=2**27, bytes_accessed=2**18, transcendentals=0),
         name="token_bias",
-    )(half, *keep(request))
+    )(half, core, *keep(request))
 
 
 def attend(query, key, value, bias):
@@ -322,6 +331,7 @@
 ):
     ways = lax.axis_size("tp")
     half = ((lax.axis_index("rep") >> 3) & 1).astype(I32).reshape(1)
+    core = (lax.axis_index("tp") & 1).astype(I32).reshape(1)
     pool = cache_block_store.reshape(POOL, 2 * PAGE, HD)
     unfinished = unfinished_block_memory.reshape(REQS, 2 * PAGE, HD)
     fresh = fresh_token_memory.reshape(STEPS, REQS, 2, HD)
@@ -330,16 +340,16 @@
 
     query = lookup_vectors.reshape(PAIRS, HEADS, HD)
     outgoing, request = send_tiles(
-        half, migration_receiver_server.reshape(MIGS), migration_sender_block, sequence_history_count, fill, switch,
+        half, core, migration_receiver_server.reshape(MIGS), migration_sender_block, sequence_history_count, fill, switch,
         pool, unfinished, fresh, query, sequence_block_index
     )
-    tiles = lax.all_to_all(outgoing, "rep", split_axis=0, concat_axis=0, axis_index_groups=HALVES, tiled=True)
+    tiles = lax.all_to_all(outgoing, ("rep", "tp"), split_axis=0, concat_axis=0, axis_index_groups=HALVES, tiled=True)
     tiles = tiles.reshape(PEERS, 4, 2 * PAGE, HD)
 
     asked = lax.ppermute(request, "rep", PARTNERS)
-    pool_bias, near_bias = token_bias(("pool", "arrived"), half, request)
+    pool_bias, near_bias = token_bias(("pool", "arrived"), half, core, request)
     mixed, log = local_part(fill, request, pool, unfinished, fresh, pool_bias)
-    (far_bias,) = token_bias(("arrived",), half, asked)
+    (far_bias,) = token_bias(("arrived",), half, core, asked)
 
     back = lax.ppermute(far_part(asked, far_bias, tiles, log), "rep", PARTNERS)
     mixed, log = near_part(request, near_bias, tiles, mixed, log)

time: 56.8 us -> 56.3 us (level)
  starting transfers between devices: 21.3 us -> 22.3 us
  blocking collectives: 22 us -> 21.2 us
    all_to_all x1, waiting for transfers between devices: 1.03 us -> 0.01 us  [body(): lax.all_to_all(outgoing, ('rep', 'tp'), split_axis=0, concat_axis=0, axis...]
    all_to_all x1, blocking collectives: 22 us -> 21.2 us  [body(): lax.all_to_all(square, 'tp', split_axis=0, concat_axis=0, axis_index_grou...]
  transfers between devices with their start and end apart: 3 -> 3, of which waited for: 3 -> 2; matrix products, arithmetic and copies ran while one was open for 0% -> 0% of each run, Pallas kernels for 9% -> 9%
where the time goes in v5:
time: 56.3 us; the launch traced here: 56 us
  starting transfers between devices  22.3 us (40%)
  blocking collectives  21.2 us (38%)
  Pallas kernels  9.49 us (17%)
  waiting for transfers between devices  2.9 us (5%)
    all_to_all x1, blocking collectives, body(): lax.all_to_all(square, 'tp', split_axis=0, concat_axis=0, axis_index_grou...  21.2 us
    all_to_all x1, starting transfers between devices, body(): lax.all_to_all(outgoing, ('rep', 'tp'), split_axis=0, concat_axis=0, axis...  10.9 us
    ppermute x1, starting transfers between devices, body(): back = lax.ppermute(far_part(asked, far_bias, tiles, log), 'rep', PARTNERS)  6.54 us
    ppermute x1, starting transfers between devices, body(): asked = lax.ppermute(request, 'rep', PARTNERS)  4.9 us
    pallas_call x1, Pallas kernels, send_tiles(): pl.pallas_call(send_kernel, out_shape=(pltpu.VMEM((PEERS * 4, 2 * PAGE, H...  2.6 us
    ppermute x1, waiting for transfers between devices, body(): asked = lax.ppermute(request, 'rep', PARTNERS)  2.15 us
    pallas_call x1, Pallas kernels, local_part(): pl.pallas_call(local_kernel, out_shape=(out, out), in_specs=[SMEM] + [VME...  2.09 us
    pallas_call x2, Pallas kernels, token_bias(): pl.pallas_call(lambda *refs: bias_kernel(sections, *refs), out_shape=(out...  1.81 us
  transfers between devices with their start and end apart: 3, of which 2 were waited for; matrix products, arithmetic and copies ran while one was open for 0% of the time, Pallas kernels for 9%

profile of v5, /device:TPU:1, one launch (start us, length us, event | category | flops | bytes accessed | tf_op | source)
XLA Modules:
  0.0 56.0 jit_solution(1182228479587997288)
XLA Ops:
  0.0 2.6 %send_tiles.1 = (bf16[128,32,128]{2,1,0:T(8,128)(2,1)}, bf16[272,128]{1,0:T(8,128)(2,1)S(1)}) custom-call(s32[1]{0:T(128)} %bitcast.half_ref.refs_0_, s32[1]{0:T(128)} %bitcast.1.core_ref.refs_1_, s32[64]{0:T(128)} %bitcast.19, s32[64]{0:T(128)} %source_ref.1, s32[128]{0:T(128)} %constant.15.clone.stand_ref, s32[4]{0:T(128)} %length_ref.1, s32[4]{0:T(128)} %fill_ref.3, ...), custom_call_target="tpu_custom_call" | custom-call | flops 1000 | bytes 2097152 | tf_op jit(solution)/shard_map/send_tiles/pallas_call | solution.py:101
  2.6 10.9 %all-to-all-start = ((bf16[128,32,128]{2,1,0:T(8,128)(2,1)}), bf16[128,32,128]{2,1,0:T(8,128)(2,1)S(1)}, u32[]{:S(2)}, u32[]{:S(2)}) async-start(bf16[128,32,128]{2,1,0:T(8,128)(2,1)} %get-tuple-element.17), calls=%async_computation | async-start | bytes 2097152 | tf_op jit(solution)/shard_map/all_to_all | solution.py:346
  13.5 4.9 %collective-permute-start = (bf16[272,128]{1,0:T(8,128)(2,1)S(1)}, bf16[272,128]{1,0:T(8,128)(2,1)S(1)}, u32[]{:S(2)}, u32[]{:S(2)}) collective-permute-start(bf16[272,128]{1,0:T(8,128)(2,1)S(1)} %get-tuple-element.15.refs_2_.request_ref), channel_id=1, source_target_pairs={{0,64},{8,72},{16,80},{24,88},{32,96},{40,104},{48,112},{56,120},{... | collective-permute-start | bytes 208904 | tf_op jit(solution)/shard_map/ppermute | solution.py:349
  18.4 1.1 %token_bias.2 = (bf16[1024,128]{1,0:T(8,128)(2,1)S(1)}, bf16[1024,128]{1,0:T(8,128)(2,1)S(1)}) custom-call(s32[1]{0:T(128)} %bitcast.half_ref.refs_0_, s32[1]{0:T(128)} %bitcast.1.core_ref.refs_1_, bf16[272,128]{1,0:T(8,128)(2,1)S(1)} %get-tuple-element.15.refs_2_.request_ref), custom_call_target="tpu_custom_call" | custom-call | flops 134217728 | bytes 262144 | tf_op jit(solution)/shard_map/token_bias/pallas_call | solution.py:153
  19.5 2.1 %local_part.1 = (f32[256,128]{1,0:T(8,128)S(1)}, f32[256,128]{1,0:T(8,128)S(1)}) custom-call(s32[4]{0:T(128)} %fill_ref.3, bf16[272,128]{1,0:T(8,128)(2,1)S(1)} %get-tuple-element.15.refs_2_.request_ref, bf16[64,32,128]{2,1,0:T(8,128)(2,1)} %bitcast.13, bf16[4,32,128]{2,1,0:T(8,128)(2,1)} %bitcast.16, bf16[4,4,2,128]{3,2,1,0:T(2,128)(2,1)} %bitcast.18, ...), custom_call_target="tpu_custom_call" | custom-call | flops 268435456 | bytes 1048576 | tf_op jit(solution)/shard_map/local_part/pallas_call | solution.py:206
  21.6 2.1 %collective-permute-done.refs_2_.request_ref = bf16[272,128]{1,0:T(8,128)(2,1)S(1)} collective-permute-done((bf16[272,128]{1,0:T(8,128)(2,1)S(1)}, bf16[272,128]{1,0:T(8,128)(2,1)S(1)}, u32[]{:S(2)}, u32[]{:S(2)}) %collective-permute-start) | collective-permute-done | bytes 69664 | tf_op jit(solution)/shard_map/ppermute | solution.py:349
  23.8 0.7 %token_bias.3.bias_ref = bf16[1024,128]{1,0:T(8,128)(2,1)S(1)} custom-call(s32[1]{0:T(128)} %bitcast.half_ref.refs_0_, s32[1]{0:T(128)} %bitcast.1.core_ref.refs_1_, bf16[272,128]{1,0:T(8,128)(2,1)S(1)} %collective-permute-done.refs_2_.request_ref), custom_call_target="tpu_custom_call" | custom-call | flops 134217728 | bytes 262144 | tf_op jit(solution)/shard_map/token_bias/pallas_call | solution.py:153
  24.5 0.0 all-to-all-done
  24.5 1.0 %far_part.1 = bf16[272,128]{1,0:T(8,128)(2,1)S(1)} custom-call(bf16[272,128]{1,0:T(8,128)(2,1)S(1)} %collective-permute-done.refs_2_.request_ref, bf16[1024,128]{1,0:T(8,128)(2,1)S(1)} %token_bias.3.bias_ref, bf16[32,4,32,128]{3,2,1,0:T(8,128)(2,1)S(1)} %bitcast.9, f32[256,128]{1,0:T(8,128)S(1)} %get-tuple-element.20.log_ref.after_ref), custom_call_target="tpu_custom_call" | custom-call | flops 268435456 | bytes 1048576 | tf_op jit(solution)/shard_map/far_part/pallas_call | solution.py:238
  25.5 6.5 %collective-permute-start.1 = (bf16[272,128]{1,0:T(8,128)(2,1)S(1)}, bf16[272,128]{1,0:T(8,128)(2,1)S(1)}, u32[]{:S(2)}, u32[]{:S(2)}) collective-permute-start(bf16[272,128]{1,0:T(8,128)(2,1)S(1)} %far_part.1), channel_id=1, source_target_pairs={{0,64},{8,72},{16,80},{24,88},{32,96},{40,104},{48,112},{56,120},{... | collective-permute-start | bytes 208904 | tf_op jit(solution)/shard_map/ppermute | solution.py:354
  32.0 0.9 %near_part.1 = (f32[256,128]{1,0:T(8,128)S(1)}, f32[256,128]{1,0:T(8,128)S(1)}) custom-call(bf16[272,128]{1,0:T(8,128)(2,1)S(1)} %get-tuple-element.15.refs_2_.request_ref, bf16[1024,128]{1,0:T(8,128)(2,1)S(1)} %get-tuple-element.16.bias_ref, bf16[32,4,32,128]{3,2,1,0:T(8,128)(2,1)S(1)} %bitcast.10, f32[256,128]{1,0:T(8,128)S(1)} %get-tuple-element.19.mixed_ref, ...), custom_call_target="tpu_custom_call" | custom-call | flops 268435456 | bytes 1048576 | tf_op jit(solution)/shard_map/near_part/pallas_call | solution.py:257
  33.0 0.8 %collective-permute-done.1.back_ref = bf16[272,128]{1,0:T(8,128)(2,1)S(1)} collective-permute-done((bf16[272,128]{1,0:T(8,128)(2,1)S(1)}, bf16[272,128]{1,0:T(8,128)(2,1)S(1)}, u32[]{:S(2)}, u32[]{:S(2)}) %collective-permute-start.1) | collective-permute-done | bytes 69664 | tf_op jit(solution)/shard_map/ppermute | solution.py:354
  33.7 0.3 merge.1
  34.0 0.0 copy-start
  34.0 21.2 %all_to_all.10.square_ref = f32[8,1,128]{2,1,0:T(1,128)S(1)} all-to-all(f32[8,1,128]{2,1,0:T(1,128)S(1)} %get-tuple-element.24), channel_id=1, replica_groups={{4,5,2,3,6,7,0,1},{12,13,10,11,14,15,8,9},{20,21,18,19,22,23,16,17},{28..., dimensions={0} | all-to-all | bytes 8192 | tf_op jit(solution)/shard_map/all_to_all | solution.py:357
  55.2 0.0 copy-done
  55.2 0.7 %normalize.1 = bf16[4,4,2048]{2,1,0:T(4,128)(2,1)} custom-call(bf16[256,128]{1,0:T(8,128)(2,1)S(1)} %get-tuple-element.23.attn_ref, f32[8,1,128]{2,1,0:T(1,128)S(1)} %all_to_all.10.square_ref, f32[16,128]{1,0:T(8,128)S(1)} %bitcast.11), custom_call_target="tpu_custom_call" | custom-call | tf_op jit(solution)/shard_map/normalize/pallas_call | solution.py:310
Async XLA Ops:
  2.6 21.9 %all-to-all-start = ((bf16[128,32,128]{2,1,0:T(8,128)(2,1)}), bf16[128,32,128]{2,1,0:T(8,128)(2,1)S(1)}, u32[]{:S(2)}, u32[]{:S(2)}) async-start(bf16[128,32,128]{2,1,0:T(8,128)(2,1)} %get-tuple-element.17), calls=%async_computation | async-start | bytes 2097152 | tf_op jit(solution)/shard_map/all_to_all | solution.py:346
  13.5 10.3 %collective-permute-start = (bf16[272,128]{1,0:T(8,128)(2,1)S(1)}, bf16[272,128]{1,0:T(8,128)(2,1)S(1)}, u32[]{:S(2)}, u32[]{:S(2)}) collective-permute-start(bf16[272,128]{1,0:T(8,128)(2,1)S(1)} %get-tuple-element.15.refs_2_.request_ref), channel_id=1, source_target_pairs={{0,64},{8,72},{16,80},{24,88},{32,96},{40,104},{48,112},{56,120},{... | collective-permute-start | bytes 208904 | tf_op jit(solution)/shard_map/ppermute | solution.py:349
  25.5 8.2 %collective-permute-start.1 = (bf16[272,128]{1,0:T(8,128)(2,1)S(1)}, bf16[272,128]{1,0:T(8,128)(2,1)S(1)}, u32[]{:S(2)}, u32[]{:S(2)}) collective-permute-start(bf16[272,128]{1,0:T(8,128)(2,1)S(1)} %far_part.1), channel_id=1, source_target_pairs={{0,64},{8,72},{16,80},{24,88},{32,96},{40,104},{48,112},{56,120},{... | collective-permute-start | bytes 208904 | tf_op jit(solution)/shard_map/ppermute | solution.py:354
  34.0 21.2 %copy-start = (f32[2048]{0:T(1024)S(1)}, f32[2048]{0:T(1024)}, u32[]{:S(2)}) copy-start(f32[2048]{0:T(1024)} %param.22) | copy-start | bytes 24580

commit v6 on v5

--- a/solution.py
+++ b/solution.py
@@ -25,11 +25,27 @@
 
 PLACES = [[place_of(j, core) for j in range(PEERS)] for core in range(2)]
 ORDERS = [[places.index(k) for k in range(PEERS)] for places in PLACES]
-HALVES = [
-    [(((j >> 3) << 4) | (half << 3) | (j & 7)) * 8 + tp for j in ORDERS[tp % 2]] for half in range(2) for tp in range(8)
-]
-STANDS = [PLACES[c][((t >> 4) << 3) | (t & 7)] * 4 + ((t >> 3) & 1) * 2 for c in range(2) for t in range(64)]
-PARTNERS = [(p, p ^ 8) for p in range(64)]
+
+
+def half_of(replica, core):
+    half = (replica >> 3) & 1
+    return half if core else half ^ ((replica >> 2) & 1)
+
+
+def replica_of(member, half, core):
+    zh = half if core else half ^ ((member >> 2) & 1)
+    return ((member >> 3) << 4) | (zh << 3) | (member & 7)
+
+
+def stand_of(target, core):
+    far = half_of(target, core)
+    image = target if core or not far else target ^ 4
+    return PLACES[core][((image >> 4) << 3) | (image & 7)] * 4 + far * 2
+
+
+HALVES = [[replica_of(j, half, tp % 2) * 8 + tp for j in ORDERS[tp % 2]] for half in range(2) for tp in range(8)]
+STANDS = [stand_of(t, c) for c in range(2) for t in range(64)]
+PARTNERS = [(p * 8 + tp, (p ^ (8 if tp % 2 else 4)) * 8 + tp) for p in range(64) for tp in range(8)]
 SUMMED = [[4, 5, 2, 3, 6, 7, 0, 1]]
 F32, BF16, I32 = jnp.float32, jnp.bfloat16, jnp.int32
 VMEM = pl.BlockSpec(memory_space=pltpu.VMEM)
@@ -67,7 +83,7 @@
         value = tail_tile(r, 1, fill, unfinished_ref, fresh_ref)
         key = jnp.where(rows < fill + switch_ref[r], key, MARK)
         tiles_ref[POOL + r] = jnp.concatenate([key, value], 0).astype(BF16)
-    flip = half_ref[0] * 2
+    flip = half_ref[0] * jnp.where(core_ref[0] == 1, 2, 2 + 4 * 4)
     table = core_ref[0] * 64
     low = jnp.int32(0)
     high = jnp.int32(0)
@@ -113,16 +129,15 @@
     info = request_ref[ROWS:, :].astype(F32).astype(I32)
     half = half_ref[0]
     token = iota((TOKENS, HD), 0)
-    entry = iota((TOKENS, HD), 1)
-    place, offset = token // PAGE, token % PAGE
+    entry = iota((1, HD), 1)
     lane = iota((1, HD), 1)
     pair, part = lane % PAIRS, lane // PAIRS
     step, req = pair // REQS, pair % REQS
-    inside, weights = [], []
+    held, weights = [], []
     late = jnp.zeros((1, HD), jnp.bool_)
     for g in range(REQS):
         pages, rest, moment = (info[REQS + i : REQS + i + 1, g : g + 1] for i in range(3))
-        inside.append(entry * PAGE + offset < pages * PAGE + rest)
+        held.append(jnp.clip(pages * PAGE + rest - entry * PAGE, 0, PAGE).astype(jnp.uint32))
         late = late | ((req == g) & (step < moment))
         spread = iota((HD, HD), 1)
         weights.append(((spread % REQS == g) & (spread < 3 * PAIRS)).astype(BF16))
@@ -132,13 +147,17 @@
         if section != "pool":
             slot = spot - POOL
             peer = slot >> 1
-            here = (slot >= 0) & (((peer >> 3) & 1) == half)
+            side = jnp.where(core_ref[0] == 1, half_of(peer, 1), half_of(peer, 0))
+            here = (slot >= 0) & (side == half)
             peer = ((peer >> 4) << 3) | (peer & 7)
             peer = jnp.where(core_ref[0] == 1, place_of(peer, 1), place_of(peer, 0))
-            spot = jnp.where(here, peer * 2 + (slot & 1), -1)
-        hits = [jnp.where((spot[g : g + 1, :] == place) & inside[g], 1.0, 0.0).astype(BF16) for g in range(REQS)]
+            spot = jnp.where(here, peer * 2 + (slot & 1), POOL)
+        first = spot * PAGE
+        hits = [
+            jnp.where((token - first[g : g + 1, :]).astype(jnp.uint32) < held[g], 1.0, 0.0).astype(BF16) for g in range(REQS)
+        ]
         count = dot(jnp.concatenate(hits, 1), weights, 1, 0)
-        log = jnp.log2(jnp.maximum(count, 1.0)) / SCALE
+        log = jnp.log2(jnp.maximum(count, 1.0)) * (1.0 / SCALE)
         high = log.astype(BF16).astype(F32)
         middle = (log - high).astype(BF16).astype(F32)
         parts = jnp.where(part == 0, high, jnp.where(part == 1, middle, log - high - middle))
@@ -330,8 +349,10 @@
     output_scaling_weights,
 ):
     ways = lax.axis_size("tp")
-    half = ((lax.axis_index("rep") >> 3) & 1).astype(I32).reshape(1)
-    core = (lax.axis_index("tp") & 1).astype(I32).reshape(1)
+    core = (lax.axis_index("tp") & 1).astype(I32)
+    replica = lax.axis_index("rep").astype(I32)
+    half = (((replica >> 3) ^ ((replica >> 2) & (1 - core))) & 1).reshape(1)
+    core = core.reshape(1)
     pool = cache_block_store.reshape(POOL, 2 * PAGE, HD)
     unfinished = unfinished_block_memory.reshape(REQS, 2 * PAGE, HD)
     fresh = fresh_token_memory.reshape(STEPS, REQS, 2, HD)
@@ -346,12 +367,12 @@
     tiles = lax.all_to_all(outgoing, ("rep", "tp"), split_axis=0, concat_axis=0, axis_index_groups=HALVES, tiled=True)
     tiles = tiles.reshape(PEERS, 4, 2 * PAGE, HD)
 
-    asked = lax.ppermute(request, "rep", PARTNERS)
+    asked = lax.ppermute(request, ("rep", "tp"), PARTNERS)
     pool_bias, near_bias = token_bias(("pool", "arrived"), half, core, request)
     mixed, log = local_part(fill, request, pool, unfinished, fresh, pool_bias)
     (far_bias,) = token_bias(("arrived",), half, core, asked)
 
-    back = lax.ppermute(far_part(asked, far_bias, tiles, log), "rep", PARTNERS)
+    back = lax.ppermute(far_part(asked, far_bias, tiles, log), ("rep", "tp"), PARTNERS)
     mixed, log = near_part(request, near_bias, tiles, mixed, log)
     attn, square = merge(mixed, log, back, ways)
     square = lax.all_to_all(square, "tp", split_axis=0, concat_axis=0, axis_index_groups=SUMMED, tiled=True)

time: 56.3 us -> 56.6 us (level)
  starting transfers between devices: 22.3 us -> 23.9 us
  blocking collectives: 21.2 us -> 20.6 us
    ppermute x2, starting transfers between devices: 11.4 us -> 13 us  [the longest x1 8.07 us: body(): lax.ppermute(far_part(asked, far_bias, tiles, log), ('rep', 'tp'), PARTNERS)]
    all_to_all x1, blocking collectives: 21.2 us -> 20.6 us  [body(): lax.all_to_all(square, 'tp', split_axis=0, concat_axis=0, axis_index_grou...]
  transfers between devices with their start and end apart: 3 -> 3, of which waited for: 2 -> 2; matrix products, arithmetic and copies ran while one was open for 0% -> 0% of each run, Pallas kernels for 9% -> 8%
where the time goes in v6:
time: 56.6 us; the launch traced here: 56.2 us
  starting transfers between devices  23.9 us (42%)
  blocking collectives  20.6 us (36%)
  Pallas kernels  9.31 us (16%)
  waiting for transfers between devices  2.36 us (4%)
    all_to_all x1, blocking collectives, body(): lax.all_to_all(square, 'tp', split_axis=0, concat_axis=0, axis_index_grou...  20.6 us
    all_to_all x1, starting transfers between devices, body(): lax.all_to_all(outgoing, ('rep', 'tp'), split_axis=0, concat_axis=0, axis...  10.9 us
    ppermute x1, starting transfers between devices, body(): lax.ppermute(far_part(asked, far_bias, tiles, log), ('rep', 'tp'), PARTNERS)  8.07 us
    ppermute x1, starting transfers between devices, body(): asked = lax.ppermute(request, ('rep', 'tp'), PARTNERS)  4.9 us
    pallas_call x1, Pallas kernels, send_tiles(): pl.pallas_call(send_kernel, out_shape=(pltpu.VMEM((PEERS * 4, 2 * PAGE, H...  2.59 us
    pallas_call x1, Pallas kernels, local_part(): pl.pallas_call(local_kernel, out_shape=(out, out), in_specs=[SMEM] + [VME...  2.09 us
    pallas_call x2, Pallas kernels, token_bias(): pl.pallas_call(lambda *refs: bias_kernel(sections, *refs), out_shape=(out...  1.63 us
    ppermute x1, waiting for transfers between devices, body(): asked = lax.ppermute(request, ('rep', 'tp'), PARTNERS)  1.6 us
  transfers between devices with their start and end apart: 3, of which 2 were waited for; matrix products, arithmetic and copies ran while one was open for 0% of the time, Pallas kernels for 8%

profile of v6, /device:TPU:1, one launch (start us, length us, event | category | flops | bytes accessed | tf_op | source)
XLA Modules:
  0.0 56.2 jit_solution(10270525479245000821)
XLA Ops:
  0.0 2.6 %send_tiles.1 = (bf16[128,32,128]{2,1,0:T(8,128)(2,1)}, bf16[272,128]{1,0:T(8,128)(2,1)S(1)}) custom-call(s32[1]{0:T(128)} %bitcast.half_ref.refs_0_, s32[1]{0:T(128)} %bitcast.1.core_ref.refs_1_, s32[64]{0:T(128)} %bitcast.19, s32[64]{0:T(128)} %source_ref.1, s32[128]{0:T(128)} %constant.17.clone.stand_ref, s32[4]{0:T(128)} %length_ref.1, s32[4]{0:T(128)} %fill_ref.3, ...), custom_call_target="tpu_custom_call" | custom-call | flops 1000 | bytes 2097152 | tf_op jit(solution)/shard_map/send_tiles/pallas_call | solution.py:117
  2.6 10.9 %all-to-all-start = ((bf16[128,32,128]{2,1,0:T(8,128)(2,1)}), bf16[128,32,128]{2,1,0:T(8,128)(2,1)S(1)}, u32[]{:S(2)}, u32[]{:S(2)}) async-start(bf16[128,32,128]{2,1,0:T(8,128)(2,1)} %get-tuple-element.17), calls=%async_computation | async-start | bytes 2097152 | tf_op jit(solution)/shard_map/all_to_all | solution.py:367
  13.5 4.9 %collective-permute-start = (bf16[272,128]{1,0:T(8,128)(2,1)S(1)}, bf16[272,128]{1,0:T(8,128)(2,1)S(1)}, u32[]{:S(2)}, u32[]{:S(2)}) collective-permute-start(bf16[272,128]{1,0:T(8,128)(2,1)S(1)} %get-tuple-element.15.refs_2_.request_ref), channel_id=1, source_target_pairs={{0,32},{1,65},{2,34},{3,67},{4,36},{5,69},{6,38},{7,71},{8,40},{9,... | collective-permute-start | bytes 208904 | tf_op jit(solution)/shard_map/ppermute | solution.py:370
  18.4 1.1 %token_bias.2 = (bf16[1024,128]{1,0:T(8,128)(2,1)S(1)}, bf16[1024,128]{1,0:T(8,128)(2,1)S(1)}) custom-call(s32[1]{0:T(128)} %bitcast.half_ref.refs_0_, s32[1]{0:T(128)} %bitcast.1.core_ref.refs_1_, bf16[272,128]{1,0:T(8,128)(2,1)S(1)} %get-tuple-element.15.refs_2_.request_ref), custom_call_target="tpu_custom_call" | custom-call | flops 134217728 | bytes 262144 | tf_op jit(solution)/shard_map/token_bias/pallas_call | solution.py:172
  19.5 2.1 %local_part.1 = (f32[256,128]{1,0:T(8,128)S(1)}, f32[256,128]{1,0:T(8,128)S(1)}) custom-call(s32[4]{0:T(128)} %fill_ref.3, bf16[272,128]{1,0:T(8,128)(2,1)S(1)} %get-tuple-element.15.refs_2_.request_ref, bf16[64,32,128]{2,1,0:T(8,128)(2,1)} %bitcast.13, bf16[4,32,128]{2,1,0:T(8,128)(2,1)} %bitcast.16, bf16[4,4,2,128]{3,2,1,0:T(2,128)(2,1)} %bitcast.18, ...), custom_call_target="tpu_custom_call" | custom-call | flops 268435456 | bytes 1048576 | tf_op jit(solution)/shard_map/local_part/pallas_call | solution.py:225
  21.6 1.6 %collective-permute-done.refs_2_.request_ref = bf16[272,128]{1,0:T(8,128)(2,1)S(1)} collective-permute-done((bf16[272,128]{1,0:T(8,128)(2,1)S(1)}, bf16[272,128]{1,0:T(8,128)(2,1)S(1)}, u32[]{:S(2)}, u32[]{:S(2)}) %collective-permute-start) | collective-permute-done | bytes 69664 | tf_op jit(solution)/shard_map/ppermute | solution.py:370
  23.2 0.6 %token_bias.3.bias_ref = bf16[1024,128]{1,0:T(8,128)(2,1)S(1)} custom-call(s32[1]{0:T(128)} %bitcast.half_ref.refs_0_, s32[1]{0:T(128)} %bitcast.1.core_ref.refs_1_, bf16[272,128]{1,0:T(8,128)(2,1)S(1)} %collective-permute-done.refs_2_.request_ref), custom_call_target="tpu_custom_call" | custom-call | flops 134217728 | bytes 262144 | tf_op jit(solution)/shard_map/token_bias/pallas_call | solution.py:172
  23.8 0.0 all-to-all-done
  23.8 1.0 %far_part.1 = bf16[272,128]{1,0:T(8,128)(2,1)S(1)} custom-call(bf16[272,128]{1,0:T(8,128)(2,1)S(1)} %collective-permute-done.refs_2_.request_ref, bf16[1024,128]{1,0:T(8,128)(2,1)S(1)} %token_bias.3.bias_ref, bf16[32,4,32,128]{3,2,1,0:T(8,128)(2,1)S(1)} %bitcast.9, f32[256,128]{1,0:T(8,128)S(1)} %get-tuple-element.20.log_ref.after_ref), custom_call_target="tpu_custom_call" | custom-call | flops 268435456 | bytes 1048576 | tf_op jit(solution)/shard_map/far_part/pallas_call | solution.py:257
  24.8 8.1 %collective-permute-start.1 = (bf16[272,128]{1,0:T(8,128)(2,1)S(1)}, bf16[272,128]{1,0:T(8,128)(2,1)S(1)}, u32[]{:S(2)}, u32[]{:S(2)}) collective-permute-start(bf16[272,128]{1,0:T(8,128)(2,1)S(1)} %far_part.1), channel_id=1, source_target_pairs={{0,32},{1,65},{2,34},{3,67},{4,36},{5,69},{6,38},{7,71},{8,40},{9,... | collective-permute-start | bytes 208904 | tf_op jit(solution)/shard_map/ppermute | solution.py:375
  32.8 0.9 %near_part.1 = (f32[256,128]{1,0:T(8,128)S(1)}, f32[256,128]{1,0:T(8,128)S(1)}) custom-call(bf16[272,128]{1,0:T(8,128)(2,1)S(1)} %get-tuple-element.15.refs_2_.request_ref, bf16[1024,128]{1,0:T(8,128)(2,1)S(1)} %get-tuple-element.16.bias_ref, bf16[32,4,32,128]{3,2,1,0:T(8,128)(2,1)S(1)} %bitcast.10, f32[256,128]{1,0:T(8,128)S(1)} %get-tuple-element.19.mixed_ref, ...), custom_call_target="tpu_custom_call" | custom-call | flops 268435456 | bytes 1048576 | tf_op jit(solution)/shard_map/near_part/pallas_call | solution.py:276
  33.8 0.8 %collective-permute-done.1.back_ref = bf16[272,128]{1,0:T(8,128)(2,1)S(1)} collective-permute-done((bf16[272,128]{1,0:T(8,128)(2,1)S(1)}, bf16[272,128]{1,0:T(8,128)(2,1)S(1)}, u32[]{:S(2)}, u32[]{:S(2)}) %collective-permute-start.1) | collective-permute-done | bytes 69664 | tf_op jit(solution)/shard_map/ppermute | solution.py:375
  34.5 0.3 merge.1
  34.8 0.0 copy-start
  34.9 20.6 %all_to_all.10.square_ref = f32[8,1,128]{2,1,0:T(1,128)S(1)} all-to-all(f32[8,1,128]{2,1,0:T(1,128)S(1)} %get-tuple-element.24), channel_id=1, replica_groups={{4,5,2,3,6,7,0,1},{12,13,10,11,14,15,8,9},{20,21,18,19,22,23,16,17},{28..., dimensions={0} | all-to-all | bytes 8192 | tf_op jit(solution)/shard_map/all_to_all | solution.py:378
  55.4 0.0 copy-done
  55.5 0.7 %normalize.1 = bf16[4,4,2048]{2,1,0:T(4,128)(2,1)} custom-call(bf16[256,128]{1,0:T(8,128)(2,1)S(1)} %get-tuple-element.23.attn_ref, f32[8,1,128]{2,1,0:T(1,128)S(1)} %all_to_all.10.square_ref, f32[16,128]{1,0:T(8,128)S(1)} %bitcast.11), custom_call_target="tpu_custom_call" | custom-call | tf_op jit(solution)/shard_map/normalize/pallas_call | solution.py:329
Async XLA Ops:
  2.6 21.2 %all-to-all-start = ((bf16[128,32,128]{2,1,0:T(8,128)(2,1)}), bf16[128,32,128]{2,1,0:T(8,128)(2,1)S(1)}, u32[]{:S(2)}, u32[]{:S(2)}) async-start(bf16[128,32,128]{2,1,0:T(8,128)(2,1)} %get-tuple-element.17), calls=%async_computation | async-start | bytes 2097152 | tf_op jit(solution)/shard_map/all_to_all | solution.py:367
  13.5 9.7 %collective-permute-start = (bf16[272,128]{1,0:T(8,128)(2,1)S(1)}, bf16[272,128]{1,0:T(8,128)(2,1)S(1)}, u32[]{:S(2)}, u32[]{:S(2)}) collective-permute-start(bf16[272,128]{1,0:T(8,128)(2,1)S(1)} %get-tuple-element.15.refs_2_.request_ref), channel_id=1, source_target_pairs={{0,32},{1,65},{2,34},{3,67},{4,36},{5,69},{6,38},{7,71},{8,40},{9,... | collective-permute-start | bytes 208904 | tf_op jit(solution)/shard_map/ppermute | solution.py:370
  24.8 9.8 %collective-permute-start.1 = (bf16[272,128]{1,0:T(8,128)(2,1)S(1)}, bf16[272,128]{1,0:T(8,128)(2,1)S(1)}, u32[]{:S(2)}, u32[]{:S(2)}) collective-permute-start(bf16[272,128]{1,0:T(8,128)(2,1)S(1)} %far_part.1), channel_id=1, source_target_pairs={{0,32},{1,65},{2,34},{3,67},{4,36},{5,69},{6,38},{7,71},{8,40},{9,... | collective-permute-start | bytes 208904 | tf_op jit(solution)/shard_map/ppermute | solution.py:375
  34.8 20.6 %copy-start = (f32[2048]{0:T(1024)S(1)}, f32[2048]{0:T(1024)}, u32[]{:S(2)}) copy-start(f32[2048]{0:T(1024)} %param.22) | copy-start | bytes 24580

commit v7 on v6

--- a/solution.py
+++ b/solution.py
@@ -18,7 +18,7 @@
 SCALE = 1.4426950408889634 / HD**0.5
 def place_of(member, core):
     if core == 0:
-        return member ^ 27
+        return member ^ 18
     place = member ^ 31
     return ((place & 3) << 3) | (place & 4) | (place >> 3)
 

time: 56.6 us -> 55.7 us (0.984)
  blocking collectives: 20.6 us -> 19.7 us
    all_to_all x1, blocking collectives: 20.6 us -> 19.7 us  [body(): lax.all_to_all(square, 'tp', split_axis=0, concat_axis=0, axis_index_grou...]
  transfers between devices with their start and end apart: 3 -> 3, of which waited for: 2 -> 3; matrix products, arithmetic and copies ran while one was open for 0% -> 0% of each run, Pallas kernels for 8% -> 8%
where the time goes in v7:
time: 55.7 us; the launch traced here: 55.4 us
  starting transfers between devices  24 us (43%)
  blocking collectives  19.7 us (35%)
  Pallas kernels  9.31 us (17%)
  waiting for transfers between devices  2.27 us (4%)
    all_to_all x1, blocking collectives, body(): lax.all_to_all(square, 'tp', split_axis=0, concat_axis=0, axis_index_grou...  19.7 us
    all_to_all x1, starting transfers between devices, body(): lax.all_to_all(outgoing, ('rep', 'tp'), split_axis=0, concat_axis=0, axis...  10.9 us
    ppermute x1, starting transfers between devices, body(): lax.ppermute(far_part(asked, far_bias, tiles, log), ('rep', 'tp'), PARTNERS)  8.17 us
    ppermute x1, starting transfers between devices, body(): asked = lax.ppermute(request, ('rep', 'tp'), PARTNERS)  4.9 us
    pallas_call x1, Pallas kernels, send_tiles(): pl.pallas_call(send_kernel, out_shape=(pltpu.VMEM((PEERS * 4, 2 * PAGE, H...  2.59 us
    pallas_call x1, Pallas kernels, local_part(): pl.pallas_call(local_kernel, out_shape=(out, out), in_specs=[SMEM] + [VME...  2.09 us
    pallas_call x2, Pallas kernels, token_bias(): pl.pallas_call(lambda *refs: bias_kernel(sections, *refs), out_shape=(out...  1.64 us
    ppermute x1, waiting for transfers between devices, body(): asked = lax.ppermute(request, ('rep', 'tp'), PARTNERS)  1.38 us
  transfers between devices with their start and end apart: 3, of which 3 were waited for; matrix products, arithmetic and copies ran while one was open for 0% of the time, Pallas kernels for 8%

profile of v7, /device:TPU:1, one launch (start us, length us, event | category | flops | bytes accessed | tf_op | source)
XLA Modules:
  0.0 55.4 jit_solution(4427129802994040538)
XLA Ops:
  0.0 2.6 %send_tiles.1 = (bf16[128,32,128]{2,1,0:T(8,128)(2,1)}, bf16[272,128]{1,0:T(8,128)(2,1)S(1)}) custom-call(s32[1]{0:T(128)} %bitcast.half_ref.refs_0_, s32[1]{0:T(128)} %bitcast.1.core_ref.refs_1_, s32[64]{0:T(128)} %bitcast.19, s32[64]{0:T(128)} %source_ref.1, s32[128]{0:T(128)} %constant.17.clone.stand_ref, s32[4]{0:T(128)} %length_ref.1, s32[4]{0:T(128)} %fill_ref.3, ...), custom_call_target="tpu_custom_call" | custom-call | flops 1000 | bytes 2097152 | tf_op jit(solution)/shard_map/send_tiles/pallas_call | solution.py:117
  2.6 10.9 %all-to-all-start = ((bf16[128,32,128]{2,1,0:T(8,128)(2,1)}), bf16[128,32,128]{2,1,0:T(8,128)(2,1)S(1)}, u32[]{:S(2)}, u32[]{:S(2)}) async-start(bf16[128,32,128]{2,1,0:T(8,128)(2,1)} %get-tuple-element.17), calls=%async_computation | async-start | bytes 2097152 | tf_op jit(solution)/shard_map/all_to_all | solution.py:367
  13.5 4.9 %collective-permute-start = (bf16[272,128]{1,0:T(8,128)(2,1)S(1)}, bf16[272,128]{1,0:T(8,128)(2,1)S(1)}, u32[]{:S(2)}, u32[]{:S(2)}) collective-permute-start(bf16[272,128]{1,0:T(8,128)(2,1)S(1)} %get-tuple-element.15.refs_2_.request_ref), channel_id=1, source_target_pairs={{0,32},{1,65},{2,34},{3,67},{4,36},{5,69},{6,38},{7,71},{8,40},{9,... | collective-permute-start | bytes 208904 | tf_op jit(solution)/shard_map/ppermute | solution.py:370
  18.4 1.1 %token_bias.2 = (bf16[1024,128]{1,0:T(8,128)(2,1)S(1)}, bf16[1024,128]{1,0:T(8,128)(2,1)S(1)}) custom-call(s32[1]{0:T(128)} %bitcast.half_ref.refs_0_, s32[1]{0:T(128)} %bitcast.1.core_ref.refs_1_, bf16[272,128]{1,0:T(8,128)(2,1)S(1)} %get-tuple-element.15.refs_2_.request_ref), custom_call_target="tpu_custom_call" | custom-call | flops 134217728 | bytes 262144 | tf_op jit(solution)/shard_map/token_bias/pallas_call | solution.py:172
  19.5 2.1 %local_part.1 = (f32[256,128]{1,0:T(8,128)S(1)}, f32[256,128]{1,0:T(8,128)S(1)}) custom-call(s32[4]{0:T(128)} %fill_ref.3, bf16[272,128]{1,0:T(8,128)(2,1)S(1)} %get-tuple-element.15.refs_2_.request_ref, bf16[64,32,128]{2,1,0:T(8,128)(2,1)} %bitcast.13, bf16[4,32,128]{2,1,0:T(8,128)(2,1)} %bitcast.16, bf16[4,4,2,128]{3,2,1,0:T(2,128)(2,1)} %bitcast.18, ...), custom_call_target="tpu_custom_call" | custom-call | flops 268435456 | bytes 1048576 | tf_op jit(solution)/shard_map/local_part/pallas_call | solution.py:225
  21.6 1.4 %collective-permute-done.refs_2_.request_ref = bf16[272,128]{1,0:T(8,128)(2,1)S(1)} collective-permute-done((bf16[272,128]{1,0:T(8,128)(2,1)S(1)}, bf16[272,128]{1,0:T(8,128)(2,1)S(1)}, u32[]{:S(2)}, u32[]{:S(2)}) %collective-permute-start) | collective-permute-done | bytes 69664 | tf_op jit(solution)/shard_map/ppermute | solution.py:370
  23.0 0.6 %token_bias.3.bias_ref = bf16[1024,128]{1,0:T(8,128)(2,1)S(1)} custom-call(s32[1]{0:T(128)} %bitcast.half_ref.refs_0_, s32[1]{0:T(128)} %bitcast.1.core_ref.refs_1_, bf16[272,128]{1,0:T(8,128)(2,1)S(1)} %collective-permute-done.refs_2_.request_ref), custom_call_target="tpu_custom_call" | custom-call | flops 134217728 | bytes 262144 | tf_op jit(solution)/shard_map/token_bias/pallas_call | solution.py:172
  23.5 0.1 all-to-all-done
  23.7 1.0 %far_part.1 = bf16[272,128]{1,0:T(8,128)(2,1)S(1)} custom-call(bf16[272,128]{1,0:T(8,128)(2,1)S(1)} %collective-permute-done.refs_2_.request_ref, bf16[1024,128]{1,0:T(8,128)(2,1)S(1)} %token_bias.3.bias_ref, bf16[32,4,32,128]{3,2,1,0:T(8,128)(2,1)S(1)} %bitcast.9, f32[256,128]{1,0:T(8,128)S(1)} %get-tuple-element.20.log_ref.after_ref), custom_call_target="tpu_custom_call" | custom-call | flops 268435456 | bytes 1048576 | tf_op jit(solution)/shard_map/far_part/pallas_call | solution.py:257
  24.7 8.2 %collective-permute-start.1 = (bf16[272,128]{1,0:T(8,128)(2,1)S(1)}, bf16[272,128]{1,0:T(8,128)(2,1)S(1)}, u32[]{:S(2)}, u32[]{:S(2)}) collective-permute-start(bf16[272,128]{1,0:T(8,128)(2,1)S(1)} %far_part.1), channel_id=1, source_target_pairs={{0,32},{1,65},{2,34},{3,67},{4,36},{5,69},{6,38},{7,71},{8,40},{9,... | collective-permute-start | bytes 208904 | tf_op jit(solution)/shard_map/ppermute | solution.py:375
  32.8 0.9 %near_part.1 = (f32[256,128]{1,0:T(8,128)S(1)}, f32[256,128]{1,0:T(8,128)S(1)}) custom-call(bf16[272,128]{1,0:T(8,128)(2,1)S(1)} %get-tuple-element.15.refs_2_.request_ref, bf16[1024,128]{1,0:T(8,128)(2,1)S(1)} %get-tuple-element.16.bias_ref, bf16[32,4,32,128]{3,2,1,0:T(8,128)(2,1)S(1)} %bitcast.10, f32[256,128]{1,0:T(8,128)S(1)} %get-tuple-element.19.mixed_ref, ...), custom_call_target="tpu_custom_call" | custom-call | flops 268435456 | bytes 1048576 | tf_op jit(solution)/shard_map/near_part/pallas_call | solution.py:276
  33.8 0.8 %collective-permute-done.1.back_ref = bf16[272,128]{1,0:T(8,128)(2,1)S(1)} collective-permute-done((bf16[272,128]{1,0:T(8,128)(2,1)S(1)}, bf16[272,128]{1,0:T(8,128)(2,1)S(1)}, u32[]{:S(2)}, u32[]{:S(2)}) %collective-permute-start.1) | collective-permute-done | bytes 69664 | tf_op jit(solution)/shard_map/ppermute | solution.py:375
  34.5 0.3 merge.1
  34.8 0.0 copy-start
  34.9 19.7 %all_to_all.10.square_ref = f32[8,1,128]{2,1,0:T(1,128)S(1)} all-to-all(f32[8,1,128]{2,1,0:T(1,128)S(1)} %get-tuple-element.24), channel_id=1, replica_groups={{4,5,2,3,6,7,0,1},{12,13,10,11,14,15,8,9},{20,21,18,19,22,23,16,17},{28..., dimensions={0} | all-to-all | bytes 8192 | tf_op jit(solution)/shard_map/all_to_all | solution.py:378
  54.6 0.0 copy-done
  54.6 0.7 %normalize.1 = bf16[4,4,2048]{2,1,0:T(4,128)(2,1)} custom-call(bf16[256,128]{1,0:T(8,128)(2,1)S(1)} %get-tuple-element.23.attn_ref, f32[8,1,128]{2,1,0:T(1,128)S(1)} %all_to_all.10.square_ref, f32[16,128]{1,0:T(8,128)S(1)} %bitcast.11), custom_call_target="tpu_custom_call" | custom-call | tf_op jit(solution)/shard_map/normalize/pallas_call | solution.py:329
Async XLA Ops:
  2.6 21.1 %all-to-all-start = ((bf16[128,32,128]{2,1,0:T(8,128)(2,1)}), bf16[128,32,128]{2,1,0:T(8,128)(2,1)S(1)}, u32[]{:S(2)}, u32[]{:S(2)}) async-start(bf16[128,32,128]{2,1,0:T(8,128)(2,1)} %get-tuple-element.17), calls=%async_computation | async-start | bytes 2097152 | tf_op jit(solution)/shard_map/all_to_all | solution.py:367
  13.5 9.5 %collective-permute-start = (bf16[272,128]{1,0:T(8,128)(2,1)S(1)}, bf16[272,128]{1,0:T(8,128)(2,1)S(1)}, u32[]{:S(2)}, u32[]{:S(2)}) collective-permute-start(bf16[272,128]{1,0:T(8,128)(2,1)S(1)} %get-tuple-element.15.refs_2_.request_ref), channel_id=1, source_target_pairs={{0,32},{1,65},{2,34},{3,67},{4,36},{5,69},{6,38},{7,71},{8,40},{9,... | collective-permute-start | bytes 208904 | tf_op jit(solution)/shard_map/ppermute | solution.py:370
  24.7 9.9 %collective-permute-start.1 = (bf16[272,128]{1,0:T(8,128)(2,1)S(1)}, bf16[272,128]{1,0:T(8,128)(2,1)S(1)}, u32[]{:S(2)}, u32[]{:S(2)}) collective-permute-start(bf16[272,128]{1,0:T(8,128)(2,1)S(1)} %far_part.1), channel_id=1, source_target_pairs={{0,32},{1,65},{2,34},{3,67},{4,36},{5,69},{6,38},{7,71},{8,40},{9,... | collective-permute-start | bytes 208904 | tf_op jit(solution)/shard_map/ppermute | solution.py:375
  34.8 19.8 %copy-start = (f32[2048]{0:T(1024)S(1)}, f32[2048]{0:T(1024)}, u32[]{:S(2)}) copy-start(f32[2048]{0:T(1024)} %param.22) | copy-start | bytes 24580

commit v8 on v7

--- a/solution.py
+++ b/solution.py
@@ -19,7 +19,7 @@
 def place_of(member, core):
     if core == 0:
         return member ^ 18
-    place = member ^ 31
+    place = member ^ 18
     return ((place & 3) << 3) | (place & 4) | (place >> 3)
 
 

time: 55.7 us -> 55.7 us (level)
  transfers between devices with their start and end apart: 3 -> 3, of which waited for: 3 -> 2; matrix products, arithmetic and copies ran while one was open for 0% -> 0% of each run, Pallas kernels for 8% -> 8%
where the time goes in v8:
time: 55.7 us; the launch traced here: 55.3 us
  starting transfers between devices  24.1 us (43%)
  blocking collectives  20 us (36%)
  Pallas kernels  9.31 us (17%)
  waiting for transfers between devices  1.87 us (3%)
    all_to_all x1, blocking collectives, body(): lax.all_to_all(square, 'tp', split_axis=0, concat_axis=0, axis_index_grou...  20 us
    all_to_all x1, starting transfers between devices, body(): lax.all_to_all(outgoing, ('rep', 'tp'), split_axis=0, concat_axis=0, axis...  10.6 us
    ppermute x1, starting transfers between devices, body(): lax.ppermute(far_part(asked, far_bias, tiles, log), ('rep', 'tp'), PARTNERS)  8.56 us
    ppermute x1, starting transfers between devices, body(): asked = lax.ppermute(request, ('rep', 'tp'), PARTNERS)  4.9 us
    pallas_call x1, Pallas kernels, send_tiles(): pl.pallas_call(send_kernel, out_shape=(pltpu.VMEM((PEERS * 4, 2 * PAGE, H...  2.59 us
    pallas_call x1, Pallas kernels, local_part(): pl.pallas_call(local_kernel, out_shape=(out, out), in_specs=[SMEM] + [VME...  2.09 us
    pallas_call x2, Pallas kernels, token_bias(): pl.pallas_call(lambda *refs: bias_kernel(sections, *refs), out_shape=(out...  1.64 us
  transfers between devices with their start and end apart: 3, of which 2 were waited for; matrix products, arithmetic and copies ran while one was open for 0% of the time, Pallas kernels for 8%

profile of v8, /device:TPU:1, one launch (start us, length us, event | category | flops | bytes accessed | tf_op | source)
XLA Modules:
  0.0 55.3 jit_solution(15199520133951607056)
XLA Ops:
  0.0 2.6 %send_tiles.1 = (bf16[128,32,128]{2,1,0:T(8,128)(2,1)}, bf16[272,128]{1,0:T(8,128)(2,1)S(1)}) custom-call(s32[1]{0:T(128)} %bitcast.half_ref.refs_0_, s32[1]{0:T(128)} %bitcast.1.core_ref.refs_1_, s32[64]{0:T(128)} %bitcast.19, s32[64]{0:T(128)} %source_ref.1, s32[128]{0:T(128)} %constant.17.clone.stand_ref, s32[4]{0:T(128)} %length_ref.1, s32[4]{0:T(128)} %fill_ref.3, ...), custom_call_target="tpu_custom_call" | custom-call | flops 1000 | bytes 2097152 | tf_op jit(solution)/shard_map/send_tiles/pallas_call | solution.py:117
  2.6 10.6 %all-to-all-start = ((bf16[128,32,128]{2,1,0:T(8,128)(2,1)}), bf16[128,32,128]{2,1,0:T(8,128)(2,1)S(1)}, u32[]{:S(2)}, u32[]{:S(2)}) async-start(bf16[128,32,128]{2,1,0:T(8,128)(2,1)} %get-tuple-element.17), calls=%async_computation | async-start | bytes 2097152 | tf_op jit(solution)/shard_map/all_to_all | solution.py:367
  13.2 4.9 %collective-permute-start = (bf16[272,128]{1,0:T(8,128)(2,1)S(1)}, bf16[272,128]{1,0:T(8,128)(2,1)S(1)}, u32[]{:S(2)}, u32[]{:S(2)}) collective-permute-start(bf16[272,128]{1,0:T(8,128)(2,1)S(1)} %get-tuple-element.15.refs_2_.request_ref), channel_id=1, source_target_pairs={{0,32},{1,65},{2,34},{3,67},{4,36},{5,69},{6,38},{7,71},{8,40},{9,... | collective-permute-start | bytes 208904 | tf_op jit(solution)/shard_map/ppermute | solution.py:370
  18.1 1.1 %token_bias.2 = (bf16[1024,128]{1,0:T(8,128)(2,1)S(1)}, bf16[1024,128]{1,0:T(8,128)(2,1)S(1)}) custom-call(s32[1]{0:T(128)} %bitcast.half_ref.refs_0_, s32[1]{0:T(128)} %bitcast.1.core_ref.refs_1_, bf16[272,128]{1,0:T(8,128)(2,1)S(1)} %get-tuple-element.15.refs_2_.request_ref), custom_call_target="tpu_custom_call" | custom-call | flops 134217728 | bytes 262144 | tf_op jit(solution)/shard_map/token_bias/pallas_call | solution.py:172
  19.2 2.1 %local_part.1 = (f32[256,128]{1,0:T(8,128)S(1)}, f32[256,128]{1,0:T(8,128)S(1)}) custom-call(s32[4]{0:T(128)} %fill_ref.3, bf16[272,128]{1,0:T(8,128)(2,1)S(1)} %get-tuple-element.15.refs_2_.request_ref, bf16[64,32,128]{2,1,0:T(8,128)(2,1)} %bitcast.13, bf16[4,32,128]{2,1,0:T(8,128)(2,1)} %bitcast.16, bf16[4,4,2,128]{3,2,1,0:T(2,128)(2,1)} %bitcast.18, ...), custom_call_target="tpu_custom_call" | custom-call | flops 268435456 | bytes 1048576 | tf_op jit(solution)/shard_map/local_part/pallas_call | solution.py:225
  21.3 1.1 %collective-permute-done.refs_2_.request_ref = bf16[272,128]{1,0:T(8,128)(2,1)S(1)} collective-permute-done((bf16[272,128]{1,0:T(8,128)(2,1)S(1)}, bf16[272,128]{1,0:T(8,128)(2,1)S(1)}, u32[]{:S(2)}, u32[]{:S(2)}) %collective-permute-start) | collective-permute-done | bytes 69664 | tf_op jit(solution)/shard_map/ppermute | solution.py:370
  22.4 0.6 %token_bias.3.bias_ref = bf16[1024,128]{1,0:T(8,128)(2,1)S(1)} custom-call(s32[1]{0:T(128)} %bitcast.half_ref.refs_0_, s32[1]{0:T(128)} %bitcast.1.core_ref.refs_1_, bf16[272,128]{1,0:T(8,128)(2,1)S(1)} %collective-permute-done.refs_2_.request_ref), custom_call_target="tpu_custom_call" | custom-call | flops 134217728 | bytes 262144 | tf_op jit(solution)/shard_map/token_bias/pallas_call | solution.py:172
  23.0 0.0 all-to-all-done
  23.0 1.0 %far_part.1 = bf16[272,128]{1,0:T(8,128)(2,1)S(1)} custom-call(bf16[272,128]{1,0:T(8,128)(2,1)S(1)} %collective-permute-done.refs_2_.request_ref, bf16[1024,128]{1,0:T(8,128)(2,1)S(1)} %token_bias.3.bias_ref, bf16[32,4,32,128]{3,2,1,0:T(8,128)(2,1)S(1)} %bitcast.9, f32[256,128]{1,0:T(8,128)S(1)} %get-tuple-element.20.log_ref.after_ref), custom_call_target="tpu_custom_call" | custom-call | flops 268435456 | bytes 1048576 | tf_op jit(solution)/shard_map/far_part/pallas_call | solution.py:257
  24.0 8.6 %collective-permute-start.1 = (bf16[272,128]{1,0:T(8,128)(2,1)S(1)}, bf16[272,128]{1,0:T(8,128)(2,1)S(1)}, u32[]{:S(2)}, u32[]{:S(2)}) collective-permute-start(bf16[272,128]{1,0:T(8,128)(2,1)S(1)} %far_part.1), channel_id=1, source_target_pairs={{0,32},{1,65},{2,34},{3,67},{4,36},{5,69},{6,38},{7,71},{8,40},{9,... | collective-permute-start | bytes 208904 | tf_op jit(solution)/shard_map/ppermute | solution.py:375
  32.6 0.9 %near_part.1 = (f32[256,128]{1,0:T(8,128)S(1)}, f32[256,128]{1,0:T(8,128)S(1)}) custom-call(bf16[272,128]{1,0:T(8,128)(2,1)S(1)} %get-tuple-element.15.refs_2_.request_ref, bf16[1024,128]{1,0:T(8,128)(2,1)S(1)} %get-tuple-element.16.bias_ref, bf16[32,4,32,128]{3,2,1,0:T(8,128)(2,1)S(1)} %bitcast.10, f32[256,128]{1,0:T(8,128)S(1)} %get-tuple-element.19.mixed_ref, ...), custom_call_target="tpu_custom_call" | custom-call | flops 268435456 | bytes 1048576 | tf_op jit(solution)/shard_map/near_part/pallas_call | solution.py:276
  33.5 0.8 %collective-permute-done.1.back_ref = bf16[272,128]{1,0:T(8,128)(2,1)S(1)} collective-permute-done((bf16[272,128]{1,0:T(8,128)(2,1)S(1)}, bf16[272,128]{1,0:T(8,128)(2,1)S(1)}, u32[]{:S(2)}, u32[]{:S(2)}) %collective-permute-start.1) | collective-permute-done | bytes 69664 | tf_op jit(solution)/shard_map/ppermute | solution.py:375
  34.3 0.3 merge.1
  34.6 0.0 copy-start
  34.6 20.0 %all_to_all.10.square_ref = f32[8,1,128]{2,1,0:T(1,128)S(1)} all-to-all(f32[8,1,128]{2,1,0:T(1,128)S(1)} %get-tuple-element.24), channel_id=1, replica_groups={{4,5,2,3,6,7,0,1},{12,13,10,11,14,15,8,9},{20,21,18,19,22,23,16,17},{28..., dimensions={0} | all-to-all | bytes 8192 | tf_op jit(solution)/shard_map/all_to_all | solution.py:378
  54.6 0.0 copy-done
  54.6 0.7 %normalize.1 = bf16[4,4,2048]{2,1,0:T(4,128)(2,1)} custom-call(bf16[256,128]{1,0:T(8,128)(2,1)S(1)} %get-tuple-element.23.attn_ref, f32[8,1,128]{2,1,0:T(1,128)S(1)} %all_to_all.10.square_ref, f32[16,128]{1,0:T(8,128)S(1)} %bitcast.11), custom_call_target="tpu_custom_call" | custom-call | tf_op jit(solution)/shard_map/normalize/pallas_call | solution.py:329
Async XLA Ops:
  2.6 20.4 %all-to-all-start = ((bf16[128,32,128]{2,1,0:T(8,128)(2,1)}), bf16[128,32,128]{2,1,0:T(8,128)(2,1)S(1)}, u32[]{:S(2)}, u32[]{:S(2)}) async-start(bf16[128,32,128]{2,1,0:T(8,128)(2,1)} %get-tuple-element.17), calls=%async_computation | async-start | bytes 2097152 | tf_op jit(solution)/shard_map/all_to_all | solution.py:367
  13.2 9.2 %collective-permute-start = (bf16[272,128]{1,0:T(8,128)(2,1)S(1)}, bf16[272,128]{1,0:T(8,128)(2,1)S(1)}, u32[]{:S(2)}, u32[]{:S(2)}) collective-permute-start(bf16[272,128]{1,0:T(8,128)(2,1)S(1)} %get-tuple-element.15.refs_2_.request_ref), channel_id=1, source_target_pairs={{0,32},{1,65},{2,34},{3,67},{4,36},{5,69},{6,38},{7,71},{8,40},{9,... | collective-permute-start | bytes 208904 | tf_op jit(solution)/shard_map/ppermute | solution.py:370
  24.0 10.3 %collective-permute-start.1 = (bf16[272,128]{1,0:T(8,128)(2,1)S(1)}, bf16[272,128]{1,0:T(8,128)(2,1)S(1)}, u32[]{:S(2)}, u32[]{:S(2)}) collective-permute-start(bf16[272,128]{1,0:T(8,128)(2,1)S(1)} %far_part.1), channel_id=1, source_target_pairs={{0,32},{1,65},{2,34},{3,67},{4,36},{5,69},{6,38},{7,71},{8,40},{9,... | collective-permute-start | bytes 208904 | tf_op jit(solution)/shard_map/ppermute | solution.py:375
  34.6 20.0 %copy-start = (f32[2048]{0:T(1024)S(1)}, f32[2048]{0:T(1024)}, u32[]{:S(2)}) copy-start(f32[2048]{0:T(1024)} %param.22) | copy-start | bytes 24580

commit v9 on v8

--- a/solution.py
+++ b/solution.py
@@ -17,7 +17,7 @@
 MARK = 4096.0
 SCALE = 1.4426950408889634 / HD**0.5
 def place_of(member, core):
-    if core == 0:
+    if core == 1:
         return member ^ 18
     place = member ^ 18
     return ((place & 3) << 3) | (place & 4) | (place >> 3)

time: 55.7 us -> 56 us (level)
  waiting for transfers between devices: 1.87 us -> 2.44 us
    ppermute x1, waiting for transfers between devices: 1.11 us -> 1.68 us  [body(): asked = lax.ppermute(request, ('rep', 'tp'), PARTNERS)]
where the time goes in v9:
time: 56 us; the launch traced here: 55.6 us
  starting transfers between devices  23.7 us (42%)
  blocking collectives  20.1 us (36%)
  Pallas kernels  9.31 us (17%)
  waiting for transfers between devices  2.44 us (4%)
    all_to_all x1, blocking collectives, body(): lax.all_to_all(square, 'tp', split_axis=0, concat_axis=0, axis_index_grou...  20.1 us
    all_to_all x1, starting transfers between devices, body(): lax.all_to_all(outgoing, ('rep', 'tp'), split_axis=0, concat_axis=0, axis...  10.6 us
    ppermute x1, starting transfers between devices, body(): lax.ppermute(far_part(asked, far_bias, tiles, log), ('rep', 'tp'), PARTNERS)  8.13 us
    ppermute x1, starting transfers between devices, body(): asked = lax.ppermute(request, ('rep', 'tp'), PARTNERS)  4.9 us
    pallas_call x1, Pallas kernels, send_tiles(): pl.pallas_call(send_kernel, out_shape=(pltpu.VMEM((PEERS * 4, 2 * PAGE, H...  2.59 us
    pallas_call x1, Pallas kernels, local_part(): pl.pallas_call(local_kernel, out_shape=(out, out), in_specs=[SMEM] + [VME...  2.09 us
    ppermute x1, waiting for transfers between devices, body(): asked = lax.ppermute(request, ('rep', 'tp'), PARTNERS)  1.68 us
    pallas_call x2, Pallas kernels, token_bias(): pl.pallas_call(lambda *refs: bias_kernel(sections, *refs), out_shape=(out...  1.63 us
  transfers between devices with their start and end apart: 3, of which 2 were waited for; matrix products, arithmetic and copies ran while one was open for 0% of the time, Pallas kernels for 8%

profile of v9, /device:TPU:1, one launch (start us, length us, event | category | flops | bytes accessed | tf_op | source)
XLA Modules:
  0.0 55.6 jit_solution(3072540095585131704)
XLA Ops:
  0.0 2.6 %send_tiles.1 = (bf16[128,32,128]{2,1,0:T(8,128)(2,1)}, bf16[272,128]{1,0:T(8,128)(2,1)S(1)}) custom-call(s32[1]{0:T(128)} %bitcast.half_ref.refs_0_, s32[1]{0:T(128)} %bitcast.1.core_ref.refs_1_, s32[64]{0:T(128)} %bitcast.19, s32[64]{0:T(128)} %source_ref.1, s32[128]{0:T(128)} %constant.17.clone.stand_ref, s32[4]{0:T(128)} %length_ref.1, s32[4]{0:T(128)} %fill_ref.3, ...), custom_call_target="tpu_custom_call" | custom-call | flops 1000 | bytes 2097152 | tf_op jit(solution)/shard_map/send_tiles/pallas_call | solution.py:117
  2.6 10.6 %all-to-all-start = ((bf16[128,32,128]{2,1,0:T(8,128)(2,1)}), bf16[128,32,128]{2,1,0:T(8,128)(2,1)S(1)}, u32[]{:S(2)}, u32[]{:S(2)}) async-start(bf16[128,32,128]{2,1,0:T(8,128)(2,1)} %get-tuple-element.17), calls=%async_computation | async-start | bytes 2097152 | tf_op jit(solution)/shard_map/all_to_all | solution.py:367
  13.2 4.9 %collective-permute-start = (bf16[272,128]{1,0:T(8,128)(2,1)S(1)}, bf16[272,128]{1,0:T(8,128)(2,1)S(1)}, u32[]{:S(2)}, u32[]{:S(2)}) collective-permute-start(bf16[272,128]{1,0:T(8,128)(2,1)S(1)} %get-tuple-element.15.refs_2_.request_ref), channel_id=1, source_target_pairs={{0,32},{1,65},{2,34},{3,67},{4,36},{5,69},{6,38},{7,71},{8,40},{9,... | collective-permute-start | bytes 208904 | tf_op jit(solution)/shard_map/ppermute | solution.py:370
  18.1 1.1 %token_bias.2 = (bf16[1024,128]{1,0:T(8,128)(2,1)S(1)}, bf16[1024,128]{1,0:T(8,128)(2,1)S(1)}) custom-call(s32[1]{0:T(128)} %bitcast.half_ref.refs_0_, s32[1]{0:T(128)} %bitcast.1.core_ref.refs_1_, bf16[272,128]{1,0:T(8,128)(2,1)S(1)} %get-tuple-element.15.refs_2_.request_ref), custom_call_target="tpu_custom_call" | custom-call | flops 134217728 | bytes 262144 | tf_op jit(solution)/shard_map/token_bias/pallas_call | solution.py:172
  19.2 2.1 %local_part.1 = (f32[256,128]{1,0:T(8,128)S(1)}, f32[256,128]{1,0:T(8,128)S(1)}) custom-call(s32[4]{0:T(128)} %fill_ref.3, bf16[272,128]{1,0:T(8,128)(2,1)S(1)} %get-tuple-element.15.refs_2_.request_ref, bf16[64,32,128]{2,1,0:T(8,128)(2,1)} %bitcast.13, bf16[4,32,128]{2,1,0:T(8,128)(2,1)} %bitcast.16, bf16[4,4,2,128]{3,2,1,0:T(2,128)(2,1)} %bitcast.18, ...), custom_call_target="tpu_custom_call" | custom-call | flops 268435456 | bytes 1048576 | tf_op jit(solution)/shard_map/local_part/pallas_call | solution.py:225
  21.3 1.7 %collective-permute-done.refs_2_.request_ref = bf16[272,128]{1,0:T(8,128)(2,1)S(1)} collective-permute-done((bf16[272,128]{1,0:T(8,128)(2,1)S(1)}, bf16[272,128]{1,0:T(8,128)(2,1)S(1)}, u32[]{:S(2)}, u32[]{:S(2)}) %collective-permute-start) | collective-permute-done | bytes 69664 | tf_op jit(solution)/shard_map/ppermute | solution.py:370
  23.0 0.6 %token_bias.3.bias_ref = bf16[1024,128]{1,0:T(8,128)(2,1)S(1)} custom-call(s32[1]{0:T(128)} %bitcast.half_ref.refs_0_, s32[1]{0:T(128)} %bitcast.1.core_ref.refs_1_, bf16[272,128]{1,0:T(8,128)(2,1)S(1)} %collective-permute-done.refs_2_.request_ref), custom_call_target="tpu_custom_call" | custom-call | flops 134217728 | bytes 262144 | tf_op jit(solution)/shard_map/token_bias/pallas_call | solution.py:172
  23.6 0.0 all-to-all-done
  23.6 1.0 %far_part.1 = bf16[272,128]{1,0:T(8,128)(2,1)S(1)} custom-call(bf16[272,128]{1,0:T(8,128)(2,1)S(1)} %collective-permute-done.refs_2_.request_ref, bf16[1024,128]{1,0:T(8,128)(2,1)S(1)} %token_bias.3.bias_ref, bf16[32,4,32,128]{3,2,1,0:T(8,128)(2,1)S(1)} %bitcast.9, f32[256,128]{1,0:T(8,128)S(1)} %get-tuple-element.20.log_ref.after_ref), custom_call_target="tpu_custom_call" | custom-call | flops 268435456 | bytes 1048576 | tf_op jit(solution)/shard_map/far_part/pallas_call | solution.py:257
  24.6 8.1 %collective-permute-start.1 = (bf16[272,128]{1,0:T(8,128)(2,1)S(1)}, bf16[272,128]{1,0:T(8,128)(2,1)S(1)}, u32[]{:S(2)}, u32[]{:S(2)}) collective-permute-start(bf16[272,128]{1,0:T(8,128)(2,1)S(1)} %far_part.1), channel_id=1, source_target_pairs={{0,32},{1,65},{2,34},{3,67},{4,36},{5,69},{6,38},{7,71},{8,40},{9,... | collective-permute-start | bytes 208904 | tf_op jit(solution)/shard_map/ppermute | solution.py:375
  32.7 0.9 %near_part.1 = (f32[256,128]{1,0:T(8,128)S(1)}, f32[256,128]{1,0:T(8,128)S(1)}) custom-call(bf16[272,128]{1,0:T(8,128)(2,1)S(1)} %get-tuple-element.15.refs_2_.request_ref, bf16[1024,128]{1,0:T(8,128)(2,1)S(1)} %get-tuple-element.16.bias_ref, bf16[32,4,32,128]{3,2,1,0:T(8,128)(2,1)S(1)} %bitcast.10, f32[256,128]{1,0:T(8,128)S(1)} %get-tuple-element.19.mixed_ref, ...), custom_call_target="tpu_custom_call" | custom-call | flops 268435456 | bytes 1048576 | tf_op jit(solution)/shard_map/near_part/pallas_call | solution.py:276
  33.6 0.8 %collective-permute-done.1.back_ref = bf16[272,128]{1,0:T(8,128)(2,1)S(1)} collective-permute-done((bf16[272,128]{1,0:T(8,128)(2,1)S(1)}, bf16[272,128]{1,0:T(8,128)(2,1)S(1)}, u32[]{:S(2)}, u32[]{:S(2)}) %collective-permute-start.1) | collective-permute-done | bytes 69664 | tf_op jit(solution)/shard_map/ppermute | solution.py:375
  34.4 0.3 merge.1
  34.7 0.0 copy-start
  34.7 20.1 %all_to_all.10.square_ref = f32[8,1,128]{2,1,0:T(1,128)S(1)} all-to-all(f32[8,1,128]{2,1,0:T(1,128)S(1)} %get-tuple-element.24), channel_id=1, replica_groups={{4,5,2,3,6,7,0,1},{12,13,10,11,14,15,8,9},{20,21,18,19,22,23,16,17},{28..., dimensions={0} | all-to-all | bytes 8192 | tf_op jit(solution)/shard_map/all_to_all | solution.py:378
  54.8 0.0 copy-done
  54.8 0.7 %normalize.1 = bf16[4,4,2048]{2,1,0:T(4,128)(2,1)} custom-call(bf16[256,128]{1,0:T(8,128)(2,1)S(1)} %get-tuple-element.23.attn_ref, f32[8,1,128]{2,1,0:T(1,128)S(1)} %all_to_all.10.square_ref, f32[16,128]{1,0:T(8,128)S(1)} %bitcast.11), custom_call_target="tpu_custom_call" | custom-call | tf_op jit(solution)/shard_map/normalize/pallas_call | solution.py:329
Async XLA Ops:
  2.6 21.0 %all-to-all-start = ((bf16[128,32,128]{2,1,0:T(8,128)(2,1)}), bf16[128,32,128]{2,1,0:T(8,128)(2,1)S(1)}, u32[]{:S(2)}, u32[]{:S(2)}) async-start(bf16[128,32,128]{2,1,0:T(8,128)(2,1)} %get-tuple-element.17), calls=%async_computation | async-start | bytes 2097152 | tf_op jit(solution)/shard_map/all_to_all | solution.py:367
  13.2 9.8 %collective-permute-start = (bf16[272,128]{1,0:T(8,128)(2,1)S(1)}, bf16[272,128]{1,0:T(8,128)(2,1)S(1)}, u32[]{:S(2)}, u32[]{:S(2)}) collective-permute-start(bf16[272,128]{1,0:T(8,128)(2,1)S(1)} %get-tuple-element.15.refs_2_.request_ref), channel_id=1, source_target_pairs={{0,32},{1,65},{2,34},{3,67},{4,36},{5,69},{6,38},{7,71},{8,40},{9,... | collective-permute-start | bytes 208904 | tf_op jit(solution)/shard_map/ppermute | solution.py:370
  24.6 9.8 %collective-permute-start.1 = (bf16[272,128]{1,0:T(8,128)(2,1)S(1)}, bf16[272,128]{1,0:T(8,128)(2,1)S(1)}, u32[]{:S(2)}, u32[]{:S(2)}) collective-permute-start(bf16[272,128]{1,0:T(8,128)(2,1)S(1)} %far_part.1), channel_id=1, source_target_pairs={{0,32},{1,65},{2,34},{3,67},{4,36},{5,69},{6,38},{7,71},{8,40},{9,... | collective-permute-start | bytes 208904 | tf_op jit(solution)/shard_map/ppermute | solution.py:375
  34.7 20.1 %copy-start = (f32[2048]{0:T(1024)S(1)}, f32[2048]{0:T(1024)}, u32[]{:S(2)}) copy-start(f32[2048]{0:T(1024)} %param.22) | copy-start | bytes 24580
